TPU v7x, 512 devices: a whole 4x8x8 slice. The times are simulated.
512 devices in a mesh: lon: 64 (over z, y_hi, core), lat: 8 (over x, y_lo).
Axes of the slice: x: 4, y: 8 (y_hi: 4, y_lo: 2; y = y_hi * 2 + y_lo), z: 8, core: 2. Of those that a mesh axis runs over, the one named last changes fastest.
Arguments:
- activations: bfloat16 [4, 48, 768, 512], P(None, 'lat', 'lon'), may hold values from -6 to 6
- cotangent: bfloat16 [4, 48, 768, 512], P(None, 'lat', 'lon'), may hold values from -6 to 6
- qkv_weight: bfloat16 [512, 1536], replicated, may hold values from -0.397747564 to 0.397747564, as said below
- proj_weight: bfloat16 [512, 512], replicated, may hold values from -0.25 to 0.25
Outputs:
- input_grad: bfloat16 [4, 48, 768, 512], P(None, 'lat', 'lon')
- qkv_weight_grad: bfloat16 [512, 1536], replicated
- proj_weight_grad: bfloat16 [512, 512], replicated
Inputs may be any that keep to these rules, and one draw needn't show every extreme that they name: `qkv_weight`: most entries of order 512 ** -0.5; a few columns up to 9 times that.
All inputs are finite; a program needn't handle non-finite values.
Results may differ from a plain program's by a relative error of at most 0.01.
Values may be sent and summed in bfloat16 or wider, within the bound.
No kernel may reach another device: no remote copies, remote signals or barrier semaphores. Data moves between devices by JAX's collectives and lax.ppermute only.
A program may use at most 64 MiB of HBM per device.

v0:
```python
import jax
import jax.numpy as jnp
from jax import lax
from jax.sharding import PartitionSpec as P

D = 512
HEADS = 8
WIN_LEV = 2
WIN_LAT = 6
WIN_LON = 12


def shifted(value, axis, by):
    count = lax.axis_size(axis)
    return lax.ppermute(value, axis, [(i, (i + by) % count) for i in range(count)])


def to_windows(grid):
    levels, rows, cols, width = grid.shape
    blocks = grid.reshape(
        levels // WIN_LEV, WIN_LEV, rows // WIN_LAT, WIN_LAT, cols // WIN_LON, WIN_LON, width
    )
    blocks = blocks.transpose(0, 2, 4, 1, 3, 5, 6)
    return blocks.reshape(
        levels // WIN_LEV * (rows // WIN_LAT) * (cols // WIN_LON),
        WIN_LEV * WIN_LAT * WIN_LON,
        width,
    )


def from_windows(blocks, levels, rows, cols):
    width = blocks.shape[-1]
    grid = blocks.reshape(
        levels // WIN_LEV, rows // WIN_LAT, cols // WIN_LON, WIN_LEV, WIN_LAT, WIN_LON, width
    )
    return grid.transpose(0, 3, 1, 4, 2, 5, 6).reshape(levels, rows, cols, width)


def attend(qkv_win, grad_win, same):
    head_width = D // HEADS
    scale = head_width ** (-0.5)
    split = qkv_win.reshape(qkv_win.shape[:-1] + (3, HEADS, head_width))
    query = split[..., 0, :, :]
    keys = split[..., 1, :, :]
    values = split[..., 2, :, :]
    scores = jnp.einsum("bqhd,bkhd->bhqk", query, keys, preferred_element_type=jnp.float32) * scale
    scores = jnp.where(same[:, None], scores, -1000000000.0)
    top = jnp.max(scores, axis=-1, keepdims=True)
    expo = jnp.exp(scores - top)
    probs = expo / jnp.sum(expo, axis=-1, keepdims=True)
    probs_low = probs.astype(jnp.bfloat16)
    attended = jnp.einsum(
        "bhqk,bkhd->bqhd", probs_low, values, preferred_element_type=jnp.float32
    ).astype(jnp.bfloat16)
    upstream = grad_win.reshape(grad_win.shape[:-1] + (HEADS, head_width))
    prob_grad = jnp.einsum("bqhd,bkhd->bhqk", upstream, values, preferred_element_type=jnp.float32)
    value_grad = jnp.einsum(
        "bhqk,bqhd->bkhd", probs_low, upstream, preferred_element_type=jnp.float32
    ).astype(jnp.bfloat16)
    inner = jnp.sum(probs * prob_grad, axis=-1, keepdims=True)
    score_grad = (probs * (prob_grad - inner) * scale).astype(jnp.bfloat16)
    query_grad = jnp.einsum(
        "bhqk,bkhd->bqhd", score_grad, keys, preferred_element_type=jnp.float32
    ).astype(jnp.bfloat16)
    key_grad = jnp.einsum(
        "bhqk,bqhd->bkhd", score_grad, query, preferred_element_type=jnp.float32
    ).astype(jnp.bfloat16)
    qkv_grad = jnp.stack([query_grad, key_grad, value_grad], axis=-3).reshape(qkv_win.shape)
    return (attended.reshape(grad_win.shape), qkv_grad)


def region(index, total, window):
    return jnp.where(
        index < total - window, 0, jnp.where(index < total - window // 2, 1, 2)
    ).astype(jnp.int32)


def per_device(activations, cotangent, qkv_weight, proj_weight):
    levels, lat_rows, lon_cols, width = activations.shape
    half_lev = WIN_LEV // 2
    half_lat = WIN_LAT // 2
    half_lon = WIN_LON // 2
    strips = shifted(
        jnp.stack([activations[:, :, :half_lon], cotangent[:, :, :half_lon]]), "lon", -1
    )
    moved = jnp.concatenate(
        [jnp.stack([activations[:, :, half_lon:], cotangent[:, :, half_lon:]]), strips], axis=3
    )
    edge_rows = shifted(moved[:, :, :half_lat], "lat", -1)
    moved = jnp.concatenate([moved[:, :, half_lat:], edge_rows], axis=2)
    moved = jnp.roll(moved, -half_lev, axis=1)
    rolled_input = moved[0]
    rolled_cot = moved[1]
    float_values = rolled_input.astype(jnp.float32)
    centered_input = jnp.mean(float_values, axis=-1, keepdims=True)
    variance = jnp.mean((float_values - centered_input) ** 2, axis=-1, keepdims=True)
    inverse_deviation = lax.rsqrt(variance + 1e-05)
    standardized_input = (float_values - centered_input) * inverse_deviation
    norm_output = standardized_input.astype(jnp.bfloat16)
    flat_normed = norm_output.reshape(-1, width)
    qkv = jnp.dot(flat_normed, qkv_weight, preferred_element_type=jnp.float32).astype(jnp.bfloat16)
    flat_cot = rolled_cot.reshape(-1, width)
    attended_grad = jnp.einsum(
        "tc,dc->td", flat_cot, proj_weight, preferred_element_type=jnp.float32
    ).astype(jnp.bfloat16)
    lat_count = lat_rows * lax.axis_size("lat")
    lon_count = lon_cols * lax.axis_size("lon")
    global_rows = lax.axis_index("lat") * lat_rows + jnp.arange(lat_rows, dtype=jnp.int32)
    global_cols = lax.axis_index("lon") * lon_cols + jnp.arange(lon_cols, dtype=jnp.int32)
    level_label = region(jnp.arange(levels, dtype=jnp.int32), levels, WIN_LEV)
    lat_label = region(global_rows, lat_count, WIN_LAT)
    lon_label = region(global_cols, lon_count, WIN_LON)
    labels = (
        9 * level_label[:, None, None, None]
        + 3 * lat_label[None, :, None, None]
        + lon_label[None, None, :, None]
    )
    label_win = to_windows(labels)[..., 0]
    same = label_win[..., :, None] == label_win[..., None, :]
    qkv_win = to_windows(qkv.reshape(levels, lat_rows, lon_cols, 3 * width))
    grad_win = to_windows(attended_grad.reshape(levels, lat_rows, lon_cols, width))
    attended_win, qkv_grad_win = attend(qkv_win, grad_win, same)
    attended = from_windows(attended_win, levels, lat_rows, lon_cols).reshape(-1, width)
    qkv_grad = from_windows(qkv_grad_win, levels, lat_rows, lon_cols).reshape(-1, 3 * width)
    norm_output_gradient = jnp.einsum(
        "te,ce->tc", qkv_grad, qkv_weight, preferred_element_type=jnp.float32
    )
    norm_output_gradient = norm_output_gradient.reshape(levels, lat_rows, lon_cols, width)
    average_gradient = jnp.mean(norm_output_gradient, axis=-1, keepdims=True)
    average_product = jnp.mean(norm_output_gradient * standardized_input, axis=-1, keepdims=True)
    residual_branch_gradient = (
        inverse_deviation
        * (norm_output_gradient - average_gradient - standardized_input * average_product)
    ).astype(jnp.bfloat16)
    residual_branch_gradient = jnp.roll(residual_branch_gradient, half_lev, axis=0)
    back_rows = shifted(residual_branch_gradient[:, lat_rows - half_lat :], "lat", 1)
    residual_branch_gradient = jnp.concatenate(
        [back_rows, residual_branch_gradient[:, : lat_rows - half_lat]], axis=1
    )
    back_cols = shifted(residual_branch_gradient[:, :, lon_cols - half_lon :], "lon", 1)
    residual_branch_gradient = jnp.concatenate(
        [back_cols, residual_branch_gradient[:, :, : lon_cols - half_lon]], axis=2
    )
    input_grad = (
        cotangent.astype(jnp.float32) + residual_branch_gradient.astype(jnp.float32)
    ).astype(jnp.bfloat16)
    local_qkv = jnp.einsum("tc,te->ce", flat_normed, qkv_grad, preferred_element_type=jnp.float32)
    local_proj = jnp.einsum("tc,td->cd", attended, flat_cot, preferred_element_type=jnp.float32)
    token_count = levels * lat_rows * lon_cols * lax.axis_size("lon") * lax.axis_size("lat")
    factor = token_count ** (-0.5)
    summed_qkv, summed_proj = lax.psum((local_qkv, local_proj), ("lon", "lat"))
    qkv_weight_grad = (summed_qkv * factor).astype(jnp.bfloat16)
    proj_weight_grad = (summed_proj * factor).astype(jnp.bfloat16)
    return (input_grad, qkv_weight_grad, proj_weight_grad)


def solution(mesh):
    placed = (P(None, "lat", "lon", None), P(None, "lat", "lon", None), P(), P())
    return jax.shard_map(
        per_device,
        mesh=mesh,
        in_specs=placed,
        out_specs=(P(None, "lat", "lon", None), P(), P()),
        check_vma=False,
    )
```

profile of v0, /device:TPU:1, one launch (start us, length us, event | category | flops | bytes accessed | tf_op | source)
XLA Modules:
  0.0 404.8 jit_solution(18185948743827364665)
XLA Ops:
  9.7 8.8 %collective-permute-start = (bf16[2,4,6,6,512]{4,3,2,1,0:T(8,128)(2,1)S(1)}, bf16[2,4,6,6,512]{4,3,2,1,0:T(8,128)(2,1)S(1)}, u32[]{:S(2)}, u32[]{:S(2)}) collective-permute-start(bf16[2,4,6,6,512]{4,3,2,1,0:T(8,128)(2,1)S(1)} %pad_maximum_fusion.4), channel_id=1, source_target_pairs={{0,504},{8,0},{16,8},{24,16},{32,24},{40,32},{48,40},{56,48},{64,5... | collective-permute-start | bytes 884744 | tf_op jit(solution)/shard_map/ppermute | solution.py:15
  18.6 6.3 %collective-permute-done = bf16[2,4,6,6,512]{4,3,2,1,0:T(8,128)(2,1)S(1)} collective-permute-done((bf16[2,4,6,6,512]{4,3,2,1,0:T(8,128)(2,1)S(1)}, bf16[2,4,6,6,512]{4,3,2,1,0:T(8,128)(2,1)S(1)}, u32[]{:S(2)}, u32[]{:S(2)}) %collective-permute-start) | collective-permute-done | bytes 294944 | tf_op jit(solution)/shard_map/ppermute | solution.py:15
  25.3 2.3 collective-permute-start.1
  28.5 6.8 %collective-permute-done.1 = bf16[2,4,3,12,512]{4,3,2,1,0:T(8,128)(2,1)S(1)} collective-permute-done((bf16[2,4,3,12,512]{4,3,2,1,0:T(8,128)(2,1)S(1)}, bf16[2,4,3,12,512]{4,3,2,1,0:T(8,128)(2,1)S(1)}, u32[]{:S(2)}, u32[]{:S(2)}) %collective-permute-start.1) | collective-permute-done | bytes 294944 | tf_op jit(solution)/shard_map/ppermute | solution.py:15
  38.0 2.2 convolution_convert_fusion.3
  45.5 2.6 convolution_convert_fusion
  48.1 3.4 reshape_reshape_transpose_reshape_reshape.12
  51.6 2.3 fusion.71
  53.9 2.2 copy.47
  57.8 3.0 fusion.39
  60.7 3.7 fusion.75
  64.4 3.0 fusion.20
  67.4 5.7 %fusion.22 = bf16[2,144,1,8,64]{1,4,3,0,2:T(8,128)(2,1)} fusion(f32[2,8,144,144]{2,3,1,0:T(8,128)} %fusion.39, bf16[2,144,1,8,64]{1,4,3,0,2:T(8,128)(2,1)} %copy.48, f32[2,8,144,144]{2,3,1,0:T(8,128)} %get-tuple-element.27, f32[2,8,144]{2,1,0:T(8,128)S(1)} %get-tuple-element.26), kind=kOutput, calls=%fused_computation.21 | convolution fusion | flops 44939664 | bytes 3253248 | tf_op jit(solution)/shard_map/bhqk,bqhd->bkhd/dot_general | solution.py:65
  73.1 5.4 %fusion.25 = bf16[2,144,1,8,64]{1,4,3,0,2:T(8,128)(2,1)} fusion(f32[2,8,144,144]{2,3,1,0:T(8,128)} %fusion.39, bf16[2,144,1,8,64]{1,4,3,0,2:T(8,128)(2,1)S(1)} %copy-done.7, f32[2,8,144,144]{2,3,1,0:T(8,128)} %get-tuple-element.27, f32[2,8,144]{2,1,0:T(8,128)S(1)} %get-tuple-element.26), kind=kOutput, calls=%fused_computation.22 | convolution fusion | flops 44939664 | bytes 3253248 | tf_op jit(solution)/shard_map/bhqk,bkhd->bqhd/dot_general | solution.py:62
  79.5 2.9 fusion.21
  83.9 2.9 copy.35
  94.8 2.5 fusion.81
  97.3 3.9 fusion.80
  103.3 2.3 fusion.70
  107.9 6.6 %collective-permute-done.2 = bf16[4,3,12,512]{3,2,1,0:T(8,128)(2,1)S(1)} collective-permute-done((bf16[4,3,12,512]{3,2,1,0:T(8,128)(2,1)S(1)}, bf16[4,3,12,512]{3,2,1,0:T(8,128)(2,1)S(1)}, u32[]{:S(2)}, u32[]{:S(2)}) %collective-permute-start.2) | collective-permute-done | bytes 147488 | tf_op jit(solution)/shard_map/ppermute | solution.py:15
  114.6 3.7 collective-permute-start.3
  118.3 10.1 %collective-permute-done.3 = bf16[4,6,6,512]{3,2,1,0:T(8,128)(2,1)S(1)} collective-permute-done((bf16[4,6,6,512]{3,2,1,0:T(8,128)(2,1)S(1)}, bf16[4,6,6,512]{3,2,1,0:T(8,128)(2,1)S(1)}, u32[]{:S(2)}, u32[]{:S(2)}) %collective-permute-start.3) | collective-permute-done | bytes 147488 | tf_op jit(solution)/shard_map/ppermute | solution.py:15
  129.5 264.0 %all-reduce.3.cloned.1.call-done = (f32[512,1536]{1,0:T(8,128)}, f32[512,512]{1,0:T(8,128)}) async-done(((f32[512,1536]{1,0:T(8,128)}, f32[512,512]{1,0:T(8,128)}), (f32[512,1536]{1,0:T(8,128)}, f32[512,512]{1,0:T(8,128)})) %all-reduce.3.cloned.1.call-update) | async-done | bytes 4194320 | tf_op jit(solution)/shard_map/psum | solution.py:151
  393.5 3.5 multiply_convert_fusion
  (76 shorter events, 30.3 us)
Async XLA Ops:
  7.2 38.3 %copy-start = (bf16[512,1536]{1,0:T(8,128)(2,1)S(1)}, bf16[512,1536]{1,0:T(8,128)(2,1)}, u32[]{:S(2)}) copy-start(bf16[512,1536]{1,0:T(8,128)(2,1)} %param.6) | copy-start | bytes 4718596
  7.2 386.4 %all-reduce.3.cloned.1.call-start = ((), (), s32[]{:S(2)}) async-start(), calls=%async_computation | async-start | bytes 8388608 | tf_op jit(solution)/shard_map/psum | solution.py:151
  9.7 15.3 %collective-permute-start = (bf16[2,4,6,6,512]{4,3,2,1,0:T(8,128)(2,1)S(1)}, bf16[2,4,6,6,512]{4,3,2,1,0:T(8,128)(2,1)S(1)}, u32[]{:S(2)}, u32[]{:S(2)}) collective-permute-start(bf16[2,4,6,6,512]{4,3,2,1,0:T(8,128)(2,1)S(1)} %pad_maximum_fusion.4), channel_id=1, source_target_pairs={{0,504},{8,0},{16,8},{24,16},{32,24},{40,32},{48,40},{56,48},{64,5... | collective-permute-start | bytes 884744 | tf_op jit(solution)/shard_map/ppermute | solution.py:15
  25.3 9.9 %collective-permute-start.1 = (bf16[2,4,3,12,512]{4,3,2,1,0:T(8,128)(2,1)S(1)}, bf16[2,4,3,12,512]{4,3,2,1,0:T(8,128)(2,1)S(1)}, u32[]{:S(2)}, u32[]{:S(2)}) collective-permute-start(bf16[2,4,3,12,512]{4,3,2,1,0:T(8,128)(2,1)S(1)} %get-tuple-element.19), channel_id=1, source_target_pairs={{0,7},{1,0},{2,1},{3,2},{4,3},{5,4},{6,5},{7,6},{8,15},{9,8},{10,9... | collective-permute-start | bytes 884744 | tf_op jit(solution)/shard_map/ppermute | solution.py:15
  35.4 43.1 %copy-start.1 = (bf16[2,4,6,12,512]{4,3,2,1,0:T(8,128)(2,1)}, bf16[2,4,6,12,512]{4,3,2,1,0:T(8,128)(2,1)S(1)}, u32[]{:S(2)}) copy-start(bf16[2,4,6,12,512]{4,3,2,1,0:T(8,128)(2,1)S(1)} %fusion.33) | copy-start | bytes 1769476
  36.9 8.5 %copy-start.11 = (f32[4,6,12]{2,1,0:T(8,128)}, f32[4,6,12]{2,1,0:T(8,128)S(1)}, u32[]{:S(2)}) copy-start(f32[4,6,12]{2,1,0:T(8,128)S(1)} %add_rsqrt_fusion) | copy-start | bytes 3460
  37.9 10.2 %copy-start.3 = (bf16[288,512]{1,0:T(8,128)(2,1)}, bf16[288,512]{1,0:T(8,128)(2,1)S(1)}, u32[]{:S(2)}) copy-start(bf16[288,512]{1,0:T(8,128)(2,1)S(1)} %reshape_squeeze.3) | copy-start | bytes 884740
  60.7 3.7 copy-start.4
  67.4 5.7 %copy-start.7 = (bf16[2,144,1,8,64]{1,4,3,0,2:T(8,128)(2,1)S(1)}, bf16[2,144,1,8,64]{1,4,3,0,2:T(8,128)(2,1)}, u32[]{:S(2)}) copy-start(bf16[2,144,1,8,64]{1,4,3,0,2:T(8,128)(2,1)} %copy.47) | copy-start | bytes 884740
  73.1 5.4 %copy-start.12 = (f32[4,6,12]{2,1,0:T(8,128)S(1)}, f32[4,6,12]{2,1,0:T(8,128)}, u32[]{:S(2)}) copy-start(f32[4,6,12]{2,1,0:T(8,128)} %copy-done.11) | copy-start | bytes 3460
  79.5 2.9 copy-start.8
  79.5 2.9 copy-start.9
  79.5 2.9 copy-start.10
  103.2 2.3 copy-start.2
  105.6 22.8 %copy-start.5 = (bf16[4,6,12,512]{3,0,2,1:T(4,128)(2,1)S(1)}, bf16[4,6,12,512]{3,0,2,1:T(4,128)(2,1)}, u32[]{:S(2)}) copy-start(bf16[4,6,12,512]{3,0,2,1:T(4,128)(2,1)} %param.5) | copy-start | bytes 884740
  106.0 8.5 %collective-permute-start.2 = (bf16[4,3,12,512]{3,2,1,0:T(8,128)(2,1)S(1)}, bf16[4,3,12,512]{3,2,1,0:T(8,128)(2,1)S(1)}, u32[]{:S(2)}, u32[]{:S(2)}) collective-permute-start(bf16[4,3,12,512]{3,2,1,0:T(8,128)(2,1)S(1)} %fusion.49), channel_id=1, source_target_pairs={{0,1},{1,2},{2,3},{3,4},{4,5},{5,6},{6,7},{7,0},{8,9},{9,10},{10,1... | collective-permute-start | bytes 442376 | tf_op jit(solution)/shard_map/ppermute | solution.py:15
  114.6 13.8 %collective-permute-start.3 = (bf16[4,6,6,512]{3,2,1,0:T(8,128)(2,1)S(1)}, bf16[4,6,6,512]{3,2,1,0:T(8,128)(2,1)S(1)}, u32[]{:S(2)}, u32[]{:S(2)}) collective-permute-start(bf16[4,6,6,512]{3,2,1,0:T(8,128)(2,1)S(1)} %get-tuple-element.20), channel_id=1, source_target_pairs={{0,8},{8,16},{16,24},{24,32},{32,40},{40,48},{48,56},{56,64},{64,7... | collective-permute-start | bytes 442376 | tf_op jit(solution)/shard_map/ppermute | solution.py:15
  393.5 3.5 copy-start.6
Sparse Core Ops, SparseCore 0:
  101.4 292.1 all-reduce.2
where the time goes:
time: 407 us; the launch traced here: 405 us
  waiting for transfers between devices  294 us (72%)
  matrix products  37.3 us (9%)
  local copies, waits for them, and re-layouts  32.6 us (8%)
  starting transfers between devices  16.7 us (4%)
  between operations  14.3 us (4%)
  other arithmetic  10.1 us (2%)
    psum x1, waiting for transfers between devices, per_device(): summed_qkv, summed_proj = lax.psum((local_qkv, local_proj), ('lon', 'lat'))  264 us
    ppermute x4, waiting for transfers between devices, shifted(): lax.ppermute(value, axis, [(i, (i + by) % count) for i in range(count)])  29.7 us
    ppermute x4, starting transfers between devices, shifted(): lax.ppermute(value, axis, [(i, (i + by) % count) for i in range(count)])  16.7 us
  transfers between devices with their start and end apart: 5, of which 5 were waited for; matrix products, arithmetic and copies ran while one was open for 2% of the time, Pallas kernels for 0%

commit v1 on v0

v1 whole, which is shorter than its diff:
```python
import jax
import jax.numpy as jnp
from jax import lax
from jax.experimental import pallas as pl
from jax.experimental.pallas import tpu as pltpu
from jax.sharding import Mesh, PartitionSpec as P

D = 512
HEADS = 8
HEAD_DIM = 64
GROUP = 4
LEVELS = 4
HALF_LAT = 3
HALF_LON = 6
ROWS = 6
COLS = 12
PAIRS = ((1, 2), (3, 0))
QUARTER = 2 * HALF_LAT * HALF_LON
WINDOW = 4 * QUARTER
TOKENS = 2 * WINDOW

LON = ("z2", "z1", "z0", "y2", "y1", "core")
LAT = ("x1", "x0", "y0")
CORE = ("core",)
NEAR = ("z0", "y0", "x0")
MIDDLE = ("x1", "z2", "z1")
FAR = ("y2", "y1")


def dot(a, b, a_dim, b_dim):
    return lax.dot_general(a, b, (((a_dim,), (b_dim,)), ((), ())), preferred_element_type=jnp.float32)


def owner_of(kind, lat, lon):
    lat = lat + kind // 2
    return lat, lon + kind % 2 * (-1 if lat % 2 == 1 else 1)


def moved(value, kind, back):
    lons, lats = lax.axis_size(LON), lax.axis_size(LAT)
    pairs = []
    for lon in range(lons):
        for lat in range(lats):
            to_lat, to_lon = owner_of(kind, lat, lon)
            pair = (lon * lats + lat, to_lon % lons * lats + to_lat % lats)
            pairs.append(pair[::-1] if back else pair)
    return lax.ppermute(value, LON + LAT, pairs)


def token_labels(token, window, lat_edge, lon_edge):
    quarter = token // QUARTER
    level = token % QUARTER // (QUARTER // 2)
    return level * window + 2 * lat_edge * (quarter // 2) + 4 * lon_edge * (quarter % 2)


def pack_kernel(place, act_ref, cot_ref, own, lon, lat, both):
    pieces = {(row_half, col_half): [] for row_half in range(2) for col_half in range(2)}
    for ref in (act_ref, cot_ref):
        for pair in PAIRS:
            for level in pair:
                for row in range(ROWS):
                    line = ref[level, row].astype(jnp.float32)
                    for half in range(2):
                        cut = line[half * HALF_LON : half * HALF_LON + HALF_LON]
                        pieces[row // HALF_LAT, half].append(cut)
    whole = {at: jnp.concatenate(cuts, axis=0).astype(jnp.bfloat16) for at, cuts in pieces.items()}

    def put(parity):
        own[...] = whole[0, parity]
        lon[...] = whole[0, 1 - parity]
        lat[...] = whole[1, 1 - parity]
        both[...] = whole[1, parity]

    for parity in range(2):
        pl.when(place[0] == parity)(lambda parity=parity: put(parity))


def pack(place, activations, cotangent):
    whole = pl.BlockSpec(memory_space=pltpu.VMEM)
    return pl.pallas_call(
        pack_kernel,
        out_shape=(jax.ShapeDtypeStruct((4 * QUARTER, D), jnp.bfloat16),) * 4,
        in_specs=[pl.BlockSpec(memory_space=pltpu.SMEM)] + [whole] * 2,
        out_specs=(whole,) * 4,
        compiler_params=pltpu.CompilerParams(vmem_limit_bytes=32 * 2**20),
        cost_estimate=pl.CostEstimate(flops=0, bytes_accessed=1200000, transcendentals=0),
        name="pack",
    )(place, activations, cotangent)


def unpack_kernel(place, cot_ref, *refs):
    own, lon, lat, both = [ref[...].astype(jnp.float32) for ref in refs[:4]]
    out = refs[4]
    even = place[0] == 0
    whole = {
        (0, 0): jnp.where(even, own, lon),
        (0, 1): jnp.where(even, lon, own),
        (1, 0): jnp.where(even, both, lat),
        (1, 1): jnp.where(even, lat, both),
    }
    at = [0, 0]
    for pair in PAIRS:
        for level in pair:
            for row in range(ROWS):
                half = row // HALF_LAT
                cuts = [whole[half, col_half][at[half] : at[half] + HALF_LON] for col_half in range(2)]
                at[half] += HALF_LON
                line = cot_ref[level, row].astype(jnp.float32) + jnp.concatenate(cuts, axis=0)
                out[level, row] = line.astype(jnp.bfloat16)


def unpack(place, cotangent, quarters):
    whole = pl.BlockSpec(memory_space=pltpu.VMEM)
    return pl.pallas_call(
        unpack_kernel,
        out_shape=jax.ShapeDtypeStruct(cotangent.shape, jnp.bfloat16),
        in_specs=[pl.BlockSpec(memory_space=pltpu.SMEM)] + [whole] * 5,
        out_specs=whole,
        compiler_params=pltpu.CompilerParams(vmem_limit_bytes=32 * 2**20),
        cost_estimate=pl.CostEstimate(flops=0, bytes_accessed=900000, transcendentals=0),
        name="unpack",
    )(place, cotangent, *quarters)


def block_kernel(place, *refs):
    quarters, (qkv_weight, proj_weight), branch, (grads_ref, x_held, cot_held) = refs[:4], refs[4:6], refs[6:10], refs[10:13]
    normed, qkv, upstream, attended, qkv_grad = refs[13:]
    held = [ref[...].astype(jnp.float32) for ref in quarters]
    for kind, target in enumerate((x_held, cot_held)):
        chunks = [
            held[quarter][(2 * kind + window) * QUARTER : (2 * kind + window + 1) * QUARTER]
            for window in range(2)
            for quarter in range(4)
        ]
        target[...] = jnp.concatenate(chunks, axis=0).astype(jnp.bfloat16)
    x = x_held[...].astype(jnp.float32)
    centered = x - jnp.mean(x, axis=-1, keepdims=True)
    inverse = lax.rsqrt(jnp.mean(centered * centered, axis=-1, keepdims=True) + 1e-05)
    normed[...] = (centered * inverse).astype(jnp.bfloat16)

    @pl.loop(0, 3 * D // 256)
    def _(step):
        cols = pl.ds(pl.multiple_of(step * 256, 256), 256)
        gain = jnp.where(step < D // 256, HEAD_DIM ** (-0.5), 1.0)
        qkv[:, cols] = (dot(normed[...], qkv_weight[:, cols], 1, 0) * gain).astype(jnp.bfloat16)

    @pl.loop(0, D // 256)
    def _(step):
        cols = pl.ds(pl.multiple_of(step * 256, 256), 256)
        upstream[:, cols] = dot(cot_held[...], proj_weight[cols, :], 1, 1).astype(jnp.bfloat16)

    head_of = lax.broadcasted_iota(jnp.int32, (WINDOW, GROUP * HEAD_DIM), 1) // HEAD_DIM
    zero = jnp.zeros((WINDOW, GROUP * HEAD_DIM), jnp.bfloat16)

    def apart(slab):
        return jnp.concatenate([jnp.where(head_of == head, slab, zero) for head in range(GROUP)], axis=0)

    def together(tall):
        merged = tall[:WINDOW]
        for head in range(1, GROUP):
            merged = jnp.where(head_of == head, tall[head * WINDOW : (head + 1) * WINDOW], merged)
        return merged.astype(jnp.bfloat16)

    for window in range(2):
        rows = slice(window * WINDOW, (window + 1) * WINDOW)
        shape = (WINDOW, GROUP * WINDOW)
        key_label = token_labels(lax.broadcasted_iota(jnp.int32, shape, 0), window, place[1], place[2])
        query_label = token_labels(lax.broadcasted_iota(jnp.int32, shape, 1) % WINDOW, window, place[1], place[2])
        bias = jnp.where(key_label == query_label, 0.0, -1000000000.0)
        for group in range(HEADS // GROUP):
            cols = [slice(part * D + group * GROUP * HEAD_DIM, part * D + (group + 1) * GROUP * HEAD_DIM) for part in range(3)]
            query, keys, values = (qkv[rows, at] for at in cols)
            query, grad = apart(query), apart(upstream[rows, cols[0]])
            scores = dot(keys, query, 1, 1) + bias
            expo = jnp.exp(scores - jnp.max(scores, axis=0, keepdims=True))
            probs = expo * (1.0 / jnp.sum(expo, axis=0, keepdims=True))
            low = probs.astype(jnp.bfloat16)
            prob_grad = dot(values, grad, 1, 1)
            inner = jnp.sum(probs * prob_grad, axis=0, keepdims=True)
            score_grad = (probs * (prob_grad - inner)).astype(jnp.bfloat16)
            attended[rows, cols[0]] = together(dot(low, values, 0, 0))
            qkv_grad[rows, cols[0]] = together(dot(score_grad, keys, 0, 0) * HEAD_DIM ** (-0.5))
            qkv_grad[rows, cols[1]] = dot(score_grad, query, 1, 0).astype(jnp.bfloat16)
            qkv_grad[rows, cols[2]] = dot(low, grad, 1, 0).astype(jnp.bfloat16)

    normed_grad = dot(qkv_grad[...], qkv_weight[...], 1, 1)
    x = x_held[...].astype(jnp.float32)
    centered = x - jnp.mean(x, axis=-1, keepdims=True)
    inverse = lax.rsqrt(jnp.mean(centered * centered, axis=-1, keepdims=True) + 1e-05)
    xhat = centered * inverse
    average = jnp.mean(normed_grad, axis=-1, keepdims=True)
    product = jnp.mean(normed_grad * xhat, axis=-1, keepdims=True)
    dx = inverse * (normed_grad - average - xhat * product)
    for quarter in range(4):
        chunks = [dx[(4 * window + quarter) * QUARTER : (4 * window + quarter + 1) * QUARTER] for window in range(2)]
        branch[quarter][...] = jnp.concatenate(chunks, axis=0).astype(jnp.bfloat16)

    def put(step, block):
        block = block.astype(jnp.bfloat16)
        for half in range(2):
            grads_ref[:, 2 * step + half] = block[:, 128 * half : 128 * half + 128].reshape(D // 16, 16, 128)

    @pl.loop(0, 3 * D // 256)
    def _(step):
        cols = pl.ds(pl.multiple_of(step * 256, 256), 256)
        put(step, dot(normed[...], qkv_grad[:, cols], 0, 0))

    @pl.loop(0, D // 256)
    def _(step):
        cols = pl.ds(pl.multiple_of(step * 256, 256), 256)
        put(step + 3 * D // 256, dot(attended[...], cot_held[:, cols], 0, 0))


def block(place, quarters, qkv_weight, proj_weight):
    whole = pl.BlockSpec(memory_space=pltpu.VMEM)
    return pl.pallas_call(
        block_kernel,
        out_shape=(jax.ShapeDtypeStruct((2 * QUARTER, D), jnp.bfloat16),) * 4
        + (jax.ShapeDtypeStruct((D // 16, 4 * D // 128, 16, 128), jnp.bfloat16),),
        in_specs=[pl.BlockSpec(memory_space=pltpu.SMEM)] + [whole] * 6,
        out_specs=(whole,) * 5,
        scratch_shapes=[
            pltpu.VMEM((TOKENS, D), jnp.bfloat16),
            pltpu.VMEM((TOKENS, D), jnp.bfloat16),
            pltpu.VMEM((TOKENS, D), jnp.bfloat16),
            pltpu.VMEM((TOKENS, 3 * D), jnp.bfloat16),
            pltpu.VMEM((TOKENS, D), jnp.bfloat16),
            pltpu.VMEM((TOKENS, D), jnp.bfloat16),
            pltpu.VMEM((TOKENS, 3 * D), jnp.bfloat16),
        ],
        compiler_params=pltpu.CompilerParams(vmem_limit_bytes=48 * 2**20),
        cost_estimate=pl.CostEstimate(flops=2 * 10**9, bytes_accessed=6 * 10**6, transcendentals=6 * 10**5),
        name="block",
    )(place, *quarters, qkv_weight, proj_weight)


def added(arrived):
    total = arrived[0].astype(jnp.float32)
    for part in range(1, arrived.shape[0]):
        total = total + arrived[part].astype(jnp.float32)
    return total


def scattered_sum(tiles, axes):
    groups = lax.axis_size(axes)
    split = tiles.reshape((groups, tiles.shape[0] // groups) + tiles.shape[1:])
    return added(lax.all_to_all(split, axes, 0, 0))


def exchanged(tiles, axes):
    groups = lax.axis_size(axes)
    return lax.all_to_all(jnp.broadcast_to(tiles[None], (groups,) + tiles.shape), axes, 0, 0)


def summed_over_mesh(tiles, factor, branch):
    tiles = scattered_sum(tiles, CORE).astype(jnp.bfloat16)
    tiles, branch = lax.optimization_barrier((tiles, branch))
    tiles = scattered_sum(tiles, NEAR).astype(jnp.bfloat16)
    quarters = [branch[0]] + [moved(branch[kind], kind, True) for kind in range(1, 4)]
    tiles, quarters = lax.optimization_barrier((tiles, quarters))
    tiles = scattered_sum(tiles, MIDDLE).astype(jnp.bfloat16)
    tiles = (added(exchanged(tiles, FAR)) * factor).astype(jnp.bfloat16)
    tiles, quarters = lax.optimization_barrier((exchanged(tiles, MIDDLE), quarters))
    tiles = tiles.reshape((-1,) + tiles.shape[2:])
    for axes in (NEAR, CORE):
        tiles = exchanged(tiles, axes)
        tiles = tiles.reshape((-1,) + tiles.shape[2:])
    return tiles, quarters


def untile_kernel(tiles, qkv_out, proj_out):
    for col in range(4 * D // 128):
        strip = tiles[:, col].reshape(D, 128)
        if col < 3 * D // 128:
            qkv_out[:, 128 * col : 128 * col + 128] = strip
        else:
            proj_out[:, 128 * col - 3 * D : 128 * col - 3 * D + 128] = strip


def untile(tiles):
    whole = pl.BlockSpec(memory_space=pltpu.VMEM)
    return pl.pallas_call(
        untile_kernel,
        out_shape=(jax.ShapeDtypeStruct((D, 3 * D), jnp.bfloat16), jax.ShapeDtypeStruct((D, D), jnp.bfloat16)),
        in_specs=[whole],
        out_specs=(whole, whole),
        compiler_params=pltpu.CompilerParams(vmem_limit_bytes=32 * 2**20),
        cost_estimate=pl.CostEstimate(flops=0, bytes_accessed=4 * 2**20, transcendentals=0),
        name="untile",
    )(tiles)


def per_device(activations, cotangent, qkv_weight, proj_weight):
    lat, lon = lax.axis_index(LAT), lax.axis_index(LON)
    odd = lat % 2 == 1
    lon_edge = jnp.where(odd, lon == lax.axis_size(LON) - 1, lon == 0)
    place = jnp.stack([odd, lat == 0, lon_edge]).astype(jnp.int32)
    quarters = pack(place, activations, cotangent)
    quarters = [quarters[0]] + [moved(quarters[kind], kind, False) for kind in range(1, 4)]
    *branch, grads = block(place, quarters, qkv_weight, proj_weight)
    factor = (LEVELS * ROWS * COLS * lax.axis_size(LON + LAT)) ** (-0.5)
    tiles, quarters = summed_over_mesh(grads.reshape(-1, 16, 128), factor, branch)
    qkv_weight_grad, proj_weight_grad = untile(tiles.reshape(D // 16, 4 * D // 128, 16, 128))
    return (unpack(place, cotangent, quarters), qkv_weight_grad, proj_weight_grad)


def over(physical):
    spec = P(None, LAT, LON, None)
    return jax.shard_map(
        per_device,
        mesh=physical,
        in_specs=(spec, spec, P(), P()),
        out_specs=(spec, P(), P()),
        check_vma=False,
    )


def solution(mesh):
    return over(Mesh(mesh.devices.reshape((2,) * 9), LON + LAT))
```

time: 407 us -> 135 us (0.33)
  waiting for transfers between devices: 294 us -> 24.6 us
  blocking collectives: 0 us -> 53.4 us
  matrix products: 37.3 us -> 0 us
  local copies, waits for them, and re-layouts: 32.6 us -> 4.56 us
  starting transfers between devices: 16.7 us -> 37.7 us
  between operations: 14.3 us -> 0.84 us
  Pallas kernels: 0 us -> 12.3 us
  other arithmetic: 10.1 us -> 1.5 us
    psum x1 -> x0, waiting for transfers between devices: 264 us -> none  [per_device(): summed_qkv, summed_proj = lax.psum((local_qkv, local_proj), ('lon', 'lat'))]
    all_to_all x0 -> x5, blocking collectives: none -> 53.4 us  [the longest x3 30.9 us: exchanged(): lax.all_to_all(jnp.broadcast_to(tiles[None], (groups,) + tiles.shape), ax...]
    dot_general x10 -> x0, matrix products: 33.6 us -> none  [the longest x1 5.66 us: attend(): jnp.einsum('bhqk,bqhd->bkhd', score_grad, query, preferred_element_type=j...]
    ppermute x4 -> x6, waiting for transfers between devices: 29.7 us -> 6.9 us  [moved(): return lax.ppermute(value, LON + LAT, pairs)]
    all_to_all x0 -> x2, waiting for transfers between devices: none -> 17.7 us  [the longest x1 11.1 us: exchanged(): lax.all_to_all(jnp.broadcast_to(tiles[None], (groups,) + tiles.shape), ax...]
    another operation x8 -> x0, local copies, waits for them, and re-layouts: 15.9 us -> none  [the longest x2 4.33 us: attend(): upstream = grad_win.reshape(grad_win.shape[:-1] + (HEADS, head_width))]
    ppermute x4 -> x6, starting transfers between devices: 16.7 us -> 29.1 us  [moved(): return lax.ppermute(value, LON + LAT, pairs)]
    pallas_call x0 -> x4, Pallas kernels: none -> 12.3 us  [the longest x1 9.01 us: block(): pl.pallas_call(block_kernel, out_shape=(jax.ShapeDtypeStruct((2 * QUARTER...]
  transfers between devices with their start and end apart: 5 -> 8, of which waited for: 5 -> 5; matrix products, arithmetic and copies ran while one was open for 2% -> 1% of each run, Pallas kernels for 0% -> 1%
where the time goes in v1:
time: 135 us
  blocking collectives  53.4 us (40%)
  starting transfers between devices  37.7 us (28%)
  waiting for transfers between devices  24.6 us (18%)
  Pallas kernels  12.3 us (9%)
  local copies, waits for them, and re-layouts  4.56 us (3%)
  other arithmetic  1.5 us (1%)
    all_to_all x3, blocking collectives, exchanged(): lax.all_to_all(jnp.broadcast_to(tiles[None], (groups,) + tiles.shape), ax...  30.9 us
    ppermute x6, starting transfers between devices, moved(): return lax.ppermute(value, LON + LAT, pairs)  29.1 us
    all_to_all x2, blocking collectives, scattered_sum(): return added(lax.all_to_all(split, axes, 0, 0))  22.5 us
    all_to_all x1, waiting for transfers between devices, exchanged(): lax.all_to_all(jnp.broadcast_to(tiles[None], (groups,) + tiles.shape), ax...  11.1 us
    pallas_call x1, Pallas kernels, block(): pl.pallas_call(block_kernel, out_shape=(jax.ShapeDtypeStruct((2 * QUARTER...  9.01 us
    ppermute x6, waiting for transfers between devices, moved(): return lax.ppermute(value, LON + LAT, pairs)  6.9 us
    all_to_all x1, waiting for transfers between devices, scattered_sum(): return added(lax.all_to_all(split, axes, 0, 0))  6.62 us
    all_to_all x1, starting transfers between devices, exchanged(): lax.all_to_all(jnp.broadcast_to(tiles[None], (groups,) + tiles.shape), ax...  5.01 us
  transfers between devices with their start and end apart: 8, of which 5 were waited for; matrix products, arithmetic and copies ran while one was open for 1% of the time, Pallas kernels for 1%

profile of v1, /device:TPU:1, one launch (start us, length us, event | category | flops | bytes accessed | tf_op | source)
XLA Modules:
  0.0 134.9 jit_solution(14543883603169602416)
XLA Ops:
  0.7 1.2 copy.9.cot_ref
  1.9 1.0 copy.7.act_ref
  3.9 5.6 %collective-permute-start = (bf16[144,512]{1,0:T(8,128)(2,1)S(1)}, bf16[144,512]{1,0:T(8,128)(2,1)S(1)}, u32[]{:S(2)}, u32[]{:S(2)}) collective-permute-start(bf16[144,512]{1,0:T(8,128)(2,1)S(1)} %get-tuple-element.30), channel_id=1, source_target_pairs={{0,8},{1,505},{2,10},{3,507},{4,12},{5,509},{6,14},{7,511},{8,16},... | collective-permute-start | bytes 442376 | tf_op jit(solution)/shard_map/ppermute | solution.py:47
  9.5 1.9 %collective-permute-start.1 = (bf16[144,512]{1,0:T(8,128)(2,1)S(1)}, bf16[144,512]{1,0:T(8,128)(2,1)S(1)}, u32[]{:S(2)}, u32[]{:S(2)}) collective-permute-start(bf16[144,512]{1,0:T(8,128)(2,1)S(1)} %get-tuple-element.31), channel_id=1, source_target_pairs={{0,1},{1,2},{2,3},{3,4},{4,5},{5,6},{6,7},{7,0},{8,9},{9,10},{10,1... | collective-permute-start | bytes 442376 | tf_op jit(solution)/shard_map/ppermute | solution.py:47
  11.4 12.2 %collective-permute-start.2 = (bf16[144,512]{1,0:T(8,128)(2,1)S(1)}, bf16[144,512]{1,0:T(8,128)(2,1)S(1)}, u32[]{:S(2)}, u32[]{:S(2)}) collective-permute-start(bf16[144,512]{1,0:T(8,128)(2,1)S(1)} %get-tuple-element.32), channel_id=1, source_target_pairs={{0,505},{1,10},{2,507},{3,12},{4,509},{5,14},{6,511},{7,8},{8,1},{... | collective-permute-start | bytes 442376 | tf_op jit(solution)/shard_map/ppermute | solution.py:47
  23.6 5.0 %collective-permute-done.2.refs_3_ = bf16[144,512]{1,0:T(8,128)(2,1)S(1)} collective-permute-done((bf16[144,512]{1,0:T(8,128)(2,1)S(1)}, bf16[144,512]{1,0:T(8,128)(2,1)S(1)}, u32[]{:S(2)}, u32[]{:S(2)}) %collective-permute-start.2) | collective-permute-done | bytes 147488 | tf_op jit(solution)/shard_map/ppermute | solution.py:47
  28.6 9.0 %block.1 = (bf16[72,512]{1,0:T(8,128)(2,1)S(1)}, bf16[72,512]{1,0:T(8,128)(2,1)S(1)}, bf16[72,512]{1,0:T(8,128)(2,1)S(1)}, bf16[72,512]{1,0:T(8,128)(2,1)S(1)}, bf16[32,16,16,128]{3,2,1,0:T(8,128)(2,1)S(1)}) custom-call(s32[3]{0:T(128)S(1)} %add_convert_fusion.3.place, bf16[144,512]{1,0:T(8,128)(2,1)S(1)} %get-tuple-element.29.refs_0_, ...), custom_call_target="tpu_custom_call" | custom-call | flops 2000000000 | bytes 6000000 | tf_op jit(solution)/shard_map/block/pallas_call | solution.py:216
  37.6 10.4 %all_to_all.35 = bf16[2,256,16,128]{3,2,1,0:T(8,128)(2,1)S(1)} all-to-all(bf16[2,256,16,128]{3,2,1,0:T(8,128)(2,1)S(1)} %bitcast.18), channel_id=1, replica_groups=mesh['z2'=2,'z1'=2,'z0'=2,'y2'=2,'y1'=2,'core'=2,'x1'=2,'x0'=2,'y0'=2] {..., dimensions={0} | all-to-all | bytes 4194304 | tf_op jit(solution)/shard_map/all_to_all | solution.py:247
  48.0 1.2 fusion
  49.2 3.6 %all-to-all-start.1 = ((bf16[8,32,16,128]{3,2,1,0:T(8,128)(2,1)}), bf16[8,32,16,128]{3,2,1,0:T(8,128)(2,1)S(1)}, u32[]{:S(2)}, u32[]{:S(2)}) async-start(bf16[8,32,16,128]{3,2,1,0:T(8,128)(2,1)} %bitcast.19), calls=%async_computation.1 | async-start | bytes 2097152 | tf_op jit(solution)/shard_map/all_to_all | solution.py:247
  52.8 2.3 %collective-permute-start.3 = (bf16[72,512]{1,0:T(8,128)(2,1)S(1)}, bf16[72,512]{1,0:T(8,128)(2,1)S(1)}, u32[]{:S(2)}, u32[]{:S(2)}) collective-permute-start(bf16[72,512]{1,0:T(8,128)(2,1)S(1)} %get-tuple-element.40), channel_id=1, source_target_pairs={{8,0},{505,1},{10,2},{507,3},{12,4},{509,5},{14,6},{511,7},{16,8},... | collective-permute-start | bytes 221192 | tf_op jit(solution)/shard_map/ppermute | solution.py:47
  55.1 4.2 %collective-permute-start.4 = (bf16[72,512]{1,0:T(8,128)(2,1)S(1)}, bf16[72,512]{1,0:T(8,128)(2,1)S(1)}, u32[]{:S(2)}, u32[]{:S(2)}) collective-permute-start(bf16[72,512]{1,0:T(8,128)(2,1)S(1)} %get-tuple-element.41), channel_id=1, source_target_pairs={{1,0},{2,1},{3,2},{4,3},{5,4},{6,5},{7,6},{0,7},{9,8},{10,9},{11,1... | collective-permute-start | bytes 221192 | tf_op jit(solution)/shard_map/ppermute | solution.py:47
  59.3 3.0 %collective-permute-start.5 = (bf16[72,512]{1,0:T(8,128)(2,1)S(1)}, bf16[72,512]{1,0:T(8,128)(2,1)S(1)}, u32[]{:S(2)}, u32[]{:S(2)}) collective-permute-start(bf16[72,512]{1,0:T(8,128)(2,1)S(1)} %get-tuple-element.42), channel_id=1, source_target_pairs={{505,0},{10,1},{507,2},{12,3},{509,4},{14,5},{511,6},{8,7},{1,8},{... | collective-permute-start | bytes 221192 | tf_op jit(solution)/shard_map/ppermute | solution.py:47
  62.3 6.6 %all-to-all-done.1 = bf16[8,32,16,128]{3,2,1,0:T(8,128)(2,1)S(1)} async-done(((bf16[8,32,16,128]{3,2,1,0:T(8,128)(2,1)}), bf16[8,32,16,128]{3,2,1,0:T(8,128)(2,1)S(1)}, u32[]{:S(2)}, u32[]{:S(2)}) %all-to-all-start.1) | async-done | bytes 1048608 | tf_op jit(solution)/shard_map/all_to_all | solution.py:247
  69.7 1.3 collective-permute-done.5.refs_3_
  71.0 12.1 %all_to_all.36 = bf16[8,4,16,128]{3,2,1,0:T(8,128)(2,1)S(1)} all-to-all(bf16[8,4,16,128]{3,2,1,0:T(8,128)(2,1)S(1)} %bitcast.21), channel_id=1, replica_groups=mesh['z2'=2,'z1'=2,'z0'=2,'y2'=2,'y1'=2,'core'=2,'x1'=2,'x0'=2,'y0'=2] {..., dimensions={0} | all-to-all | bytes 262144 | tf_op jit(solution)/shard_map/all_to_all | solution.py:247
  83.2 9.3 %all_to_all.37 = bf16[4,4,16,128]{3,2,1,0:T(8,128)(2,1)S(1)} all-to-all(bf16[4,4,16,128]{3,2,1,0:T(8,128)(2,1)S(1)} %broadcast_in_dim.31), channel_id=1, replica_groups=mesh['z2'=2,'z1'=2,'z0'=2,'y2'=2,'y1'=2,'core'=2,'x1'=2,'x0'=2,'y0'=2] {..., dimensions={0} | all-to-all | bytes 131072 | tf_op jit(solution)/shard_map/all_to_all | solution.py:252
  92.5 12.9 %all_to_all.38 = bf16[8,4,16,128]{3,2,1,0:T(8,128)(2,1)S(1)} all-to-all(bf16[8,4,16,128]{3,2,1,0:T(8,128)(2,1)S(1)} %broadcast_in_dim.33), channel_id=1, replica_groups=mesh['z2'=2,'z1'=2,'z0'=2,'y2'=2,'y1'=2,'core'=2,'x1'=2,'x0'=2,'y0'=2] {..., dimensions={0} | all-to-all | bytes 262144 | tf_op jit(solution)/shard_map/all_to_all | solution.py:252
  105.4 1.1 broadcast_in_dim.35
  106.5 5.0 %all-to-all-start.5 = ((bf16[8,32,16,128]{3,2,1,0:T(8,128)(2,1)}), bf16[8,32,16,128]{3,2,1,0:T(8,128)(2,1)S(1)}, u32[]{:S(2)}, u32[]{:S(2)}) async-start(bf16[8,32,16,128]{3,2,1,0:T(8,128)(2,1)} %broadcast_in_dim.35), calls=%async_computation.5 | async-start | bytes 2097152 | tf_op jit(solution)/shard_map/all_to_all | solution.py:252
  112.2 0.9 copy.10
  113.1 11.1 %all-to-all-done.5 = bf16[8,32,16,128]{3,2,1,0:T(8,128)(2,1)S(1)} async-done(((bf16[8,32,16,128]{3,2,1,0:T(8,128)(2,1)}), bf16[8,32,16,128]{3,2,1,0:T(8,128)(2,1)S(1)}, u32[]{:S(2)}, u32[]{:S(2)}) %all-to-all-start.5) | async-done | bytes 1048608 | tf_op jit(solution)/shard_map/all_to_all | solution.py:252
  124.5 8.7 %all_to_all.39 = bf16[2,256,16,128]{3,2,1,0:T(8,128)(2,1)S(1)} all-to-all(bf16[2,256,16,128]{3,2,1,0:T(8,128)(2,1)S(1)} %broadcast_in_dim.37), channel_id=1, replica_groups=mesh['z2'=2,'z1'=2,'z0'=2,'y2'=2,'y1'=2,'core'=2,'x1'=2,'x0'=2,'y0'=2] {..., dimensions={0} | all-to-all | bytes 4194304 | tf_op jit(solution)/shard_map/all_to_all | solution.py:252
  133.2 1.7 %untile.1 = (bf16[512,1536]{1,0:T(8,128)(2,1)}, bf16[512,512]{1,0:T(8,128)(2,1)}) custom-call(bf16[32,16,16,128]{3,2,1,0:T(8,128)(2,1)S(1)} %bitcast.17), custom_call_target="tpu_custom_call" | custom-call | bytes 4194304 | tf_op jit(solution)/shard_map/untile/pallas_call | solution.py:282
  (17 shorter events, 2.7 us)
Async XLA Ops:
  0.6 27.9 %copy-start.1 = (bf16[512,512]{1,0:T(8,128)(2,1)S(1)}, bf16[512,512]{1,0:T(8,128)(2,1)}, u32[]{:S(2)}) copy-start(bf16[512,512]{1,0:T(8,128)(2,1)} %refs_5_.1) | copy-start | bytes 1572868
  0.6 27.9 %copy-start = (bf16[512,1536]{1,0:T(8,128)(2,1)S(1)}, bf16[512,1536]{1,0:T(8,128)(2,1)}, u32[]{:S(2)}) copy-start(bf16[512,1536]{1,0:T(8,128)(2,1)} %refs_4_.1) | copy-start | bytes 4718596
  3.9 19.7 %collective-permute-start = (bf16[144,512]{1,0:T(8,128)(2,1)S(1)}, bf16[144,512]{1,0:T(8,128)(2,1)S(1)}, u32[]{:S(2)}, u32[]{:S(2)}) collective-permute-start(bf16[144,512]{1,0:T(8,128)(2,1)S(1)} %get-tuple-element.30), channel_id=1, source_target_pairs={{0,8},{1,505},{2,10},{3,507},{4,12},{5,509},{6,14},{7,511},{8,16},... | collective-permute-start | bytes 442376 | tf_op jit(solution)/shard_map/ppermute | solution.py:47
  9.5 14.1 %collective-permute-start.1 = (bf16[144,512]{1,0:T(8,128)(2,1)S(1)}, bf16[144,512]{1,0:T(8,128)(2,1)S(1)}, u32[]{:S(2)}, u32[]{:S(2)}) collective-permute-start(bf16[144,512]{1,0:T(8,128)(2,1)S(1)} %get-tuple-element.31), channel_id=1, source_target_pairs={{0,1},{1,2},{2,3},{3,4},{4,5},{5,6},{6,7},{7,0},{8,9},{9,10},{10,1... | collective-permute-start | bytes 442376 | tf_op jit(solution)/shard_map/ppermute | solution.py:47
  11.4 17.2 %collective-permute-start.2 = (bf16[144,512]{1,0:T(8,128)(2,1)S(1)}, bf16[144,512]{1,0:T(8,128)(2,1)S(1)}, u32[]{:S(2)}, u32[]{:S(2)}) collective-permute-start(bf16[144,512]{1,0:T(8,128)(2,1)S(1)} %get-tuple-element.32), channel_id=1, source_target_pairs={{0,505},{1,10},{2,507},{3,12},{4,509},{5,14},{6,511},{7,8},{8,1},{... | collective-permute-start | bytes 442376 | tf_op jit(solution)/shard_map/ppermute | solution.py:47
  49.2 19.7 %all-to-all-start.1 = ((bf16[8,32,16,128]{3,2,1,0:T(8,128)(2,1)}), bf16[8,32,16,128]{3,2,1,0:T(8,128)(2,1)S(1)}, u32[]{:S(2)}, u32[]{:S(2)}) async-start(bf16[8,32,16,128]{3,2,1,0:T(8,128)(2,1)} %bitcast.19), calls=%async_computation.1 | async-start | bytes 2097152 | tf_op jit(solution)/shard_map/all_to_all | solution.py:247
  52.8 16.3 %collective-permute-start.3 = (bf16[72,512]{1,0:T(8,128)(2,1)S(1)}, bf16[72,512]{1,0:T(8,128)(2,1)S(1)}, u32[]{:S(2)}, u32[]{:S(2)}) collective-permute-start(bf16[72,512]{1,0:T(8,128)(2,1)S(1)} %get-tuple-element.40), channel_id=1, source_target_pairs={{8,0},{505,1},{10,2},{507,3},{12,4},{509,5},{14,6},{511,7},{16,8},... | collective-permute-start | bytes 221192 | tf_op jit(solution)/shard_map/ppermute | solution.py:47
  55.1 14.6 %collective-permute-start.4 = (bf16[72,512]{1,0:T(8,128)(2,1)S(1)}, bf16[72,512]{1,0:T(8,128)(2,1)S(1)}, u32[]{:S(2)}, u32[]{:S(2)}) collective-permute-start(bf16[72,512]{1,0:T(8,128)(2,1)S(1)} %get-tuple-element.41), channel_id=1, source_target_pairs={{1,0},{2,1},{3,2},{4,3},{5,4},{6,5},{7,6},{0,7},{9,8},{10,9},{11,1... | collective-permute-start | bytes 221192 | tf_op jit(solution)/shard_map/ppermute | solution.py:47
  59.3 11.7 %collective-permute-start.5 = (bf16[72,512]{1,0:T(8,128)(2,1)S(1)}, bf16[72,512]{1,0:T(8,128)(2,1)S(1)}, u32[]{:S(2)}, u32[]{:S(2)}) collective-permute-start(bf16[72,512]{1,0:T(8,128)(2,1)S(1)} %get-tuple-element.42), channel_id=1, source_target_pairs={{505,0},{10,1},{507,2},{12,3},{509,4},{14,5},{511,6},{8,7},{1,8},{... | collective-permute-start | bytes 221192 | tf_op jit(solution)/shard_map/ppermute | solution.py:47
  106.5 17.8 %all-to-all-start.5 = ((bf16[8,32,16,128]{3,2,1,0:T(8,128)(2,1)}), bf16[8,32,16,128]{3,2,1,0:T(8,128)(2,1)S(1)}, u32[]{:S(2)}, u32[]{:S(2)}) async-start(bf16[8,32,16,128]{3,2,1,0:T(8,128)(2,1)} %broadcast_in_dim.35), calls=%async_computation.5 | async-start | bytes 2097152 | tf_op jit(solution)/shard_map/all_to_all | solution.py:252

commit v2 on v1

--- a/solution.py
+++ b/solution.py
@@ -19,12 +19,9 @@
 WINDOW = 4 * QUARTER
 TOKENS = 2 * WINDOW
 
-LON = ("z2", "z1", "z0", "y2", "y1", "core")
-LAT = ("x1", "x0", "y0")
-CORE = ("core",)
-NEAR = ("z0", "y0", "x0")
-MIDDLE = ("x1", "z2", "z1")
-FAR = ("y2", "y1")
+LON = ("z", "y_hi", "core")
+LAT = ("x", "y_lo")
+ALL = LON + LAT
 
 
 def dot(a, b, a_dim, b_dim):
@@ -44,7 +41,7 @@
             to_lat, to_lon = owner_of(kind, lat, lon)
             pair = (lon * lats + lat, to_lon % lons * lats + to_lat % lats)
             pairs.append(pair[::-1] if back else pair)
-    return lax.ppermute(value, LON + LAT, pairs)
+    return lax.ppermute(value, ALL, pairs)
 
 
 def token_labels(token, window, lat_edge, lon_edge):
@@ -241,36 +238,99 @@
     return total
 
 
-def scattered_sum(tiles, axes):
-    groups = lax.axis_size(axes)
-    split = tiles.reshape((groups, tiles.shape[0] // groups) + tiles.shape[1:])
-    return added(lax.all_to_all(split, axes, 0, 0))
-
-
-def exchanged(tiles, axes):
-    groups = lax.axis_size(axes)
-    return lax.all_to_all(jnp.broadcast_to(tiles[None], (groups,) + tiles.shape), axes, 0, 0)
+def device_groups(members):
+    tall, wide = lax.axis_size("y_hi"), lax.axis_size("x")
+    cores, y_los = lax.axis_size("core"), lax.axis_size("y_lo")
+
+    def index(z, y, x, core):
+        return (((z * tall + y // y_los) * cores + core) * wide + x) * y_los + y % y_los
+
+    return [[index(*at, core) for at in group] for core in range(cores) for group in members(core)]
+
+
+def chips():
+    return lax.axis_size("z"), lax.axis_size("y_hi") * lax.axis_size("y_lo"), lax.axis_size("x")
+
+
+def near_groups():
+    def along(size, core):
+        if size == 1:
+            return [[0]]
+        return [[(2 * at + 2 * core) % size, 2 * at + 1] for at in range(size // 2)]
+
+    def members(core):
+        zs, ys, xs = (along(size, core) for size in chips())
+        return [[(z, y, x) for z in za for y in ya for x in xa] for za in zs for ya in ys for xa in xs]
+
+    return device_groups(members)
+
+
+def strided(size):
+    step = min(size, 2)
+    return [list(range(parity, size, step)) for parity in range(step)]
+
+
+def middle_groups():
+    def members(core):
+        z_size, y_size, x_size = chips()
+        xs = strided(x_size)
+        if core == 0:
+            return [[(z, y, x) for x in xa for z in za] for xa in xs for za in strided(z_size) for y in range(y_size)]
+        return [[(z, y, x) for x in xa for y in ya] for xa in xs for ya in strided(y_size) for z in range(z_size)]
+
+    return device_groups(members)
+
+
+def far_groups():
+    def members(core):
+        z_size, y_size, x_size = chips()
+        if core == 0:
+            return [[(z, y, x) for y in ya] for ya in strided(y_size) for z in range(z_size) for x in range(x_size)]
+        return [[(z, y, x) for z in za] for za in strided(z_size) for y in range(y_size) for x in range(x_size)]
+
+    return device_groups(members)
+
+
+def core_groups():
+    z_size, y_size, x_size = chips()
+    at = [(z, y, x) for z in range(z_size) for y in range(y_size) for x in range(x_size)]
+    singles = device_groups(lambda core: [at])
+    return [list(pair) for pair in zip(*singles)]
+
+
+def all_to_all(split, groups):
+    return lax.all_to_all(split, ALL, 0, 0, axis_index_groups=groups)
+
+
+def scattered_sum(tiles, groups):
+    count = len(groups[0])
+    split = tiles.reshape((count, tiles.shape[0] // count) + tiles.shape[1:])
+    return added(all_to_all(split, groups)).astype(jnp.bfloat16)
+
+
+def exchanged(tiles, groups):
+    return all_to_all(jnp.broadcast_to(tiles[None], (len(groups[0]),) + tiles.shape), groups)
+
+
+def gathered(tiles, groups):
+    return exchanged(tiles, groups).reshape((-1,) + tiles.shape[1:])
 
 
 def summed_over_mesh(tiles, factor, branch):
-    tiles = scattered_sum(tiles, CORE).astype(jnp.bfloat16)
-    tiles, branch = lax.optimization_barrier((tiles, branch))
-    tiles = scattered_sum(tiles, NEAR).astype(jnp.bfloat16)
-    quarters = [branch[0]] + [moved(branch[kind], kind, True) for kind in range(1, 4)]
-    tiles, quarters = lax.optimization_barrier((tiles, quarters))
-    tiles = scattered_sum(tiles, MIDDLE).astype(jnp.bfloat16)
-    tiles = (added(exchanged(tiles, FAR)) * factor).astype(jnp.bfloat16)
-    tiles, quarters = lax.optimization_barrier((exchanged(tiles, MIDDLE), quarters))
-    tiles = tiles.reshape((-1,) + tiles.shape[2:])
-    for axes in (NEAR, CORE):
-        tiles = exchanged(tiles, axes)
-        tiles = tiles.reshape((-1,) + tiles.shape[2:])
-    return tiles, quarters
+    core, near, middle, far = core_groups(), near_groups(), middle_groups(), far_groups()
+    lon = moved(branch[1], 1, True)
+    tiles, lat, both = lax.optimization_barrier((scattered_sum(tiles, core), *branch[2:]))
+    tiles, lon, lat = lax.optimization_barrier((scattered_sum(tiles, near), lon, moved(lat, 2, True)))
+    tiles = scattered_sum(tiles, middle)
+    tiles = (added(exchanged(tiles, far)) * factor).astype(jnp.bfloat16)
+    tiles, both = lax.optimization_barrier((gathered(tiles, middle), both))
+    tiles, both = lax.optimization_barrier((gathered(tiles, near), moved(both, 3, True)))
+    return gathered(tiles, core), (branch[0], lon, lat, both)
 
 
 def untile_kernel(tiles, qkv_out, proj_out):
     for col in range(4 * D // 128):
-        strip = tiles[:, col].reshape(D, 128)
+        strip = tiles[:, col].reshape(-1, 128)
         if col < 3 * D // 128:
             qkv_out[:, 128 * col : 128 * col + 128] = strip
         else:
@@ -278,12 +338,16 @@
 
 
 def untile(tiles):
-    whole = pl.BlockSpec(memory_space=pltpu.VMEM)
+    steps = 4
     return pl.pallas_call(
         untile_kernel,
+        grid=(steps,),
         out_shape=(jax.ShapeDtypeStruct((D, 3 * D), jnp.bfloat16), jax.ShapeDtypeStruct((D, D), jnp.bfloat16)),
-        in_specs=[whole],
-        out_specs=(whole, whole),
+        in_specs=[pl.BlockSpec((D // 16 // steps, 4 * D // 128, 16, 128), lambda i: (i, 0, 0, 0))],
+        out_specs=(
+            pl.BlockSpec((D // steps, 3 * D), lambda i: (i, 0)),
+            pl.BlockSpec((D // steps, D), lambda i: (i, 0)),
+        ),
         compiler_params=pltpu.CompilerParams(vmem_limit_bytes=32 * 2**20),
         cost_estimate=pl.CostEstimate(flops=0, bytes_accessed=4 * 2**20, transcendentals=0),
         name="untile",
@@ -298,7 +362,7 @@
     quarters = pack(place, activations, cotangent)
     quarters = [quarters[0]] + [moved(quarters[kind], kind, False) for kind in range(1, 4)]
     *branch, grads = block(place, quarters, qkv_weight, proj_weight)
-    factor = (LEVELS * ROWS * COLS * lax.axis_size(LON + LAT)) ** (-0.5)
+    factor = (LEVELS * ROWS * COLS * lax.axis_size(ALL)) ** (-0.5)
     tiles, quarters = summed_over_mesh(grads.reshape(-1, 16, 128), factor, branch)
     qkv_weight_grad, proj_weight_grad = untile(tiles.reshape(D // 16, 4 * D // 128, 16, 128))
     return (unpack(place, cotangent, quarters), qkv_weight_grad, proj_weight_grad)
@@ -316,4 +380,4 @@
 
 
 def solution(mesh):
-    return over(Mesh(mesh.devices.reshape((2,) * 9), LON + LAT))
+    return over(Mesh(mesh.devices.reshape(8, 4, 2, 4, 2), ALL))

time: 135 us -> 130 us (0.963)
  waiting for transfers between devices: 24.6 us -> 17.7 us
  starting transfers between devices: 37.7 us -> 41.6 us
  blocking collectives: 53.4 us -> 50.3 us
    all_to_all x2, waiting for transfers between devices: 17.7 us -> 6.96 us  [all_to_all(): return lax.all_to_all(split, ALL, 0, 0, axis_index_groups=groups)]
    ppermute x6, starting transfers between devices: 29.1 us -> 34.2 us  [moved(): return lax.ppermute(value, ALL, pairs)]
    ppermute x6, waiting for transfers between devices: 6.9 us -> 10.8 us  [moved(): return lax.ppermute(value, ALL, pairs)]
    all_to_all x5, blocking collectives: 53.4 us -> 50.3 us  [all_to_all(): return lax.all_to_all(split, ALL, 0, 0, axis_index_groups=groups)]
  transfers between devices with their start and end apart: 8 -> 8, of which waited for: 5 -> 4; matrix products, arithmetic and copies ran while one was open for 1% -> 0% of each run, Pallas kernels for 1% -> 0%
where the time goes in v2:
time: 130 us; the launch traced here: 129 us
  blocking collectives  50.3 us (39%)
  starting transfers between devices  41.6 us (32%)
  waiting for transfers between devices  17.7 us (14%)
  Pallas kernels  12.5 us (10%)
  local copies, waits for them, and re-layouts  4.56 us (4%)
  other arithmetic  1.5 us (1%)
    all_to_all x5, blocking collectives, all_to_all(): return lax.all_to_all(split, ALL, 0, 0, axis_index_groups=groups)  50.3 us
    ppermute x6, starting transfers between devices, moved(): return lax.ppermute(value, ALL, pairs)  34.2 us
    ppermute x6, waiting for transfers between devices, moved(): return lax.ppermute(value, ALL, pairs)  10.8 us
    pallas_call x1, Pallas kernels, block(): pl.pallas_call(block_kernel, out_shape=(jax.ShapeDtypeStruct((2 * QUARTER...  9.02 us
    all_to_all x2, starting transfers between devices, all_to_all(): return lax.all_to_all(split, ALL, 0, 0, axis_index_groups=groups)  7.36 us
    all_to_all x2, waiting for transfers between devices, all_to_all(): return lax.all_to_all(split, ALL, 0, 0, axis_index_groups=groups)  6.96 us
    unnamed x7, local copies, waits for them, and re-layouts  3.15 us
  transfers between devices with their start and end apart: 8, of which 4 were waited for; matrix products, arithmetic and copies ran while one was open for 0% of the time, Pallas kernels for 0%

profile of v2, /device:TPU:1, one launch (start us, length us, event | category | flops | bytes accessed | tf_op | source)
XLA Modules:
  0.0 129.0 jit_solution(7732729014208557456)
XLA Ops:
  0.7 1.2 copy.9.cot_ref
  1.9 1.0 copy.7.act_ref
  3.0 0.9 pack.1
  3.8 5.6 %collective-permute-start = (bf16[144,512]{1,0:T(8,128)(2,1)S(1)}, bf16[144,512]{1,0:T(8,128)(2,1)S(1)}, u32[]{:S(2)}, u32[]{:S(2)}) collective-permute-start(bf16[144,512]{1,0:T(8,128)(2,1)S(1)} %get-tuple-element.25), channel_id=1, source_target_pairs={{0,8},{1,505},{2,10},{3,507},{4,12},{5,509},{6,14},{7,511},{8,16},... | collective-permute-start | bytes 442376 | tf_op jit(solution)/shard_map/ppermute | solution.py:44
  9.5 1.9 %collective-permute-start.1 = (bf16[144,512]{1,0:T(8,128)(2,1)S(1)}, bf16[144,512]{1,0:T(8,128)(2,1)S(1)}, u32[]{:S(2)}, u32[]{:S(2)}) collective-permute-start(bf16[144,512]{1,0:T(8,128)(2,1)S(1)} %get-tuple-element.26), channel_id=1, source_target_pairs={{0,1},{1,2},{2,3},{3,4},{4,5},{5,6},{6,7},{7,0},{8,9},{9,10},{10,1... | collective-permute-start | bytes 442376 | tf_op jit(solution)/shard_map/ppermute | solution.py:44
  11.4 12.2 %collective-permute-start.2 = (bf16[144,512]{1,0:T(8,128)(2,1)S(1)}, bf16[144,512]{1,0:T(8,128)(2,1)S(1)}, u32[]{:S(2)}, u32[]{:S(2)}) collective-permute-start(bf16[144,512]{1,0:T(8,128)(2,1)S(1)} %get-tuple-element.27), channel_id=1, source_target_pairs={{0,505},{1,10},{2,507},{3,12},{4,509},{5,14},{6,511},{7,8},{8,1},{... | collective-permute-start | bytes 442376 | tf_op jit(solution)/shard_map/ppermute | solution.py:44
  23.6 5.0 %collective-permute-done.2.refs_3_ = bf16[144,512]{1,0:T(8,128)(2,1)S(1)} collective-permute-done((bf16[144,512]{1,0:T(8,128)(2,1)S(1)}, bf16[144,512]{1,0:T(8,128)(2,1)S(1)}, u32[]{:S(2)}, u32[]{:S(2)}) %collective-permute-start.2) | collective-permute-done | bytes 147488 | tf_op jit(solution)/shard_map/ppermute | solution.py:44
  28.6 9.0 %block.1 = (bf16[72,512]{1,0:T(8,128)(2,1)S(1)}, bf16[72,512]{1,0:T(8,128)(2,1)S(1)}, bf16[72,512]{1,0:T(8,128)(2,1)S(1)}, bf16[72,512]{1,0:T(8,128)(2,1)S(1)}, bf16[32,16,16,128]{3,2,1,0:T(8,128)(2,1)S(1)}) custom-call(s32[3]{0:T(128)S(1)} %add_convert_fusion.3.place, bf16[144,512]{1,0:T(8,128)(2,1)S(1)} %get-tuple-element.24.refs_0_, ...), custom_call_target="tpu_custom_call" | custom-call | flops 2000000000 | bytes 6000000 | tf_op jit(solution)/shard_map/block/pallas_call | solution.py:213
  37.6 10.4 %all_to_all.35 = bf16[2,256,16,128]{3,2,1,0:T(8,128)(2,1)S(1)} all-to-all(bf16[2,256,16,128]{3,2,1,0:T(8,128)(2,1)S(1)} %bitcast.18), channel_id=1, replica_groups={{0,8},{2,10},{4,12},{6,14},{1,9},{3,11},{5,13},{7,15},{16,24},{18,26},{..., dimensions={0} | all-to-all | bytes 4194304 | tf_op jit(solution)/shard_map/all_to_all | solution.py:302
  48.0 1.2 fusion
  49.2 3.6 %all-to-all-start.1 = ((bf16[8,32,16,128]{3,2,1,0:T(8,128)(2,1)}), bf16[8,32,16,128]{3,2,1,0:T(8,128)(2,1)S(1)}, u32[]{:S(2)}, u32[]{:S(2)}) async-start(bf16[8,32,16,128]{3,2,1,0:T(8,128)(2,1)} %bitcast.20), calls=%async_computation.1 | async-start | bytes 2097152 | tf_op jit(solution)/shard_map/all_to_all | solution.py:302
  52.8 2.0 %collective-permute-start.4 = (bf16[72,512]{1,0:T(8,128)(2,1)S(1)}, bf16[72,512]{1,0:T(8,128)(2,1)S(1)}, u32[]{:S(2)}, u32[]{:S(2)}) collective-permute-start(bf16[72,512]{1,0:T(8,128)(2,1)S(1)} %get-tuple-element.34), channel_id=1, source_target_pairs={{1,0},{2,1},{3,2},{4,3},{5,4},{6,5},{7,6},{0,7},{9,8},{10,9},{11,1... | collective-permute-start | bytes 221192 | tf_op jit(solution)/shard_map/ppermute | solution.py:44
  54.8 5.4 %collective-permute-start.3 = (bf16[72,512]{1,0:T(8,128)(2,1)S(1)}, bf16[72,512]{1,0:T(8,128)(2,1)S(1)}, u32[]{:S(2)}, u32[]{:S(2)}) collective-permute-start(bf16[72,512]{1,0:T(8,128)(2,1)S(1)} %get-tuple-element.33), channel_id=1, source_target_pairs={{8,0},{505,1},{10,2},{507,3},{12,4},{509,5},{14,6},{511,7},{16,8},... | collective-permute-start | bytes 221192 | tf_op jit(solution)/shard_map/ppermute | solution.py:44
  60.2 6.2 %all-to-all-done.1 = bf16[8,32,16,128]{3,2,1,0:T(8,128)(2,1)S(1)} async-done(((bf16[8,32,16,128]{3,2,1,0:T(8,128)(2,1)}), bf16[8,32,16,128]{3,2,1,0:T(8,128)(2,1)S(1)}, u32[]{:S(2)}, u32[]{:S(2)}) %all-to-all-start.1) | async-done | bytes 1048608 | tf_op jit(solution)/shard_map/all_to_all | solution.py:302
  66.6 13.5 %all_to_all.36 = bf16[8,4,16,128]{3,2,1,0:T(8,128)(2,1)S(1)} all-to-all(bf16[8,4,16,128]{3,2,1,0:T(8,128)(2,1)S(1)} %bitcast.21), channel_id=1, replica_groups={{0,128,256,384,4,132,260,388},{1,129,257,385,5,133,261,389},{16,144,272..., dimensions={0} | all-to-all | bytes 262144 | tf_op jit(solution)/shard_map/all_to_all | solution.py:302
  80.1 9.3 %all_to_all.37 = bf16[4,4,16,128]{3,2,1,0:T(8,128)(2,1)S(1)} all-to-all(bf16[4,4,16,128]{3,2,1,0:T(8,128)(2,1)S(1)} %broadcast_in_dim.13), channel_id=1, replica_groups={{0,16,32,48},{2,18,34,50},{4,20,36,52},{6,22,38,54},{64,80,96,112},{66,..., dimensions={0} | all-to-all | bytes 131072 | tf_op jit(solution)/shard_map/all_to_all | solution.py:302
  89.4 11.8 %all_to_all.38 = bf16[8,4,16,128]{3,2,1,0:T(8,128)(2,1)S(1)} all-to-all(bf16[8,4,16,128]{3,2,1,0:T(8,128)(2,1)S(1)} %broadcast_in_dim.15), channel_id=1, replica_groups={{0,128,256,384,4,132,260,388},{1,129,257,385,5,133,261,389},{16,144,272..., dimensions={0} | all-to-all | bytes 262144 | tf_op jit(solution)/shard_map/all_to_all | solution.py:302
  101.2 1.1 broadcast_in_dim.32
  102.3 3.8 %all-to-all-start.5 = ((bf16[8,32,16,128]{3,2,1,0:T(8,128)(2,1)}), bf16[8,32,16,128]{3,2,1,0:T(8,128)(2,1)S(1)}, u32[]{:S(2)}, u32[]{:S(2)}) async-start(bf16[8,32,16,128]{3,2,1,0:T(8,128)(2,1)} %broadcast_in_dim.32), calls=%async_computation.5 | async-start | bytes 2097152 | tf_op jit(solution)/shard_map/all_to_all | solution.py:302
  106.1 7.1 %collective-permute-start.5 = (bf16[72,512]{1,0:T(8,128)(2,1)S(1)}, bf16[72,512]{1,0:T(8,128)(2,1)S(1)}, u32[]{:S(2)}, u32[]{:S(2)}) collective-permute-start(bf16[72,512]{1,0:T(8,128)(2,1)S(1)} %get-tuple-element.40), channel_id=1, source_target_pairs={{505,0},{10,1},{507,2},{12,3},{509,4},{14,5},{511,6},{8,7},{1,8},{... | collective-permute-start | bytes 221192 | tf_op jit(solution)/shard_map/ppermute | solution.py:44
  113.3 5.8 %collective-permute-done.5.refs_3_ = bf16[72,512]{1,0:T(8,128)(2,1)S(1)} collective-permute-done((bf16[72,512]{1,0:T(8,128)(2,1)S(1)}, bf16[72,512]{1,0:T(8,128)(2,1)S(1)}, u32[]{:S(2)}, u32[]{:S(2)}) %collective-permute-start.5) | collective-permute-done | bytes 73760 | tf_op jit(solution)/shard_map/ppermute | solution.py:44
  120.5 0.9 copy.10
  121.7 5.4 %all_to_all.39 = bf16[2,256,16,128]{3,2,1,0:T(8,128)(2,1)S(1)} all-to-all(bf16[2,256,16,128]{3,2,1,0:T(8,128)(2,1)S(1)} %broadcast_in_dim.33), channel_id=1, replica_groups={{0,8},{2,10},{4,12},{6,14},{1,9},{3,11},{5,13},{7,15},{16,24},{18,26},{..., dimensions={0} | all-to-all | bytes 4194304 | tf_op jit(solution)/shard_map/all_to_all | solution.py:302
  127.1 1.9 %untile.1 = (bf16[512,1536]{1,0:T(8,128)(2,1)}, bf16[512,512]{1,0:T(8,128)(2,1)}) custom-call(bf16[32,16,16,128]{3,2,1,0:T(8,128)(2,1)S(1)} %bitcast.17), custom_call_target="tpu_custom_call" | custom-call | bytes 4194304 | tf_op jit(solution)/shard_map/untile/pallas_call | solution.py:342
  (17 shorter events, 2.0 us)
Async XLA Ops:
  0.6 27.9 %copy-start.1 = (bf16[512,512]{1,0:T(8,128)(2,1)S(1)}, bf16[512,512]{1,0:T(8,128)(2,1)}, u32[]{:S(2)}) copy-start(bf16[512,512]{1,0:T(8,128)(2,1)} %refs_5_.1) | copy-start | bytes 1572868
  0.6 27.9 %copy-start = (bf16[512,1536]{1,0:T(8,128)(2,1)S(1)}, bf16[512,1536]{1,0:T(8,128)(2,1)}, u32[]{:S(2)}) copy-start(bf16[512,1536]{1,0:T(8,128)(2,1)} %refs_4_.1) | copy-start | bytes 4718596
  3.8 19.7 %collective-permute-start = (bf16[144,512]{1,0:T(8,128)(2,1)S(1)}, bf16[144,512]{1,0:T(8,128)(2,1)S(1)}, u32[]{:S(2)}, u32[]{:S(2)}) collective-permute-start(bf16[144,512]{1,0:T(8,128)(2,1)S(1)} %get-tuple-element.25), channel_id=1, source_target_pairs={{0,8},{1,505},{2,10},{3,507},{4,12},{5,509},{6,14},{7,511},{8,16},... | collective-permute-start | bytes 442376 | tf_op jit(solution)/shard_map/ppermute | solution.py:44
  9.5 14.1 %collective-permute-start.1 = (bf16[144,512]{1,0:T(8,128)(2,1)S(1)}, bf16[144,512]{1,0:T(8,128)(2,1)S(1)}, u32[]{:S(2)}, u32[]{:S(2)}) collective-permute-start(bf16[144,512]{1,0:T(8,128)(2,1)S(1)} %get-tuple-element.26), channel_id=1, source_target_pairs={{0,1},{1,2},{2,3},{3,4},{4,5},{5,6},{6,7},{7,0},{8,9},{9,10},{10,1... | collective-permute-start | bytes 442376 | tf_op jit(solution)/shard_map/ppermute | solution.py:44
  11.4 17.2 %collective-permute-start.2 = (bf16[144,512]{1,0:T(8,128)(2,1)S(1)}, bf16[144,512]{1,0:T(8,128)(2,1)S(1)}, u32[]{:S(2)}, u32[]{:S(2)}) collective-permute-start(bf16[144,512]{1,0:T(8,128)(2,1)S(1)} %get-tuple-element.27), channel_id=1, source_target_pairs={{0,505},{1,10},{2,507},{3,12},{4,509},{5,14},{6,511},{7,8},{8,1},{... | collective-permute-start | bytes 442376 | tf_op jit(solution)/shard_map/ppermute | solution.py:44
  49.2 17.2 %all-to-all-start.1 = ((bf16[8,32,16,128]{3,2,1,0:T(8,128)(2,1)}), bf16[8,32,16,128]{3,2,1,0:T(8,128)(2,1)S(1)}, u32[]{:S(2)}, u32[]{:S(2)}) async-start(bf16[8,32,16,128]{3,2,1,0:T(8,128)(2,1)} %bitcast.20), calls=%async_computation.1 | async-start | bytes 2097152 | tf_op jit(solution)/shard_map/all_to_all | solution.py:302
  52.8 13.8 %collective-permute-start.4 = (bf16[72,512]{1,0:T(8,128)(2,1)S(1)}, bf16[72,512]{1,0:T(8,128)(2,1)S(1)}, u32[]{:S(2)}, u32[]{:S(2)}) collective-permute-start(bf16[72,512]{1,0:T(8,128)(2,1)S(1)} %get-tuple-element.34), channel_id=1, source_target_pairs={{1,0},{2,1},{3,2},{4,3},{5,4},{6,5},{7,6},{0,7},{9,8},{10,9},{11,1... | collective-permute-start | bytes 221192 | tf_op jit(solution)/shard_map/ppermute | solution.py:44
  54.8 11.8 %collective-permute-start.3 = (bf16[72,512]{1,0:T(8,128)(2,1)S(1)}, bf16[72,512]{1,0:T(8,128)(2,1)S(1)}, u32[]{:S(2)}, u32[]{:S(2)}) collective-permute-start(bf16[72,512]{1,0:T(8,128)(2,1)S(1)} %get-tuple-element.33), channel_id=1, source_target_pairs={{8,0},{505,1},{10,2},{507,3},{12,4},{509,5},{14,6},{511,7},{16,8},... | collective-permute-start | bytes 221192 | tf_op jit(solution)/shard_map/ppermute | solution.py:44
  102.3 17.5 %all-to-all-start.5 = ((bf16[8,32,16,128]{3,2,1,0:T(8,128)(2,1)}), bf16[8,32,16,128]{3,2,1,0:T(8,128)(2,1)S(1)}, u32[]{:S(2)}, u32[]{:S(2)}) async-start(bf16[8,32,16,128]{3,2,1,0:T(8,128)(2,1)} %broadcast_in_dim.32), calls=%async_computation.5 | async-start | bytes 2097152 | tf_op jit(solution)/shard_map/all_to_all | solution.py:302
  106.1 12.9 %collective-permute-start.5 = (bf16[72,512]{1,0:T(8,128)(2,1)S(1)}, bf16[72,512]{1,0:T(8,128)(2,1)S(1)}, u32[]{:S(2)}, u32[]{:S(2)}) collective-permute-start(bf16[72,512]{1,0:T(8,128)(2,1)S(1)} %get-tuple-element.40), channel_id=1, source_target_pairs={{505,0},{10,1},{507,2},{12,3},{509,4},{14,5},{511,6},{8,7},{1,8},{... | collective-permute-start | bytes 221192 | tf_op jit(solution)/shard_map/ppermute | solution.py:44

commit v3 on v2

--- a/solution.py
+++ b/solution.py
@@ -1,3 +1,5 @@
+import itertools
+
 import jax
 import jax.numpy as jnp
 from jax import lax
@@ -50,17 +52,25 @@
     return level * window + 2 * lat_edge * (quarter // 2) + 4 * lon_edge * (quarter % 2)
 
 
-def pack_kernel(place, act_ref, cot_ref, own, lon, lat, both):
-    pieces = {(row_half, col_half): [] for row_half in range(2) for col_half in range(2)}
-    for ref in (act_ref, cot_ref):
-        for pair in PAIRS:
-            for level in pair:
-                for row in range(ROWS):
-                    line = ref[level, row].astype(jnp.float32)
-                    for half in range(2):
-                        cut = line[half * HALF_LON : half * HALF_LON + HALF_LON]
-                        pieces[row // HALF_LAT, half].append(cut)
-    whole = {at: jnp.concatenate(cuts, axis=0).astype(jnp.bfloat16) for at, cuts in pieces.items()}
+def pack_kernel(place, act_ref, cot_ref, own, lon, lat, both, lines):
+    whole = {}
+    for row_half in range(2):
+        for col_half in range(2):
+            cuts = []
+            for kind, ref in enumerate((act_ref, cot_ref)):
+                held = [lines.at[4 * (4 * kind + 2 * row_half + col_half) + part] for part in range(4)]
+                for row in range(HALF_LAT):
+                    for col in range(HALF_LON):
+                        token = ref[row_half * HALF_LAT + row, col_half * HALF_LON + col]
+                        token = token.astype(jnp.float32)
+                        for part in range(4):
+                            at = pl.ds(LEVELS * (row * HALF_LON + col), LEVELS)
+                            held[part][at] = token[:, 128 * part : 128 * part + 128]
+                for pair in PAIRS:
+                    for level in pair:
+                        at = pl.ds(level, HALF_LAT * HALF_LON, stride=LEVELS)
+                        cuts.append(jnp.concatenate([part[at] for part in held], axis=1))
+            whole[row_half, col_half] = jnp.concatenate(cuts, axis=0).astype(jnp.bfloat16)
 
     def put(parity):
         own[...] = whole[0, parity]
@@ -79,15 +89,17 @@
         out_shape=(jax.ShapeDtypeStruct((4 * QUARTER, D), jnp.bfloat16),) * 4,
         in_specs=[pl.BlockSpec(memory_space=pltpu.SMEM)] + [whole] * 2,
         out_specs=(whole,) * 4,
+        scratch_shapes=[pltpu.VMEM((32, LEVELS * HALF_LAT * HALF_LON, 128), jnp.float32)],
         compiler_params=pltpu.CompilerParams(vmem_limit_bytes=32 * 2**20),
         cost_estimate=pl.CostEstimate(flops=0, bytes_accessed=1200000, transcendentals=0),
         name="pack",
-    )(place, activations, cotangent)
+    )(place, activations.transpose(1, 2, 0, 3), cotangent.transpose(1, 2, 0, 3))
 
 
 def unpack_kernel(place, cot_ref, *refs):
-    own, lon, lat, both = [ref[...].astype(jnp.float32) for ref in refs[:4]]
-    out = refs[4]
+    own, lon_ref, lat_both, out = refs
+    own, lon = (ref[: 2 * QUARTER].astype(jnp.float32) for ref in (own, lon_ref))
+    lat, both = (lat_both[part * 2 * QUARTER : (part + 1) * 2 * QUARTER].astype(jnp.float32) for part in range(2))
     even = place[0] == 0
     whole = {
         (0, 0): jnp.where(even, own, lon),
@@ -106,12 +118,12 @@
                 out[level, row] = line.astype(jnp.bfloat16)
 
 
-def unpack(place, cotangent, quarters):
+def unpack(place, cotangent, *quarters):
     whole = pl.BlockSpec(memory_space=pltpu.VMEM)
     return pl.pallas_call(
         unpack_kernel,
         out_shape=jax.ShapeDtypeStruct(cotangent.shape, jnp.bfloat16),
-        in_specs=[pl.BlockSpec(memory_space=pltpu.SMEM)] + [whole] * 5,
+        in_specs=[pl.BlockSpec(memory_space=pltpu.SMEM)] + [whole] * 4,
         out_specs=whole,
         compiler_params=pltpu.CompilerParams(vmem_limit_bytes=32 * 2**20),
         cost_estimate=pl.CostEstimate(flops=0, bytes_accessed=900000, transcendentals=0),
@@ -119,9 +131,34 @@
     )(place, cotangent, *quarters)
 
 
+def half_grads(half, normed, attended, qkv_grad, cot_held, tiles):
+    rows = pl.ds(pl.multiple_of(half * (D // 2), D // 2), D // 2)
+
+    def put(step, block):
+        block = block.astype(jnp.bfloat16)
+        for part in range(2):
+            tiles[:, 2 * step + part] = block[:, 128 * part : 128 * part + 128].reshape(D // 32, 16, 128)
+
+    @pl.loop(0, 3 * D // 256)
+    def _(step):
+        cols = pl.ds(pl.multiple_of(step * 256, 256), 256)
+        put(step, dot(normed[:, rows], qkv_grad[:, cols], 0, 0))
+
+    @pl.loop(0, D // 256)
+    def _(step):
+        cols = pl.ds(pl.multiple_of(step * 256, 256), 256)
+        put(step + 3 * D // 256, dot(attended[:, rows], cot_held[:, cols], 0, 0))
+
+
 def block_kernel(place, *refs):
-    quarters, (qkv_weight, proj_weight), branch, (grads_ref, x_held, cot_held) = refs[:4], refs[4:6], refs[6:10], refs[10:13]
-    normed, qkv, upstream, attended, qkv_grad = refs[13:]
+    quarters, weights = refs[:4], refs[4:6]
+    x_held, cot_held, normed, attended, qkv_grad, tiles, qkv, upstream, qkv_weight, proj_weight, arrivals = refs[6:]
+    copies = [
+        pltpu.make_async_copy(source, target, arrivals.at[at])
+        for at, (source, target) in enumerate(zip(weights, (qkv_weight, proj_weight)))
+    ]
+    for copy in copies:
+        copy.start()
     held = [ref[...].astype(jnp.float32) for ref in quarters]
     for kind, target in enumerate((x_held, cot_held)):
         chunks = [
@@ -134,6 +171,9 @@
     centered = x - jnp.mean(x, axis=-1, keepdims=True)
     inverse = lax.rsqrt(jnp.mean(centered * centered, axis=-1, keepdims=True) + 1e-05)
     normed[...] = (centered * inverse).astype(jnp.bfloat16)
+
+    for copy in copies:
+        copy.wait()
 
     @pl.loop(0, 3 * D // 256)
     def _(step):
@@ -180,6 +220,11 @@
             qkv_grad[rows, cols[1]] = dot(score_grad, query, 1, 0).astype(jnp.bfloat16)
             qkv_grad[rows, cols[2]] = dot(low, grad, 1, 0).astype(jnp.bfloat16)
 
+    half_grads(1 - place[3], normed, attended, qkv_grad, cot_held, tiles)
+
+
+def rest_kernel(place, x_held, cot_held, normed, attended, qkv_grad, qkv_weight, tiles, own, lat, lon_both):
+    half_grads(place[3], normed, attended, qkv_grad, cot_held, tiles)
     normed_grad = dot(qkv_grad[...], qkv_weight[...], 1, 1)
     x = x_held[...].astype(jnp.float32)
     centered = x - jnp.mean(x, axis=-1, keepdims=True)
@@ -188,47 +233,51 @@
     average = jnp.mean(normed_grad, axis=-1, keepdims=True)
     product = jnp.mean(normed_grad * xhat, axis=-1, keepdims=True)
     dx = inverse * (normed_grad - average - xhat * product)
-    for quarter in range(4):
-        chunks = [dx[(4 * window + quarter) * QUARTER : (4 * window + quarter + 1) * QUARTER] for window in range(2)]
-        branch[quarter][...] = jnp.concatenate(chunks, axis=0).astype(jnp.bfloat16)
-
-    def put(step, block):
-        block = block.astype(jnp.bfloat16)
-        for half in range(2):
-            grads_ref[:, 2 * step + half] = block[:, 128 * half : 128 * half + 128].reshape(D // 16, 16, 128)
-
-    @pl.loop(0, 3 * D // 256)
-    def _(step):
-        cols = pl.ds(pl.multiple_of(step * 256, 256), 256)
-        put(step, dot(normed[...], qkv_grad[:, cols], 0, 0))
-
-    @pl.loop(0, D // 256)
-    def _(step):
-        cols = pl.ds(pl.multiple_of(step * 256, 256), 256)
-        put(step + 3 * D // 256, dot(attended[...], cot_held[:, cols], 0, 0))
+    for target, kinds in ((own, (0,)), (lat, (2,)), (lon_both, (1, 3))):
+        chunks = [
+            dx[(4 * window + kind) * QUARTER : (4 * window + kind + 1) * QUARTER] for kind in kinds for window in range(2)
+        ]
+        target[...] = jnp.concatenate(chunks, axis=0).astype(jnp.bfloat16)
+
+
+HALF_TILES = jax.ShapeDtypeStruct((D // 32, 4 * D // 128, 16, 128), jnp.bfloat16)
+
+
+def rows_of(count, width=D):
+    return jax.ShapeDtypeStruct((count, width), jnp.bfloat16)
 
 
 def block(place, quarters, qkv_weight, proj_weight):
     whole = pl.BlockSpec(memory_space=pltpu.VMEM)
     return pl.pallas_call(
         block_kernel,
-        out_shape=(jax.ShapeDtypeStruct((2 * QUARTER, D), jnp.bfloat16),) * 4
-        + (jax.ShapeDtypeStruct((D // 16, 4 * D // 128, 16, 128), jnp.bfloat16),),
-        in_specs=[pl.BlockSpec(memory_space=pltpu.SMEM)] + [whole] * 6,
-        out_specs=(whole,) * 5,
+        out_shape=(rows_of(TOKENS),) * 4 + (rows_of(TOKENS, 3 * D), HALF_TILES),
+        in_specs=[pl.BlockSpec(memory_space=pltpu.SMEM)] + [whole] * 4 + [pl.BlockSpec(memory_space=pl.ANY)] * 2,
+        out_specs=(whole,) * 6,
         scratch_shapes=[
-            pltpu.VMEM((TOKENS, D), jnp.bfloat16),
-            pltpu.VMEM((TOKENS, D), jnp.bfloat16),
-            pltpu.VMEM((TOKENS, D), jnp.bfloat16),
             pltpu.VMEM((TOKENS, 3 * D), jnp.bfloat16),
             pltpu.VMEM((TOKENS, D), jnp.bfloat16),
-            pltpu.VMEM((TOKENS, D), jnp.bfloat16),
-            pltpu.VMEM((TOKENS, 3 * D), jnp.bfloat16),
+            pltpu.VMEM((D, 3 * D), jnp.bfloat16),
+            pltpu.VMEM((D, D), jnp.bfloat16),
+            pltpu.SemaphoreType.DMA((2,)),
         ],
         compiler_params=pltpu.CompilerParams(vmem_limit_bytes=48 * 2**20),
         cost_estimate=pl.CostEstimate(flops=2 * 10**9, bytes_accessed=6 * 10**6, transcendentals=6 * 10**5),
         name="block",
     )(place, *quarters, qkv_weight, proj_weight)
+
+
+def rest(place, kept, qkv_weight):
+    whole = pl.BlockSpec(memory_space=pltpu.VMEM)
+    return pl.pallas_call(
+        rest_kernel,
+        out_shape=(HALF_TILES, rows_of(2 * QUARTER), rows_of(2 * QUARTER), rows_of(4 * QUARTER)),
+        in_specs=[pl.BlockSpec(memory_space=pltpu.SMEM)] + [whole] * 6,
+        out_specs=(whole,) * 4,
+        compiler_params=pltpu.CompilerParams(vmem_limit_bytes=48 * 2**20),
+        cost_estimate=pl.CostEstimate(flops=10**9, bytes_accessed=5 * 10**6, transcendentals=300),
+        name="rest",
+    )(place, *kept, qkv_weight)
 
 
 def added(arrived):
@@ -291,11 +340,10 @@
     return device_groups(members)
 
 
-def core_groups():
-    z_size, y_size, x_size = chips()
-    at = [(z, y, x) for z in range(z_size) for y in range(y_size) for x in range(x_size)]
-    singles = device_groups(lambda core: [at])
-    return [list(pair) for pair in zip(*singles)]
+def swapped(value):
+    at = [(z, y, x) for z, y, x in itertools.product(*(range(size) for size in chips()))]
+    first, second = device_groups(lambda core: [at])
+    return lax.ppermute(value, ALL, [*zip(first, second), *zip(second, first)])
 
 
 def all_to_all(split, groups):
@@ -316,19 +364,8 @@
     return exchanged(tiles, groups).reshape((-1,) + tiles.shape[1:])
 
 
-def summed_over_mesh(tiles, factor, branch):
-    core, near, middle, far = core_groups(), near_groups(), middle_groups(), far_groups()
-    lon = moved(branch[1], 1, True)
-    tiles, lat, both = lax.optimization_barrier((scattered_sum(tiles, core), *branch[2:]))
-    tiles, lon, lat = lax.optimization_barrier((scattered_sum(tiles, near), lon, moved(lat, 2, True)))
-    tiles = scattered_sum(tiles, middle)
-    tiles = (added(exchanged(tiles, far)) * factor).astype(jnp.bfloat16)
-    tiles, both = lax.optimization_barrier((gathered(tiles, middle), both))
-    tiles, both = lax.optimization_barrier((gathered(tiles, near), moved(both, 3, True)))
-    return gathered(tiles, core), (branch[0], lon, lat, both)
-
-
-def untile_kernel(tiles, qkv_out, proj_out):
+def untile_kernel(place, tiles, *refs):
+    qkv_out, proj_out = refs[-2:]
     for col in range(4 * D // 128):
         strip = tiles[:, col].reshape(-1, 128)
         if col < 3 * D // 128:
@@ -337,35 +374,59 @@
             proj_out[:, 128 * col - 3 * D : 128 * col - 3 * D + 128] = strip
 
 
-def untile(tiles):
-    steps = 4
+def untile(place, tiles, other, so_far=()):
+    steps = 2
+    half = D // 2
+
+    def at(step, place):
+        core = 1 - place[3] if other else place[3]
+        return (core * steps + step, 0)
+
     return pl.pallas_call(
         untile_kernel,
-        grid=(steps,),
-        out_shape=(jax.ShapeDtypeStruct((D, 3 * D), jnp.bfloat16), jax.ShapeDtypeStruct((D, D), jnp.bfloat16)),
-        in_specs=[pl.BlockSpec((D // 16 // steps, 4 * D // 128, 16, 128), lambda i: (i, 0, 0, 0))],
-        out_specs=(
-            pl.BlockSpec((D // steps, 3 * D), lambda i: (i, 0)),
-            pl.BlockSpec((D // steps, D), lambda i: (i, 0)),
+        grid_spec=pltpu.PrefetchScalarGridSpec(
+            num_scalar_prefetch=1,
+            grid=(steps,),
+            in_specs=[pl.BlockSpec((half // 16 // steps, 4 * D // 128, 16, 128), lambda step, place: (step, 0, 0, 0))]
+            + [pl.BlockSpec(memory_space=pl.ANY)] * len(so_far),
+            out_specs=(pl.BlockSpec((half // steps, 3 * D), at), pl.BlockSpec((half // steps, D), at)),
         ),
+        out_shape=(rows_of(D, 3 * D), rows_of(D)),
+        input_output_aliases={2: 0, 3: 1} if so_far else {},
         compiler_params=pltpu.CompilerParams(vmem_limit_bytes=32 * 2**20),
-        cost_estimate=pl.CostEstimate(flops=0, bytes_accessed=4 * 2**20, transcendentals=0),
-        name="untile",
-    )(tiles)
+        cost_estimate=pl.CostEstimate(flops=0, bytes_accessed=2 * 2**20, transcendentals=0),
+        name="untile_other" if other else "untile_own",
+    )(place, tiles, *so_far)
 
 
 def per_device(activations, cotangent, qkv_weight, proj_weight):
     lat, lon = lax.axis_index(LAT), lax.axis_index(LON)
     odd = lat % 2 == 1
     lon_edge = jnp.where(odd, lon == lax.axis_size(LON) - 1, lon == 0)
-    place = jnp.stack([odd, lat == 0, lon_edge]).astype(jnp.int32)
+    place = jnp.stack([odd, lat == 0, lon_edge, lax.axis_index("core") == 1]).astype(jnp.int32)
     quarters = pack(place, activations, cotangent)
     quarters = [quarters[0]] + [moved(quarters[kind], kind, False) for kind in range(1, 4)]
-    *branch, grads = block(place, quarters, qkv_weight, proj_weight)
+    *kept, theirs = block(place, quarters, qkv_weight, proj_weight)
+    arrived = swapped(theirs)
+    mine, own, lat, lon_both = rest(place, kept, qkv_weight)
+
+    near, middle, far = near_groups(), middle_groups(), far_groups()
+    tiles = (mine.astype(jnp.float32) + arrived.astype(jnp.float32)).astype(jnp.bfloat16)
+    tiles, lon_both = lax.optimization_barrier((tiles.reshape(-1, 16, 128), lon_both))
+    tiles, lon_both = lax.optimization_barrier((scattered_sum(tiles, near), moved(lon_both, 1, True)))
+    tiles = scattered_sum(tiles, middle)
     factor = (LEVELS * ROWS * COLS * lax.axis_size(ALL)) ** (-0.5)
-    tiles, quarters = summed_over_mesh(grads.reshape(-1, 16, 128), factor, branch)
-    qkv_weight_grad, proj_weight_grad = untile(tiles.reshape(D // 16, 4 * D // 128, 16, 128))
-    return (unpack(place, cotangent, quarters), qkv_weight_grad, proj_weight_grad)
+    tiles = (added(exchanged(tiles, far)) * factor).astype(jnp.bfloat16)
+    lat_both = jnp.concatenate([lat, lon_both[2 * QUARTER :]], axis=0)
+    tiles, lat_both = lax.optimization_barrier((gathered(tiles, middle), lat_both))
+    tiles, lat_both = lax.optimization_barrier((gathered(tiles, near), moved(lat_both, 2, True)))
+    tiles = tiles.reshape(HALF_TILES.shape)
+    arrived = swapped(tiles)
+    grads = untile(place, tiles, False)
+    input_grad = unpack(place, cotangent, own, lon_both, lat_both)
+    arrived, grads, input_grad = lax.optimization_barrier((arrived, grads, input_grad))
+    qkv_weight_grad, proj_weight_grad = untile(place, arrived, True, grads)
+    return (input_grad, qkv_weight_grad, proj_weight_grad)
 
 
 def over(physical):

time: 130 us -> 132 us (1.015)
  blocking collectives: 50.3 us -> 21.1 us
  waiting for transfers between devices: 17.7 us -> 34.1 us
  starting transfers between devices: 41.6 us -> 50 us
  Pallas kernels: 12.5 us -> 16.3 us
  local copies, waits for them, and re-layouts: 4.56 us -> 7.19 us
    all_to_all x5 -> x2, blocking collectives: 50.3 us -> 21.1 us  [all_to_all(): return lax.all_to_all(split, ALL, 0, 0, axis_index_groups=groups)]
    all_to_all x2 -> x3, waiting for transfers between devices: 6.96 us -> 26 us  [all_to_all(): return lax.all_to_all(split, ALL, 0, 0, axis_index_groups=groups)]
    ppermute x0 -> x2, starting transfers between devices: none -> 12.5 us  [swapped(): return lax.ppermute(value, ALL, [*zip(first, second), *zip(second, first)])]
    ppermute x6 -> x5, starting transfers between devices: 34.2 us -> 27 us  [moved(): return lax.ppermute(value, ALL, pairs)]
    pallas_call x2 -> x4, Pallas kernels: 10.9 us -> 14.7 us  [the longest x1 7.96 us: block(): pl.pallas_call(block_kernel, out_shape=(rows_of(TOKENS),) * 4 + (rows_of(...]
    all_to_all x2 -> x3, starting transfers between devices: 7.36 us -> 10.5 us  [all_to_all(): return lax.all_to_all(split, ALL, 0, 0, axis_index_groups=groups)]
    ppermute x6 -> x5, waiting for transfers between devices: 10.8 us -> 8.1 us  [moved(): return lax.ppermute(value, ALL, pairs)]
    unnamed x7 -> x14, local copies, waits for them, and re-layouts: 3.15 us -> 5.39 us
  transfers between devices with their start and end apart: 8 -> 10, of which waited for: 4 -> 5; matrix products, arithmetic and copies ran while one was open for 0% -> 0% of each run, Pallas kernels for 0% -> 4%
where the time goes in v3:
time: 132 us; the launch traced here: 131 us
  starting transfers between devices  50 us (38%)
  waiting for transfers between devices  34.1 us (26%)
  blocking collectives  21.1 us (16%)
  Pallas kernels  16.3 us (12%)
  local copies, waits for them, and re-layouts  7.19 us (5%)
  other arithmetic  1.52 us (1%)
    ppermute x5, starting transfers between devices, moved(): return lax.ppermute(value, ALL, pairs)  27 us
    all_to_all x3, waiting for transfers between devices, all_to_all(): return lax.all_to_all(split, ALL, 0, 0, axis_index_groups=groups)  26 us
    all_to_all x2, blocking collectives, all_to_all(): return lax.all_to_all(split, ALL, 0, 0, axis_index_groups=groups)  21.1 us
    ppermute x2, starting transfers between devices, swapped(): return lax.ppermute(value, ALL, [*zip(first, second), *zip(second, first)])  12.5 us
    all_to_all x3, starting transfers between devices, all_to_all(): return lax.all_to_all(split, ALL, 0, 0, axis_index_groups=groups)  10.5 us
    ppermute x5, waiting for transfers between devices, moved(): return lax.ppermute(value, ALL, pairs)  8.1 us
    pallas_call x1, Pallas kernels, block(): pl.pallas_call(block_kernel, out_shape=(rows_of(TOKENS),) * 4 + (rows_of(...  7.96 us
    unnamed x14, local copies, waits for them, and re-layouts  5.39 us
  transfers between devices with their start and end apart: 10, of which 5 were waited for; matrix products, arithmetic and copies ran while one was open for 0% of the time, Pallas kernels for 4%

profile of v3, /device:TPU:1, one launch (start us, length us, event | category | flops | bytes accessed | tf_op | source)
XLA Modules:
  0.0 131.0 jit_solution(14024647889106099472)
XLA Ops:
  3.6 5.6 %collective-permute-start = (bf16[144,512]{1,0:T(8,128)(2,1)S(1)}, bf16[144,512]{1,0:T(8,128)(2,1)S(1)}, u32[]{:S(2)}, u32[]{:S(2)}) collective-permute-start(bf16[144,512]{1,0:T(8,128)(2,1)S(1)} %get-tuple-element.34), channel_id=1, source_target_pairs={{0,8},{1,505},{2,10},{3,507},{4,12},{5,509},{6,14},{7,511},{8,16},... | collective-permute-start | bytes 442376 | tf_op jit(solution)/shard_map/ppermute | solution.py:46
  9.2 1.9 %collective-permute-start.1 = (bf16[144,512]{1,0:T(8,128)(2,1)S(1)}, bf16[144,512]{1,0:T(8,128)(2,1)S(1)}, u32[]{:S(2)}, u32[]{:S(2)}) collective-permute-start(bf16[144,512]{1,0:T(8,128)(2,1)S(1)} %get-tuple-element.35), channel_id=1, source_target_pairs={{0,1},{1,2},{2,3},{3,4},{4,5},{5,6},{6,7},{7,0},{8,9},{9,10},{10,1... | collective-permute-start | bytes 442376 | tf_op jit(solution)/shard_map/ppermute | solution.py:46
  11.1 12.2 %collective-permute-start.2 = (bf16[144,512]{1,0:T(8,128)(2,1)S(1)}, bf16[144,512]{1,0:T(8,128)(2,1)S(1)}, u32[]{:S(2)}, u32[]{:S(2)}) collective-permute-start(bf16[144,512]{1,0:T(8,128)(2,1)S(1)} %get-tuple-element.36), channel_id=1, source_target_pairs={{0,505},{1,10},{2,507},{3,12},{4,509},{5,14},{6,511},{7,8},{8,1},{... | collective-permute-start | bytes 442376 | tf_op jit(solution)/shard_map/ppermute | solution.py:46
  23.3 5.0 %collective-permute-done.2.refs_3_ = bf16[144,512]{1,0:T(8,128)(2,1)S(1)} collective-permute-done((bf16[144,512]{1,0:T(8,128)(2,1)S(1)}, bf16[144,512]{1,0:T(8,128)(2,1)S(1)}, u32[]{:S(2)}, u32[]{:S(2)}) %collective-permute-start.2) | collective-permute-done | bytes 147488 | tf_op jit(solution)/shard_map/ppermute | solution.py:46
  28.3 1.4 %copy-done.3 = bf16[512,1536]{1,0:T(8,128)(2,1)S(1)} copy-done((bf16[512,1536]{1,0:T(8,128)(2,1)S(1)}, bf16[512,1536]{1,0:T(8,128)(2,1)}, u32[]{:S(2)}) %copy-start.3) | copy-done | bytes 1572888
  30.7 8.0 %block.1 = (bf16[288,512]{1,0:T(8,128)(2,1)S(1)}, bf16[288,512]{1,0:T(8,128)(2,1)S(1)}, bf16[288,512]{1,0:T(8,128)(2,1)S(1)}, bf16[288,512]{1,0:T(8,128)(2,1)S(1...) custom-call(s32[4]{0:T(128)S(1)} %add_convert_fusion.3.place, ...), custom_call_target="tpu_custom_call" | custom-call | flops 2000000000 | bytes 6000000 | tf_op jit(solution)/shard_map/block/pallas_call | solution.py:252
  38.7 7.3 %collective-permute-start.3 = (bf16[16,16,16,128]{3,2,1,0:T(8,128)(2,1)S(1)}, bf16[16,16,16,128]{3,2,1,0:T(8,128)(2,1)S(1)}, u32[]{:S(2)}, u32[]{:S(2)}) collective-permute-start(bf16[16,16,16,128]{3,2,1,0:T(8,128)(2,1)S(1)} %get-tuple-element.43), channel_id=1, source_target_pairs={{0,8},{2,10},{4,12},{6,14},{1,9},{3,11},{5,13},{7,15},{16,24},{18,... | collective-permute-start | bytes 3145736 | tf_op jit(solution)/shard_map/ppermute | solution.py:346
  46.0 3.5 %rest.1 = (bf16[16,16,16,128]{3,2,1,0:T(8,128)(2,1)S(1)}, bf16[72,512]{1,0:T(8,128)(2,1)S(1)}, bf16[72,512]{1,0:T(8,128)(2,1)S(1)}, bf16[144,512]{1,0:T(8,128)(2,1)S(1)}) custom-call(s32[4]{0:T(128)S(1)} %add_convert_fusion.3.place, bf16[288,512]{1,0:T(8,128)(2,1)S(1)} %get-tuple-element.37.x_held, bf16[288,512]{1,0:T(8,128)(2,1)S(1)} %get-tuple-element.38.cot_held, ...), custom_call_target="tpu_custom_call" | custom-call | flops 1000000000 | bytes 5000000 | tf_op jit(solution)/shard_map/rest/pallas_call | solution.py:272
  49.5 1.2 add_convert_fusion
  50.7 3.6 %all-to-all-start = ((bf16[8,32,16,128]{3,2,1,0:T(8,128)(2,1)}), bf16[8,32,16,128]{3,2,1,0:T(8,128)(2,1)S(1)}, u32[]{:S(2)}, u32[]{:S(2)}) async-start(bf16[8,32,16,128]{3,2,1,0:T(8,128)(2,1)} %bitcast.7), calls=%async_computation | async-start | bytes 2097152 | tf_op jit(solution)/shard_map/all_to_all | solution.py:350
  54.3 1.9 %collective-permute-start.4 = (bf16[144,512]{1,0:T(8,128)(2,1)S(1)}, bf16[144,512]{1,0:T(8,128)(2,1)S(1)}, u32[]{:S(2)}, u32[]{:S(2)}) collective-permute-start(bf16[144,512]{1,0:T(8,128)(2,1)S(1)} %get-tuple-element.46), channel_id=1, source_target_pairs={{8,0},{505,1},{10,2},{507,3},{12,4},{509,5},{14,6},{511,7},{16,8},... | collective-permute-start | bytes 442376 | tf_op jit(solution)/shard_map/ppermute | solution.py:46
  56.2 11.7 %all-to-all-done = bf16[8,32,16,128]{3,2,1,0:T(8,128)(2,1)S(1)} async-done(((bf16[8,32,16,128]{3,2,1,0:T(8,128)(2,1)}), bf16[8,32,16,128]{3,2,1,0:T(8,128)(2,1)S(1)}, u32[]{:S(2)}, u32[]{:S(2)}) %all-to-all-start) | async-done | bytes 1048608 | tf_op jit(solution)/shard_map/all_to_all | solution.py:350
  68.1 11.8 %all_to_all.25 = bf16[8,4,16,128]{3,2,1,0:T(8,128)(2,1)S(1)} all-to-all(bf16[8,4,16,128]{3,2,1,0:T(8,128)(2,1)S(1)} %bitcast.23), channel_id=1, replica_groups={{0,128,256,384,4,132,260,388},{1,129,257,385,5,133,261,389},{16,144,272..., dimensions={0} | all-to-all | bytes 262144 | tf_op jit(solution)/shard_map/all_to_all | solution.py:350
  79.9 9.3 %all_to_all.26 = bf16[4,4,16,128]{3,2,1,0:T(8,128)(2,1)S(1)} all-to-all(bf16[4,4,16,128]{3,2,1,0:T(8,128)(2,1)S(1)} %broadcast_in_dim.11), channel_id=1, replica_groups={{0,16,32,48},{2,18,34,50},{4,20,36,52},{6,22,38,54},{64,80,96,112},{66,..., dimensions={0} | all-to-all | bytes 131072 | tf_op jit(solution)/shard_map/all_to_all | solution.py:350
  89.9 3.4 %all-to-all-start.3 = ((bf16[8,4,16,128]{3,2,1,0:T(8,128)(2,1)}), bf16[8,4,16,128]{3,2,1,0:T(8,128)(2,1)S(1)}, u32[]{:S(2)}, u32[]{:S(2)}) async-start(bf16[8,4,16,128]{3,2,1,0:T(8,128)(2,1)} %broadcast_in_dim.25), calls=%async_computation.3 | async-start | bytes 262144 | tf_op jit(solution)/shard_map/all_to_all | solution.py:350
  93.3 9.2 %all-to-all-done.3 = bf16[8,4,16,128]{3,2,1,0:T(8,128)(2,1)S(1)} async-done(((bf16[8,4,16,128]{3,2,1,0:T(8,128)(2,1)}), bf16[8,4,16,128]{3,2,1,0:T(8,128)(2,1)S(1)}, u32[]{:S(2)}, u32[]{:S(2)}) %all-to-all-start.3) | async-done | bytes 131104 | tf_op jit(solution)/shard_map/all_to_all | solution.py:350
  102.5 1.1 broadcast_in_dim.26
  103.6 3.6 %all-to-all-start.4 = ((bf16[8,32,16,128]{3,2,1,0:T(8,128)(2,1)}), bf16[8,32,16,128]{3,2,1,0:T(8,128)(2,1)S(1)}, u32[]{:S(2)}, u32[]{:S(2)}) async-start(bf16[8,32,16,128]{3,2,1,0:T(8,128)(2,1)} %broadcast_in_dim.26), calls=%async_computation.4 | async-start | bytes 2097152 | tf_op jit(solution)/shard_map/all_to_all | solution.py:350
  107.2 5.4 %collective-permute-start.5 = (bf16[144,512]{1,0:T(8,128)(2,1)S(1)}, bf16[144,512]{1,0:T(8,128)(2,1)S(1)}, u32[]{:S(2)}, u32[]{:S(2)}) collective-permute-start(bf16[144,512]{1,0:T(8,128)(2,1)S(1)} %pad_maximum_fusion), channel_id=1, source_target_pairs={{1,0},{2,1},{3,2},{4,3},{5,4},{6,5},{7,6},{0,7},{9,8},{10,9},{11,1... | collective-permute-start | bytes 442376 | tf_op jit(solution)/shard_map/ppermute | solution.py:46
  112.6 3.1 %collective-permute-done.5.refs_2_ = bf16[144,512]{1,0:T(8,128)(2,1)S(1)} collective-permute-done((bf16[144,512]{1,0:T(8,128)(2,1)S(1)}, bf16[144,512]{1,0:T(8,128)(2,1)S(1)}, u32[]{:S(2)}, u32[]{:S(2)}) %collective-permute-start.5) | collective-permute-done | bytes 147488 | tf_op jit(solution)/shard_map/ppermute | solution.py:46
  115.7 5.1 %all-to-all-done.4 = bf16[8,32,16,128]{3,2,1,0:T(8,128)(2,1)S(1)} async-done(((bf16[8,32,16,128]{3,2,1,0:T(8,128)(2,1)}), bf16[8,32,16,128]{3,2,1,0:T(8,128)(2,1)S(1)}, u32[]{:S(2)}, u32[]{:S(2)}) %all-to-all-start.4) | async-done | bytes 1048608 | tf_op jit(solution)/shard_map/all_to_all | solution.py:350
  120.8 5.2 %collective-permute-start.6 = (bf16[16,16,16,128]{3,2,1,0:T(8,128)(2,1)S(1)}, bf16[16,16,16,128]{3,2,1,0:T(8,128)(2,1)S(1)}, u32[]{:S(2)}, u32[]{:S(2)}) collective-permute-start(bf16[16,16,16,128]{3,2,1,0:T(8,128)(2,1)S(1)} %bitcast.18), channel_id=1, source_target_pairs={{0,8},{2,10},{4,12},{6,14},{1,9},{3,11},{5,13},{7,15},{16,24},{18,... | collective-permute-start | bytes 3145736 | tf_op jit(solution)/shard_map/ppermute | solution.py:346
  126.1 1.6 %untile_own.1 = (bf16[512,1536]{1,0:T(8,128)(2,1)}, bf16[512,512]{1,0:T(8,128)(2,1)}) custom-call(s32[4]{0:T(128)S(1)} %add_convert_fusion.3.place, bf16[16,16,16,128]{3,2,1,0:T(8,128)(2,1)S(1)} %bitcast.19), custom_call_target="tpu_custom_call" | custom-call | bytes 2097152 | tf_op jit(solution)/shard_map/untile_own/pallas_call | solution.py:385
  129.4 1.6 %untile_other.1 = (bf16[512,1536]{1,0:T(8,128)(2,1)}, bf16[512,512]{1,0:T(8,128)(2,1)}) custom-call(s32[4]{0:T(128)S(1)} %add_convert_fusion.3.place, bf16[16,16,16,128]{3,2,1,0:T(8,128)(2,1)S(1)} %collective-permute-done.6.tiles, bf16[512,1536]{1,0:T(8,128)(2,1)} %get-tuple-element.59.refs_0_, ...), custom_call_target="tpu_custom_call", output_to_operand_aliasing={{0}: (2, {}), {1}: (3, {})} | custom-call | bytes 2097152 | tf_op jit(solution)/shard_map/untile_other/pallas_call | solution.py:385
  (28 shorter events, 6.6 us)
Async XLA Ops:
  0.7 1.0 copy-start
  1.7 1.0 copy-start.2
  3.6 19.7 %collective-permute-start = (bf16[144,512]{1,0:T(8,128)(2,1)S(1)}, bf16[144,512]{1,0:T(8,128)(2,1)S(1)}, u32[]{:S(2)}, u32[]{:S(2)}) collective-permute-start(bf16[144,512]{1,0:T(8,128)(2,1)S(1)} %get-tuple-element.34), channel_id=1, source_target_pairs={{0,8},{1,505},{2,10},{3,507},{4,12},{5,509},{6,14},{7,511},{8,16},... | collective-permute-start | bytes 442376 | tf_op jit(solution)/shard_map/ppermute | solution.py:46
  9.2 14.1 %collective-permute-start.1 = (bf16[144,512]{1,0:T(8,128)(2,1)S(1)}, bf16[144,512]{1,0:T(8,128)(2,1)S(1)}, u32[]{:S(2)}, u32[]{:S(2)}) collective-permute-start(bf16[144,512]{1,0:T(8,128)(2,1)S(1)} %get-tuple-element.35), channel_id=1, source_target_pairs={{0,1},{1,2},{2,3},{3,4},{4,5},{5,6},{6,7},{7,0},{8,9},{9,10},{10,1... | collective-permute-start | bytes 442376 | tf_op jit(solution)/shard_map/ppermute | solution.py:46
  11.1 17.2 %collective-permute-start.2 = (bf16[144,512]{1,0:T(8,128)(2,1)S(1)}, bf16[144,512]{1,0:T(8,128)(2,1)S(1)}, u32[]{:S(2)}, u32[]{:S(2)}) collective-permute-start(bf16[144,512]{1,0:T(8,128)(2,1)S(1)} %get-tuple-element.36), channel_id=1, source_target_pairs={{0,505},{1,10},{2,507},{3,12},{4,509},{5,14},{6,511},{7,8},{8,1},{... | collective-permute-start | bytes 442376 | tf_op jit(solution)/shard_map/ppermute | solution.py:46
  28.3 1.4 %copy-start.3 = (bf16[512,1536]{1,0:T(8,128)(2,1)S(1)}, bf16[512,1536]{1,0:T(8,128)(2,1)}, u32[]{:S(2)}) copy-start(bf16[512,1536]{1,0:T(8,128)(2,1)} %qkv_weight.1) | copy-start | bytes 4718596
  29.7 1.0 copy-start.5
  30.7 15.2 %copy-start.4 = (bf16[512,1536]{1,0:T(8,128)(2,1)S(1)}, bf16[512,1536]{1,0:T(8,128)(2,1)}, u32[]{:S(2)}) copy-start(bf16[512,1536]{1,0:T(8,128)(2,1)} %qkv_weight.1) | copy-start | bytes 4718596
  38.7 10.8 %collective-permute-start.3 = (bf16[16,16,16,128]{3,2,1,0:T(8,128)(2,1)S(1)}, bf16[16,16,16,128]{3,2,1,0:T(8,128)(2,1)S(1)}, u32[]{:S(2)}, u32[]{:S(2)}) collective-permute-start(bf16[16,16,16,128]{3,2,1,0:T(8,128)(2,1)S(1)} %get-tuple-element.43), channel_id=1, source_target_pairs={{0,8},{2,10},{4,12},{6,14},{1,9},{3,11},{5,13},{7,15},{16,24},{18,... | collective-permute-start | bytes 3145736 | tf_op jit(solution)/shard_map/ppermute | solution.py:346
  50.7 17.2 %all-to-all-start = ((bf16[8,32,16,128]{3,2,1,0:T(8,128)(2,1)}), bf16[8,32,16,128]{3,2,1,0:T(8,128)(2,1)S(1)}, u32[]{:S(2)}, u32[]{:S(2)}) async-start(bf16[8,32,16,128]{3,2,1,0:T(8,128)(2,1)} %bitcast.7), calls=%async_computation | async-start | bytes 2097152 | tf_op jit(solution)/shard_map/all_to_all | solution.py:350
  54.3 13.8 %collective-permute-start.4 = (bf16[144,512]{1,0:T(8,128)(2,1)S(1)}, bf16[144,512]{1,0:T(8,128)(2,1)S(1)}, u32[]{:S(2)}, u32[]{:S(2)}) collective-permute-start(bf16[144,512]{1,0:T(8,128)(2,1)S(1)} %get-tuple-element.46), channel_id=1, source_target_pairs={{8,0},{505,1},{10,2},{507,3},{12,4},{509,5},{14,6},{511,7},{16,8},... | collective-permute-start | bytes 442376 | tf_op jit(solution)/shard_map/ppermute | solution.py:46
  89.9 12.6 %all-to-all-start.3 = ((bf16[8,4,16,128]{3,2,1,0:T(8,128)(2,1)}), bf16[8,4,16,128]{3,2,1,0:T(8,128)(2,1)S(1)}, u32[]{:S(2)}, u32[]{:S(2)}) async-start(bf16[8,4,16,128]{3,2,1,0:T(8,128)(2,1)} %broadcast_in_dim.25), calls=%async_computation.3 | async-start | bytes 262144 | tf_op jit(solution)/shard_map/all_to_all | solution.py:350
  102.5 23.5 %copy-start.1 = (bf16[4,6,12,512]{3,0,2,1:T(4,128)(2,1)S(1)}, bf16[4,6,12,512]{3,0,2,1:T(4,128)(2,1)}, u32[]{:S(2)}) copy-start(bf16[4,6,12,512]{3,0,2,1:T(4,128)(2,1)} %param.5) | copy-start | bytes 884740
  103.6 17.2 %all-to-all-start.4 = ((bf16[8,32,16,128]{3,2,1,0:T(8,128)(2,1)}), bf16[8,32,16,128]{3,2,1,0:T(8,128)(2,1)S(1)}, u32[]{:S(2)}, u32[]{:S(2)}) async-start(bf16[8,32,16,128]{3,2,1,0:T(8,128)(2,1)} %broadcast_in_dim.26), calls=%async_computation.4 | async-start | bytes 2097152 | tf_op jit(solution)/shard_map/all_to_all | solution.py:350
  107.2 8.5 %collective-permute-start.5 = (bf16[144,512]{1,0:T(8,128)(2,1)S(1)}, bf16[144,512]{1,0:T(8,128)(2,1)S(1)}, u32[]{:S(2)}, u32[]{:S(2)}) collective-permute-start(bf16[144,512]{1,0:T(8,128)(2,1)S(1)} %pad_maximum_fusion), channel_id=1, source_target_pairs={{1,0},{2,1},{3,2},{4,3},{5,4},{6,5},{7,6},{0,7},{9,8},{10,9},{11,1... | collective-permute-start | bytes 442376 | tf_op jit(solution)/shard_map/ppermute | solution.py:46
  120.8 7.7 %collective-permute-start.6 = (bf16[16,16,16,128]{3,2,1,0:T(8,128)(2,1)S(1)}, bf16[16,16,16,128]{3,2,1,0:T(8,128)(2,1)S(1)}, u32[]{:S(2)}, u32[]{:S(2)}) collective-permute-start(bf16[16,16,16,128]{3,2,1,0:T(8,128)(2,1)S(1)} %bitcast.18), channel_id=1, source_target_pairs={{0,8},{2,10},{4,12},{6,14},{1,9},{3,11},{5,13},{7,15},{16,24},{18,... | collective-permute-start | bytes 3145736 | tf_op jit(solution)/shard_map/ppermute | solution.py:346

commit v4 on v3

--- a/solution.py
+++ b/solution.py
@@ -1,3 +1,4 @@
+import functools
 import itertools
 
 import jax
@@ -52,25 +53,32 @@
     return level * window + 2 * lat_edge * (quarter // 2) + 4 * lon_edge * (quarter % 2)
 
 
+def fetched(sources, targets, semaphores):
+    copies = [
+        pltpu.make_async_copy(source, target, semaphores.at[at])
+        for at, (source, target) in enumerate(zip(sources, targets))
+    ]
+    for copy in copies:
+        copy.start()
+    return copies
+
+
 def pack_kernel(place, act_ref, cot_ref, own, lon, lat, both, lines):
-    whole = {}
-    for row_half in range(2):
-        for col_half in range(2):
-            cuts = []
-            for kind, ref in enumerate((act_ref, cot_ref)):
-                held = [lines.at[4 * (4 * kind + 2 * row_half + col_half) + part] for part in range(4)]
-                for row in range(HALF_LAT):
-                    for col in range(HALF_LON):
-                        token = ref[row_half * HALF_LAT + row, col_half * HALF_LON + col]
-                        token = token.astype(jnp.float32)
-                        for part in range(4):
-                            at = pl.ds(LEVELS * (row * HALF_LON + col), LEVELS)
-                            held[part][at] = token[:, 128 * part : 128 * part + 128]
-                for pair in PAIRS:
-                    for level in pair:
-                        at = pl.ds(level, HALF_LAT * HALF_LON, stride=LEVELS)
-                        cuts.append(jnp.concatenate([part[at] for part in held], axis=1))
-            whole[row_half, col_half] = jnp.concatenate(cuts, axis=0).astype(jnp.bfloat16)
+    cuts = {(row_half, col_half): [] for row_half in range(2) for col_half in range(2)}
+    for kind, ref in enumerate((act_ref, cot_ref)):
+        for row_half, col_half in cuts:
+            held = [lines.at[4 * (4 * kind + 2 * row_half + col_half) + part] for part in range(4)]
+            for row in range(HALF_LAT):
+                for col in range(HALF_LON):
+                    token = ref[row_half * HALF_LAT + row, col_half * HALF_LON + col].astype(jnp.float32)
+                    at = pl.ds(LEVELS * (row * HALF_LON + col), LEVELS)
+                    for part in range(4):
+                        held[part][at] = token[:, 128 * part : 128 * part + 128]
+            for pair in PAIRS:
+                for level in pair:
+                    at = pl.ds(level, HALF_LAT * HALF_LON, stride=LEVELS)
+                    cuts[row_half, col_half].append(jnp.concatenate([part[at] for part in held], axis=1))
+    whole = {at: jnp.concatenate(pieces, axis=0).astype(jnp.bfloat16) for at, pieces in cuts.items()}
 
     def put(parity):
         own[...] = whole[0, parity]
@@ -82,14 +90,21 @@
         pl.when(place[0] == parity)(lambda parity=parity: put(parity))
 
 
+SMEM = pl.BlockSpec(memory_space=pltpu.SMEM)
+VMEM = pl.BlockSpec(memory_space=pltpu.VMEM)
+HBM = pl.BlockSpec(memory_space=pltpu.HBM)
+LOCAL = (ROWS, COLS, LEVELS, D)
+
+
 def pack(place, activations, cotangent):
-    whole = pl.BlockSpec(memory_space=pltpu.VMEM)
     return pl.pallas_call(
         pack_kernel,
         out_shape=(jax.ShapeDtypeStruct((4 * QUARTER, D), jnp.bfloat16),) * 4,
-        in_specs=[pl.BlockSpec(memory_space=pltpu.SMEM)] + [whole] * 2,
-        out_specs=(whole,) * 4,
-        scratch_shapes=[pltpu.VMEM((32, LEVELS * HALF_LAT * HALF_LON, 128), jnp.float32)],
+        in_specs=[SMEM, VMEM, VMEM],
+        out_specs=(VMEM,) * 4,
+        scratch_shapes=[
+            pltpu.VMEM((32, LEVELS * HALF_LAT * HALF_LON, 128), jnp.float32),
+        ],
         compiler_params=pltpu.CompilerParams(vmem_limit_bytes=32 * 2**20),
         cost_estimate=pl.CostEstimate(flops=0, bytes_accessed=1200000, transcendentals=0),
         name="pack",
@@ -131,34 +146,27 @@
     )(place, cotangent, *quarters)
 
 
-def half_grads(half, normed, attended, qkv_grad, cot_held, tiles):
-    rows = pl.ds(pl.multiple_of(half * (D // 2), D // 2), D // 2)
-
-    def put(step, block):
-        block = block.astype(jnp.bfloat16)
-        for part in range(2):
-            tiles[:, 2 * step + part] = block[:, 128 * part : 128 * part + 128].reshape(D // 32, 16, 128)
-
-    @pl.loop(0, 3 * D // 256)
-    def _(step):
-        cols = pl.ds(pl.multiple_of(step * 256, 256), 256)
-        put(step, dot(normed[:, rows], qkv_grad[:, cols], 0, 0))
-
-    @pl.loop(0, D // 256)
-    def _(step):
-        cols = pl.ds(pl.multiple_of(step * 256, 256), 256)
-        put(step + 3 * D // 256, dot(attended[:, rows], cot_held[:, cols], 0, 0))
+def weights_kernel(qkv_weight, proj_weight, qkv_held, proj_held, semaphores):
+    for copy in fetched((qkv_weight, proj_weight), (qkv_held, proj_held), semaphores):
+        copy.wait()
+
+
+def near_weights(qkv_weight, proj_weight):
+    return pl.pallas_call(
+        weights_kernel,
+        out_shape=(rows_of(D, 3 * D), rows_of(D)),
+        in_specs=[HBM, HBM],
+        out_specs=(VMEM, VMEM),
+        scratch_shapes=[pltpu.SemaphoreType.DMA((2,))],
+        compiler_params=pltpu.CompilerParams(vmem_limit_bytes=32 * 2**20),
+        cost_estimate=pl.CostEstimate(flops=0, bytes_accessed=4 * 2**20, transcendentals=0),
+        name="near_weights",
+    )(qkv_weight, proj_weight)
 
 
 def block_kernel(place, *refs):
-    quarters, weights = refs[:4], refs[4:6]
-    x_held, cot_held, normed, attended, qkv_grad, tiles, qkv, upstream, qkv_weight, proj_weight, arrivals = refs[6:]
-    copies = [
-        pltpu.make_async_copy(source, target, arrivals.at[at])
-        for at, (source, target) in enumerate(zip(weights, (qkv_weight, proj_weight)))
-    ]
-    for copy in copies:
-        copy.start()
+    quarters, (qkv_weight, proj_weight), (theirs, mine, own, lat, lon_both) = refs[:4], refs[4:6], refs[6:11]
+    x_held, cot_held, normed, attended, qkv_grad, qkv, upstream, tiles = refs[11:]
     held = [ref[...].astype(jnp.float32) for ref in quarters]
     for kind, target in enumerate((x_held, cot_held)):
         chunks = [
@@ -172,18 +180,12 @@
     inverse = lax.rsqrt(jnp.mean(centered * centered, axis=-1, keepdims=True) + 1e-05)
     normed[...] = (centered * inverse).astype(jnp.bfloat16)
 
-    for copy in copies:
-        copy.wait()
-
-    @pl.loop(0, 3 * D // 256)
-    def _(step):
-        cols = pl.ds(pl.multiple_of(step * 256, 256), 256)
-        gain = jnp.where(step < D // 256, HEAD_DIM ** (-0.5), 1.0)
+    for step in range(3 * D // 256):
+        cols = slice(step * 256, (step + 1) * 256)
+        gain = HEAD_DIM ** (-0.5) if step < D // 256 else 1.0
         qkv[:, cols] = (dot(normed[...], qkv_weight[:, cols], 1, 0) * gain).astype(jnp.bfloat16)
-
-    @pl.loop(0, D // 256)
-    def _(step):
-        cols = pl.ds(pl.multiple_of(step * 256, 256), 256)
+    for step in range(D // 256):
+        cols = slice(step * 256, (step + 1) * 256)
         upstream[:, cols] = dot(cot_held[...], proj_weight[cols, :], 1, 1).astype(jnp.bfloat16)
 
     head_of = lax.broadcasted_iota(jnp.int32, (WINDOW, GROUP * HEAD_DIM), 1) // HEAD_DIM
@@ -220,11 +222,21 @@
             qkv_grad[rows, cols[1]] = dot(score_grad, query, 1, 0).astype(jnp.bfloat16)
             qkv_grad[rows, cols[2]] = dot(low, grad, 1, 0).astype(jnp.bfloat16)
 
-    half_grads(1 - place[3], normed, attended, qkv_grad, cot_held, tiles)
-
-
-def rest_kernel(place, x_held, cot_held, normed, attended, qkv_grad, qkv_weight, tiles, own, lat, lon_both):
-    half_grads(place[3], normed, attended, qkv_grad, cot_held, tiles)
+    def put(step, grads):
+        grads = grads.astype(jnp.bfloat16)
+        for half in range(2):
+            rows = grads[half * (D // 2) : (half + 1) * (D // 2)]
+            for part in range(2):
+                tiles[half, :, 2 * step + part] = rows[:, 128 * part : 128 * part + 128].reshape(D // 32, 16, 128)
+
+    tall = normed[...].T
+    for step in range(3 * D // 256):
+        put(step, dot(tall, qkv_grad[:, step * 256 : (step + 1) * 256], 1, 0))
+    tall = attended[...].T
+    for step in range(D // 256):
+        put(step + 3 * D // 256, dot(tall, cot_held[:, step * 256 : (step + 1) * 256], 1, 0))
+    theirs[...] = tiles[1 - place[3]]
+    mine[...] = tiles[place[3]]
     normed_grad = dot(qkv_grad[...], qkv_weight[...], 1, 1)
     x = x_held[...].astype(jnp.float32)
     centered = x - jnp.mean(x, axis=-1, keepdims=True)
@@ -248,18 +260,20 @@
 
 
 def block(place, quarters, qkv_weight, proj_weight):
-    whole = pl.BlockSpec(memory_space=pltpu.VMEM)
     return pl.pallas_call(
         block_kernel,
-        out_shape=(rows_of(TOKENS),) * 4 + (rows_of(TOKENS, 3 * D), HALF_TILES),
-        in_specs=[pl.BlockSpec(memory_space=pltpu.SMEM)] + [whole] * 4 + [pl.BlockSpec(memory_space=pl.ANY)] * 2,
-        out_specs=(whole,) * 6,
+        out_shape=(HALF_TILES, HALF_TILES, rows_of(2 * QUARTER), rows_of(2 * QUARTER), rows_of(4 * QUARTER)),
+        in_specs=[SMEM] + [VMEM] * 6,
+        out_specs=(VMEM,) * 5,
         scratch_shapes=[
+            pltpu.VMEM((TOKENS, D), jnp.bfloat16),
+            pltpu.VMEM((TOKENS, D), jnp.bfloat16),
+            pltpu.VMEM((TOKENS, D), jnp.bfloat16),
+            pltpu.VMEM((TOKENS, D), jnp.bfloat16),
+            pltpu.VMEM((TOKENS, 3 * D), jnp.bfloat16),
             pltpu.VMEM((TOKENS, 3 * D), jnp.bfloat16),
             pltpu.VMEM((TOKENS, D), jnp.bfloat16),
-            pltpu.VMEM((D, 3 * D), jnp.bfloat16),
-            pltpu.VMEM((D, D), jnp.bfloat16),
-            pltpu.SemaphoreType.DMA((2,)),
+            pltpu.VMEM((2,) + HALF_TILES.shape, jnp.bfloat16),
         ],
         compiler_params=pltpu.CompilerParams(vmem_limit_bytes=48 * 2**20),
         cost_estimate=pl.CostEstimate(flops=2 * 10**9, bytes_accessed=6 * 10**6, transcendentals=6 * 10**5),
@@ -267,19 +281,6 @@
     )(place, *quarters, qkv_weight, proj_weight)
 
 
-def rest(place, kept, qkv_weight):
-    whole = pl.BlockSpec(memory_space=pltpu.VMEM)
-    return pl.pallas_call(
-        rest_kernel,
-        out_shape=(HALF_TILES, rows_of(2 * QUARTER), rows_of(2 * QUARTER), rows_of(4 * QUARTER)),
-        in_specs=[pl.BlockSpec(memory_space=pltpu.SMEM)] + [whole] * 6,
-        out_specs=(whole,) * 4,
-        compiler_params=pltpu.CompilerParams(vmem_limit_bytes=48 * 2**20),
-        cost_estimate=pl.CostEstimate(flops=10**9, bytes_accessed=5 * 10**6, transcendentals=300),
-        name="rest",
-    )(place, *kept, qkv_weight)
-
-
 def added(arrived):
     total = arrived[0].astype(jnp.float32)
     for part in range(1, arrived.shape[0]):
@@ -301,41 +302,13 @@
     return lax.axis_size("z"), lax.axis_size("y_hi") * lax.axis_size("y_lo"), lax.axis_size("x")
 
 
-def near_groups():
-    def along(size, core):
-        if size == 1:
-            return [[0]]
-        return [[(2 * at + 2 * core) % size, 2 * at + 1] for at in range(size // 2)]
+def cube_groups(stride):
+    def along(size):
+        firsts = [at for at in range(size) if at // stride % 2 == 0]
+        return [[at, at + stride] if at + stride < size else [at] for at in firsts]
 
     def members(core):
-        zs, ys, xs = (along(size, core) for size in chips())
-        return [[(z, y, x) for z in za for y in ya for x in xa] for za in zs for ya in ys for xa in xs]
-
-    return device_groups(members)
-
-
-def strided(size):
-    step = min(size, 2)
-    return [list(range(parity, size, step)) for parity in range(step)]
-
-
-def middle_groups():
-    def members(core):
-        z_size, y_size, x_size = chips()
-        xs = strided(x_size)
-        if core == 0:
-            return [[(z, y, x) for x in xa for z in za] for xa in xs for za in strided(z_size) for y in range(y_size)]
-        return [[(z, y, x) for x in xa for y in ya] for xa in xs for ya in strided(y_size) for z in range(z_size)]
-
-    return device_groups(members)
-
-
-def far_groups():
-    def members(core):
-        z_size, y_size, x_size = chips()
-        if core == 0:
-            return [[(z, y, x) for y in ya] for ya in strided(y_size) for z in range(z_size) for x in range(x_size)]
-        return [[(z, y, x) for z in za] for za in strided(z_size) for y in range(y_size) for x in range(x_size)]
+        return [list(itertools.product(*lines)) for lines in itertools.product(*(along(size) for size in chips()))]
 
     return device_groups(members)
 
@@ -364,34 +337,41 @@
     return exchanged(tiles, groups).reshape((-1,) + tiles.shape[1:])
 
 
-def untile_kernel(place, tiles, *refs):
-    qkv_out, proj_out = refs[-2:]
-    for col in range(4 * D // 128):
-        strip = tiles[:, col].reshape(-1, 128)
-        if col < 3 * D // 128:
-            qkv_out[:, 128 * col : 128 * col + 128] = strip
-        else:
-            proj_out[:, 128 * col - 3 * D : 128 * col - 3 * D + 128] = strip
+def untile_kernel(other, place, tiles, *refs):
+    qkv_out, proj_out, qkv_held, proj_held, semaphores = refs[-5:]
+    first = (1 - place[3] if other else place[3]) * (D // 2)
+    chunk = D // 2 // CHUNKS
+    copies = []
+    for at in range(CHUNKS):
+        rows = slice(at * chunk, (at + 1) * chunk)
+        for col in range(4 * D // 128):
+            strip = tiles[at * chunk // 16 : (at + 1) * chunk // 16, col].reshape(chunk, 128)
+            if col < 3 * D // 128:
+                qkv_held[rows, 128 * col : 128 * col + 128] = strip
+            else:
+                proj_held[rows, 128 * col - 3 * D : 128 * col - 3 * D + 128] = strip
+        target = pl.ds(pl.multiple_of(first + at * chunk, chunk), chunk)
+        for kind, (held, out) in enumerate(((qkv_held, qkv_out), (proj_held, proj_out))):
+            copies.append(pltpu.make_async_copy(held.at[rows], out.at[target], semaphores.at[2 * at + kind]))
+            copies[-1].start()
+    for copy in copies:
+        copy.wait()
+
+
+CHUNKS = 4
 
 
 def untile(place, tiles, other, so_far=()):
-    steps = 2
-    half = D // 2
-
-    def at(step, place):
-        core = 1 - place[3] if other else place[3]
-        return (core * steps + step, 0)
-
     return pl.pallas_call(
-        untile_kernel,
-        grid_spec=pltpu.PrefetchScalarGridSpec(
-            num_scalar_prefetch=1,
-            grid=(steps,),
-            in_specs=[pl.BlockSpec((half // 16 // steps, 4 * D // 128, 16, 128), lambda step, place: (step, 0, 0, 0))]
-            + [pl.BlockSpec(memory_space=pl.ANY)] * len(so_far),
-            out_specs=(pl.BlockSpec((half // steps, 3 * D), at), pl.BlockSpec((half // steps, D), at)),
-        ),
+        functools.partial(untile_kernel, other),
+        in_specs=[SMEM, VMEM] + [HBM] * len(so_far),
+        out_specs=(HBM, HBM),
         out_shape=(rows_of(D, 3 * D), rows_of(D)),
+        scratch_shapes=[
+            pltpu.VMEM((D // 2, 3 * D), jnp.bfloat16),
+            pltpu.VMEM((D // 2, D), jnp.bfloat16),
+            pltpu.SemaphoreType.DMA((2 * CHUNKS,)),
+        ],
         input_output_aliases={2: 0, 3: 1} if so_far else {},
         compiler_params=pltpu.CompilerParams(vmem_limit_bytes=32 * 2**20),
         cost_estimate=pl.CostEstimate(flops=0, bytes_accessed=2 * 2**20, transcendentals=0),
@@ -404,14 +384,14 @@
     odd = lat % 2 == 1
     lon_edge = jnp.where(odd, lon == lax.axis_size(LON) - 1, lon == 0)
     place = jnp.stack([odd, lat == 0, lon_edge, lax.axis_index("core") == 1]).astype(jnp.int32)
-    quarters = pack(place, activations, cotangent)
-    quarters = [quarters[0]] + [moved(quarters[kind], kind, False) for kind in range(1, 4)]
-    *kept, theirs = block(place, quarters, qkv_weight, proj_weight)
-    arrived = swapped(theirs)
-    mine, own, lat, lon_both = rest(place, kept, qkv_weight)
-
-    near, middle, far = near_groups(), middle_groups(), far_groups()
-    tiles = (mine.astype(jnp.float32) + arrived.astype(jnp.float32)).astype(jnp.bfloat16)
+    own, lon, lat, both = pack(place, activations, cotangent)
+    own, qkv_weight, proj_weight = lax.optimization_barrier((own, qkv_weight, proj_weight))
+    lat, lon, both = moved(lat, 2, False), moved(lon, 1, False), moved(both, 3, False)
+    qkv_weight, proj_weight = near_weights(qkv_weight, proj_weight)
+    theirs, mine, own, lat, lon_both = block(place, (own, lon, lat, both), qkv_weight, proj_weight)
+
+    near, middle, far = cube_groups(1), cube_groups(2), cube_groups(4)
+    tiles = (mine.astype(jnp.float32) + swapped(theirs).astype(jnp.float32)).astype(jnp.bfloat16)
     tiles, lon_both = lax.optimization_barrier((tiles.reshape(-1, 16, 128), lon_both))
     tiles, lon_both = lax.optimization_barrier((scattered_sum(tiles, near), moved(lon_both, 1, True)))
     tiles = scattered_sum(tiles, middle)

time: 132 us -> 137 us (1.038)
  blocking collectives: 21.1 us -> 27.6 us
  Pallas kernels: 16.3 us -> 11.1 us
  waiting for transfers between devices: 34.1 us -> 37.9 us
    all_to_all x2, blocking collectives: 21.1 us -> 27.6 us  [all_to_all(): return lax.all_to_all(split, ALL, 0, 0, axis_index_groups=groups)]
    pallas_call x4, Pallas kernels: 14.7 us -> 9.51 us  [the longest x1 6.13 us: block(): pl.pallas_call(block_kernel, out_shape=(HALF_TILES, HALF_TILES, rows_of(2...]
    ppermute x5, waiting for transfers between devices: 8.1 us -> 12 us  [moved(): return lax.ppermute(value, ALL, pairs)]
    all_to_all x3, waiting for transfers between devices: 26 us -> 23.6 us  [all_to_all(): return lax.all_to_all(split, ALL, 0, 0, axis_index_groups=groups)]
    ppermute x2, waiting for transfers between devices: 0.01 us -> 2.27 us  [swapped(): return lax.ppermute(value, ALL, [*zip(first, second), *zip(second, first)])]
    ppermute x2, starting transfers between devices: 12.5 us -> 14.5 us  [swapped(): return lax.ppermute(value, ALL, [*zip(first, second), *zip(second, first)])]
    ppermute x5, starting transfers between devices: 27 us -> 25.1 us  [moved(): return lax.ppermute(value, ALL, pairs)]
    unnamed x14 -> x12, local copies, waits for them, and re-layouts: 5.39 us -> 5.38 us
  transfers between devices with their start and end apart: 10 -> 10, of which waited for: 5 -> 5; matrix products, arithmetic and copies ran while one was open for 0% -> 0% of each run, Pallas kernels for 4% -> 2%
where the time goes in v4:
time: 137 us; the launch traced here: 136 us
  starting transfers between devices  50 us (36%)
  waiting for transfers between devices  37.9 us (28%)
  blocking collectives  27.6 us (20%)
  Pallas kernels  11.1 us (8%)
  local copies, waits for them, and re-layouts  7.18 us (5%)
  other arithmetic  1.52 us (1%)
    all_to_all x2, blocking collectives, all_to_all(): return lax.all_to_all(split, ALL, 0, 0, axis_index_groups=groups)  27.6 us
    ppermute x5, starting transfers between devices, moved(): return lax.ppermute(value, ALL, pairs)  25.1 us
    all_to_all x3, waiting for transfers between devices, all_to_all(): return lax.all_to_all(split, ALL, 0, 0, axis_index_groups=groups)  23.6 us
    ppermute x2, starting transfers between devices, swapped(): return lax.ppermute(value, ALL, [*zip(first, second), *zip(second, first)])  14.5 us
    ppermute x5, waiting for transfers between devices, moved(): return lax.ppermute(value, ALL, pairs)  12 us
    all_to_all x3, starting transfers between devices, all_to_all(): return lax.all_to_all(split, ALL, 0, 0, axis_index_groups=groups)  10.5 us
    pallas_call x1, Pallas kernels, block(): pl.pallas_call(block_kernel, out_shape=(HALF_TILES, HALF_TILES, rows_of(2...  6.13 us
    unnamed x12, local copies, waits for them, and re-layouts  5.38 us
  transfers between devices with their start and end apart: 10, of which 5 were waited for; matrix products, arithmetic and copies ran while one was open for 0% of the time, Pallas kernels for 2%

profile of v4, /device:TPU:1, one launch (start us, length us, event | category | flops | bytes accessed | tf_op | source)
XLA Modules:
  0.0 136.1 jit_solution(2720372071522821960)
XLA Ops:
  3.6 5.6 %collective-permute-start = (bf16[144,512]{1,0:T(8,128)(2,1)S(1)}, bf16[144,512]{1,0:T(8,128)(2,1)S(1)}, u32[]{:S(2)}, u32[]{:S(2)}) collective-permute-start(bf16[144,512]{1,0:T(8,128)(2,1)S(1)} %get-tuple-element.35), channel_id=1, source_target_pairs={{0,8},{1,505},{2,10},{3,507},{4,12},{5,509},{6,14},{7,511},{8,16},... | collective-permute-start | bytes 442376 | tf_op jit(solution)/shard_map/ppermute | solution.py:47
  9.2 1.9 %collective-permute-start.1 = (bf16[144,512]{1,0:T(8,128)(2,1)S(1)}, bf16[144,512]{1,0:T(8,128)(2,1)S(1)}, u32[]{:S(2)}, u32[]{:S(2)}) collective-permute-start(bf16[144,512]{1,0:T(8,128)(2,1)S(1)} %get-tuple-element.36), channel_id=1, source_target_pairs={{0,1},{1,2},{2,3},{3,4},{4,5},{5,6},{6,7},{7,0},{8,9},{9,10},{10,1... | collective-permute-start | bytes 442376 | tf_op jit(solution)/shard_map/ppermute | solution.py:47
  11.1 12.2 %collective-permute-start.2 = (bf16[144,512]{1,0:T(8,128)(2,1)S(1)}, bf16[144,512]{1,0:T(8,128)(2,1)S(1)}, u32[]{:S(2)}, u32[]{:S(2)}) collective-permute-start(bf16[144,512]{1,0:T(8,128)(2,1)S(1)} %get-tuple-element.37), channel_id=1, source_target_pairs={{0,505},{1,10},{2,507},{3,12},{4,509},{5,14},{6,511},{7,8},{8,1},{... | collective-permute-start | bytes 442376 | tf_op jit(solution)/shard_map/ppermute | solution.py:47
  23.3 1.4 %copy-done = bf16[512,1536]{1,0:T(8,128)(2,1)S(1)} copy-done((bf16[512,1536]{1,0:T(8,128)(2,1)S(1)}, bf16[512,1536]{1,0:T(8,128)(2,1)}, u32[]{:S(2)}) %copy-start) | copy-done | bytes 1572888
  24.7 1.0 copy-done.3
  25.9 2.4 %collective-permute-done.2.refs_3_ = bf16[144,512]{1,0:T(8,128)(2,1)S(1)} collective-permute-done((bf16[144,512]{1,0:T(8,128)(2,1)S(1)}, bf16[144,512]{1,0:T(8,128)(2,1)S(1)}, u32[]{:S(2)}, u32[]{:S(2)}) %collective-permute-start.2) | collective-permute-done | bytes 147488 | tf_op jit(solution)/shard_map/ppermute | solution.py:47
  28.3 6.1 %block.1 = (bf16[16,16,16,128]{3,2,1,0:T(8,128)(2,1)S(1)}, bf16[16,16,16,128]{3,2,1,0:T(8,128)(2,1)S(1)}, bf16[72,512]{1,0:T(8,128)(2,1)S(1)}, bf16[72,512]{1,0:T(8,128)(2,1)S(1)}, bf16[144,512]{1,0:T(8,128)(2,1)S(1)}) custom-call(s32[4]{0:T(128)S(1)} %add_convert_fusion.3.place, bf16[144,512]{1,0:T(8,128)(2,1)S(1)} %get-tuple-element.34.refs_0_, ...), custom_call_target="tpu_custom_call" | custom-call | flops 2000000000 | bytes 6000000 | tf_op jit(solution)/shard_map/block/pallas_call | solution.py:263
  34.4 7.2 %collective-permute-start.3 = (bf16[16,16,16,128]{3,2,1,0:T(8,128)(2,1)S(1)}, bf16[16,16,16,128]{3,2,1,0:T(8,128)(2,1)S(1)}, u32[]{:S(2)}, u32[]{:S(2)}) collective-permute-start(bf16[16,16,16,128]{3,2,1,0:T(8,128)(2,1)S(1)} %get-tuple-element.43), channel_id=1, source_target_pairs={{0,8},{2,10},{4,12},{6,14},{1,9},{3,11},{5,13},{7,15},{16,24},{18,... | collective-permute-start | bytes 3145736 | tf_op jit(solution)/shard_map/ppermute | solution.py:319
  41.7 2.3 %collective-permute-done.3 = bf16[16,16,16,128]{3,2,1,0:T(8,128)(2,1)S(1)} collective-permute-done((bf16[16,16,16,128]{3,2,1,0:T(8,128)(2,1)S(1)}, bf16[16,16,16,128]{3,2,1,0:T(8,128)(2,1)S(1)}, u32[]{:S(2)}, u32[]{:S(2)}) %collective-permute-start.3) | collective-permute-done | bytes 1048608 | tf_op jit(solution)/shard_map/ppermute | solution.py:319
  43.9 1.2 add_convert_fusion
  45.2 3.6 %all-to-all-start = ((bf16[8,32,16,128]{3,2,1,0:T(8,128)(2,1)}), bf16[8,32,16,128]{3,2,1,0:T(8,128)(2,1)S(1)}, u32[]{:S(2)}, u32[]{:S(2)}) async-start(bf16[8,32,16,128]{3,2,1,0:T(8,128)(2,1)} %bitcast.7), calls=%async_computation | async-start | bytes 2097152 | tf_op jit(solution)/shard_map/all_to_all | solution.py:323
  48.8 2.3 %collective-permute-start.4 = (bf16[144,512]{1,0:T(8,128)(2,1)S(1)}, bf16[144,512]{1,0:T(8,128)(2,1)S(1)}, u32[]{:S(2)}, u32[]{:S(2)}) collective-permute-start(bf16[144,512]{1,0:T(8,128)(2,1)S(1)} %get-tuple-element.46), channel_id=1, source_target_pairs={{8,0},{505,1},{10,2},{507,3},{12,4},{509,5},{14,6},{511,7},{16,8},... | collective-permute-start | bytes 442376 | tf_op jit(solution)/shard_map/ppermute | solution.py:47
  51.0 14.6 %all-to-all-done = bf16[8,32,16,128]{3,2,1,0:T(8,128)(2,1)S(1)} async-done(((bf16[8,32,16,128]{3,2,1,0:T(8,128)(2,1)}), bf16[8,32,16,128]{3,2,1,0:T(8,128)(2,1)S(1)}, u32[]{:S(2)}, u32[]{:S(2)}) %all-to-all-start) | async-done | bytes 1048608 | tf_op jit(solution)/shard_map/all_to_all | solution.py:323
  65.8 11.5 %all_to_all.25 = bf16[8,4,16,128]{3,2,1,0:T(8,128)(2,1)S(1)} all-to-all(bf16[8,4,16,128]{3,2,1,0:T(8,128)(2,1)S(1)} %bitcast.23), channel_id=1, replica_groups={{0,4,16,20,128,132,144,148},{2,6,18,22,130,134,146,150},{1,5,17,21,129,..., dimensions={0} | all-to-all | bytes 262144 | tf_op jit(solution)/shard_map/all_to_all | solution.py:323
  77.4 16.0 %all_to_all.26 = bf16[4,4,16,128]{3,2,1,0:T(8,128)(2,1)S(1)} all-to-all(bf16[4,4,16,128]{3,2,1,0:T(8,128)(2,1)S(1)} %broadcast_in_dim.11), channel_id=1, replica_groups={{0,32,256,288},{2,34,258,290},{4,36,260,292},{6,38,262,294},{1,33,257,2..., dimensions={0} | all-to-all | bytes 131072 | tf_op jit(solution)/shard_map/all_to_all | solution.py:323
  94.1 3.4 %all-to-all-start.3 = ((bf16[8,4,16,128]{3,2,1,0:T(8,128)(2,1)}), bf16[8,4,16,128]{3,2,1,0:T(8,128)(2,1)S(1)}, u32[]{:S(2)}, u32[]{:S(2)}) async-start(bf16[8,4,16,128]{3,2,1,0:T(8,128)(2,1)} %broadcast_in_dim.25), calls=%async_computation.3 | async-start | bytes 262144 | tf_op jit(solution)/shard_map/all_to_all | solution.py:323
  97.5 9.0 %all-to-all-done.3 = bf16[8,4,16,128]{3,2,1,0:T(8,128)(2,1)S(1)} async-done(((bf16[8,4,16,128]{3,2,1,0:T(8,128)(2,1)}), bf16[8,4,16,128]{3,2,1,0:T(8,128)(2,1)S(1)}, u32[]{:S(2)}, u32[]{:S(2)}) %all-to-all-start.3) | async-done | bytes 131104 | tf_op jit(solution)/shard_map/all_to_all | solution.py:323
  106.5 1.1 broadcast_in_dim.26
  107.6 3.6 %all-to-all-start.4 = ((bf16[8,32,16,128]{3,2,1,0:T(8,128)(2,1)}), bf16[8,32,16,128]{3,2,1,0:T(8,128)(2,1)S(1)}, u32[]{:S(2)}, u32[]{:S(2)}) async-start(bf16[8,32,16,128]{3,2,1,0:T(8,128)(2,1)} %broadcast_in_dim.26), calls=%async_computation.4 | async-start | bytes 2097152 | tf_op jit(solution)/shard_map/all_to_all | solution.py:323
  111.2 3.1 %collective-permute-start.5 = (bf16[144,512]{1,0:T(8,128)(2,1)S(1)}, bf16[144,512]{1,0:T(8,128)(2,1)S(1)}, u32[]{:S(2)}, u32[]{:S(2)}) collective-permute-start(bf16[144,512]{1,0:T(8,128)(2,1)S(1)} %pad_maximum_fusion), channel_id=1, source_target_pairs={{1,0},{2,1},{3,2},{4,3},{5,4},{6,5},{7,6},{0,7},{9,8},{10,9},{11,1... | collective-permute-start | bytes 442376 | tf_op jit(solution)/shard_map/ppermute | solution.py:47
  114.3 9.7 %collective-permute-done.5.refs_2_ = bf16[144,512]{1,0:T(8,128)(2,1)S(1)} collective-permute-done((bf16[144,512]{1,0:T(8,128)(2,1)S(1)}, bf16[144,512]{1,0:T(8,128)(2,1)S(1)}, u32[]{:S(2)}, u32[]{:S(2)}) %collective-permute-start.5) | collective-permute-done | bytes 147488 | tf_op jit(solution)/shard_map/ppermute | solution.py:47
  123.9 7.2 %collective-permute-start.6 = (bf16[16,16,16,128]{3,2,1,0:T(8,128)(2,1)S(1)}, bf16[16,16,16,128]{3,2,1,0:T(8,128)(2,1)S(1)}, u32[]{:S(2)}, u32[]{:S(2)}) collective-permute-start(bf16[16,16,16,128]{3,2,1,0:T(8,128)(2,1)S(1)} %bitcast.18), channel_id=1, source_target_pairs={{0,8},{2,10},{4,12},{6,14},{1,9},{3,11},{5,13},{7,15},{16,24},{18,... | collective-permute-start | bytes 3145736 | tf_op jit(solution)/shard_map/ppermute | solution.py:319
  131.2 1.6 %untile_own.1 = (bf16[512,1536]{1,0:T(8,128)(2,1)}, bf16[512,512]{1,0:T(8,128)(2,1)}) custom-call(s32[4]{0:T(128)S(1)} %add_convert_fusion.3.place, bf16[16,16,16,128]{3,2,1,0:T(8,128)(2,1)S(1)} %bitcast.19), custom_call_target="tpu_custom_call" | custom-call | bytes 2097152 | tf_op jit(solution)/shard_map/untile_own/pallas_call | solution.py:365
  134.5 1.6 %untile_other.1 = (bf16[512,1536]{1,0:T(8,128)(2,1)}, bf16[512,512]{1,0:T(8,128)(2,1)}) custom-call(s32[4]{0:T(128)S(1)} %add_convert_fusion.3.place, bf16[16,16,16,128]{3,2,1,0:T(8,128)(2,1)S(1)} %collective-permute-done.6.tiles, bf16[512,1536]{1,0:T(8,128)(2,1)} %get-tuple-element.59.refs_0_, ...), custom_call_target="tpu_custom_call", output_to_operand_aliasing={{0}: (2, {}), {1}: (3, {})} | custom-call | bytes 2097152 | tf_op jit(solution)/shard_map/untile_other/pallas_call | solution.py:365
  (26 shorter events, 5.7 us)
Async XLA Ops:
  0.7 1.0 copy-start.1
  1.7 1.0 copy-start.4
  3.6 22.3 %collective-permute-start = (bf16[144,512]{1,0:T(8,128)(2,1)S(1)}, bf16[144,512]{1,0:T(8,128)(2,1)S(1)}, u32[]{:S(2)}, u32[]{:S(2)}) collective-permute-start(bf16[144,512]{1,0:T(8,128)(2,1)S(1)} %get-tuple-element.35), channel_id=1, source_target_pairs={{0,8},{1,505},{2,10},{3,507},{4,12},{5,509},{6,14},{7,511},{8,16},... | collective-permute-start | bytes 442376 | tf_op jit(solution)/shard_map/ppermute | solution.py:47
  9.2 16.7 %collective-permute-start.1 = (bf16[144,512]{1,0:T(8,128)(2,1)S(1)}, bf16[144,512]{1,0:T(8,128)(2,1)S(1)}, u32[]{:S(2)}, u32[]{:S(2)}) collective-permute-start(bf16[144,512]{1,0:T(8,128)(2,1)S(1)} %get-tuple-element.36), channel_id=1, source_target_pairs={{0,1},{1,2},{2,3},{3,4},{4,5},{5,6},{6,7},{7,0},{8,9},{9,10},{10,1... | collective-permute-start | bytes 442376 | tf_op jit(solution)/shard_map/ppermute | solution.py:47
  11.1 17.2 %collective-permute-start.2 = (bf16[144,512]{1,0:T(8,128)(2,1)S(1)}, bf16[144,512]{1,0:T(8,128)(2,1)S(1)}, u32[]{:S(2)}, u32[]{:S(2)}) collective-permute-start(bf16[144,512]{1,0:T(8,128)(2,1)S(1)} %get-tuple-element.37), channel_id=1, source_target_pairs={{0,505},{1,10},{2,507},{3,12},{4,509},{5,14},{6,511},{7,8},{8,1},{... | collective-permute-start | bytes 442376 | tf_op jit(solution)/shard_map/ppermute | solution.py:47
  23.3 1.4 %copy-start = (bf16[512,1536]{1,0:T(8,128)(2,1)S(1)}, bf16[512,1536]{1,0:T(8,128)(2,1)}, u32[]{:S(2)}) copy-start(bf16[512,1536]{1,0:T(8,128)(2,1)} %qkv_weight) | copy-start | bytes 4718596
  24.7 1.0 copy-start.3
  34.4 9.5 %collective-permute-start.3 = (bf16[16,16,16,128]{3,2,1,0:T(8,128)(2,1)S(1)}, bf16[16,16,16,128]{3,2,1,0:T(8,128)(2,1)S(1)}, u32[]{:S(2)}, u32[]{:S(2)}) collective-permute-start(bf16[16,16,16,128]{3,2,1,0:T(8,128)(2,1)S(1)} %get-tuple-element.43), channel_id=1, source_target_pairs={{0,8},{2,10},{4,12},{6,14},{1,9},{3,11},{5,13},{7,15},{16,24},{18,... | collective-permute-start | bytes 3145736 | tf_op jit(solution)/shard_map/ppermute | solution.py:319
  45.2 20.5 %all-to-all-start = ((bf16[8,32,16,128]{3,2,1,0:T(8,128)(2,1)}), bf16[8,32,16,128]{3,2,1,0:T(8,128)(2,1)S(1)}, u32[]{:S(2)}, u32[]{:S(2)}) async-start(bf16[8,32,16,128]{3,2,1,0:T(8,128)(2,1)} %bitcast.7), calls=%async_computation | async-start | bytes 2097152 | tf_op jit(solution)/shard_map/all_to_all | solution.py:323
  48.8 17.0 %collective-permute-start.4 = (bf16[144,512]{1,0:T(8,128)(2,1)S(1)}, bf16[144,512]{1,0:T(8,128)(2,1)S(1)}, u32[]{:S(2)}, u32[]{:S(2)}) collective-permute-start(bf16[144,512]{1,0:T(8,128)(2,1)S(1)} %get-tuple-element.46), channel_id=1, source_target_pairs={{8,0},{505,1},{10,2},{507,3},{12,4},{509,5},{14,6},{511,7},{16,8},... | collective-permute-start | bytes 442376 | tf_op jit(solution)/shard_map/ppermute | solution.py:47
  94.1 12.4 %all-to-all-start.3 = ((bf16[8,4,16,128]{3,2,1,0:T(8,128)(2,1)}), bf16[8,4,16,128]{3,2,1,0:T(8,128)(2,1)S(1)}, u32[]{:S(2)}, u32[]{:S(2)}) async-start(bf16[8,4,16,128]{3,2,1,0:T(8,128)(2,1)} %broadcast_in_dim.25), calls=%async_computation.3 | async-start | bytes 262144 | tf_op jit(solution)/shard_map/all_to_all | solution.py:323
  106.5 24.7 %copy-start.2 = (bf16[4,6,12,512]{3,0,2,1:T(4,128)(2,1)S(1)}, bf16[4,6,12,512]{3,0,2,1:T(4,128)(2,1)}, u32[]{:S(2)}) copy-start(bf16[4,6,12,512]{3,0,2,1:T(4,128)(2,1)} %param.5) | copy-start | bytes 884740
  107.6 16.3 %all-to-all-start.4 = ((bf16[8,32,16,128]{3,2,1,0:T(8,128)(2,1)}), bf16[8,32,16,128]{3,2,1,0:T(8,128)(2,1)S(1)}, u32[]{:S(2)}, u32[]{:S(2)}) async-start(bf16[8,32,16,128]{3,2,1,0:T(8,128)(2,1)} %broadcast_in_dim.26), calls=%async_computation.4 | async-start | bytes 2097152 | tf_op jit(solution)/shard_map/all_to_all | solution.py:323
  111.2 12.7 %collective-permute-start.5 = (bf16[144,512]{1,0:T(8,128)(2,1)S(1)}, bf16[144,512]{1,0:T(8,128)(2,1)S(1)}, u32[]{:S(2)}, u32[]{:S(2)}) collective-permute-start(bf16[144,512]{1,0:T(8,128)(2,1)S(1)} %pad_maximum_fusion), channel_id=1, source_target_pairs={{1,0},{2,1},{3,2},{4,3},{5,4},{6,5},{7,6},{0,7},{9,8},{10,9},{11,1... | collective-permute-start | bytes 442376 | tf_op jit(solution)/shard_map/ppermute | solution.py:47
  123.9 9.7 %collective-permute-start.6 = (bf16[16,16,16,128]{3,2,1,0:T(8,128)(2,1)S(1)}, bf16[16,16,16,128]{3,2,1,0:T(8,128)(2,1)S(1)}, u32[]{:S(2)}, u32[]{:S(2)}) collective-permute-start(bf16[16,16,16,128]{3,2,1,0:T(8,128)(2,1)S(1)} %bitcast.18), channel_id=1, source_target_pairs={{0,8},{2,10},{4,12},{6,14},{1,9},{3,11},{5,13},{7,15},{16,24},{18,... | collective-permute-start | bytes 3145736 | tf_op jit(solution)/shard_map/ppermute | solution.py:319

commit v5 on v4

--- a/solution.py
+++ b/solution.py
@@ -111,8 +111,8 @@
     )(place, activations.transpose(1, 2, 0, 3), cotangent.transpose(1, 2, 0, 3))
 
 
-def unpack_kernel(place, cot_ref, *refs):
-    own, lon_ref, lat_both, out = refs
+def unpack_kernel(place, own, lon_ref, lat_both, cot, out, cot_ref, lines, semaphores):
+    (copy,) = fetched((cot,), (cot_ref,), semaphores)
     own, lon = (ref[: 2 * QUARTER].astype(jnp.float32) for ref in (own, lon_ref))
     lat, both = (lat_both[part * 2 * QUARTER : (part + 1) * 2 * QUARTER].astype(jnp.float32) for part in range(2))
     even = place[0] == 0
@@ -122,28 +122,38 @@
         (1, 0): jnp.where(even, both, lat),
         (1, 1): jnp.where(even, lat, both),
     }
-    at = [0, 0]
-    for pair in PAIRS:
-        for level in pair:
-            for row in range(ROWS):
-                half = row // HALF_LAT
-                cuts = [whole[half, col_half][at[half] : at[half] + HALF_LON] for col_half in range(2)]
-                at[half] += HALF_LON
-                line = cot_ref[level, row].astype(jnp.float32) + jnp.concatenate(cuts, axis=0)
-                out[level, row] = line.astype(jnp.bfloat16)
+    copy.wait()
+    count = HALF_LAT * HALF_LON
+    for (row_half, col_half), quarter in whole.items():
+        held = [lines.at[4 * (2 * row_half + col_half) + part] for part in range(4)]
+        for at, level in enumerate(PAIRS[0] + PAIRS[1]):
+            for part in range(4):
+                cut = quarter[at * count : (at + 1) * count, 128 * part : 128 * part + 128]
+                held[part][pl.ds(level, count, stride=LEVELS)] = cut
+        for row in range(HALF_LAT):
+            for col in range(HALF_LON):
+                at = pl.ds(LEVELS * (row * HALF_LON + col), LEVELS)
+                token = jnp.concatenate([part[at] for part in held], axis=1)
+                place_of = (row_half * HALF_LAT + row, col_half * HALF_LON + col)
+                out[place_of] = (cot_ref[place_of].astype(jnp.float32) + token).astype(jnp.bfloat16)
 
 
 def unpack(place, cotangent, *quarters):
-    whole = pl.BlockSpec(memory_space=pltpu.VMEM)
-    return pl.pallas_call(
+    local = pl.pallas_call(
         unpack_kernel,
-        out_shape=jax.ShapeDtypeStruct(cotangent.shape, jnp.bfloat16),
-        in_specs=[pl.BlockSpec(memory_space=pltpu.SMEM)] + [whole] * 4,
-        out_specs=whole,
+        out_shape=jax.ShapeDtypeStruct(LOCAL, jnp.bfloat16),
+        in_specs=[SMEM] + [VMEM] * 3 + [HBM],
+        out_specs=VMEM,
+        scratch_shapes=[
+            pltpu.VMEM(LOCAL, jnp.bfloat16),
+            pltpu.VMEM((16, LEVELS * HALF_LAT * HALF_LON, 128), jnp.float32),
+            pltpu.SemaphoreType.DMA((1,)),
+        ],
         compiler_params=pltpu.CompilerParams(vmem_limit_bytes=32 * 2**20),
         cost_estimate=pl.CostEstimate(flops=0, bytes_accessed=900000, transcendentals=0),
         name="unpack",
-    )(place, cotangent, *quarters)
+    )(place, *quarters, cotangent.transpose(1, 2, 0, 3))
+    return local.transpose(2, 0, 1, 3)
 
 
 def weights_kernel(qkv_weight, proj_weight, qkv_held, proj_held, semaphores):
@@ -313,6 +323,32 @@
     return device_groups(members)
 
 
+def strided(size):
+    step = min(size, 2)
+    return [list(range(parity, size, step)) for parity in range(step)]
+
+
+def middle_groups():
+    def members(core):
+        z_size, y_size, x_size = chips()
+        xs = strided(x_size)
+        if core == 0:
+            return [[(z, y, x) for x in xa for z in za] for xa in xs for za in strided(z_size) for y in range(y_size)]
+        return [[(z, y, x) for x in xa for y in ya] for xa in xs for ya in strided(y_size) for z in range(z_size)]
+
+    return device_groups(members)
+
+
+def far_groups():
+    def members(core):
+        z_size, y_size, x_size = chips()
+        if core == 0:
+            return [[(z, y, x) for y in ya] for ya in strided(y_size) for z in range(z_size) for x in range(x_size)]
+        return [[(z, y, x) for z in za] for za in strided(z_size) for y in range(y_size) for x in range(x_size)]
+
+    return device_groups(members)
+
+
 def swapped(value):
     at = [(z, y, x) for z, y, x in itertools.product(*(range(size) for size in chips()))]
     first, second = device_groups(lambda core: [at])
@@ -386,25 +422,27 @@
     place = jnp.stack([odd, lat == 0, lon_edge, lax.axis_index("core") == 1]).astype(jnp.int32)
     own, lon, lat, both = pack(place, activations, cotangent)
     own, qkv_weight, proj_weight = lax.optimization_barrier((own, qkv_weight, proj_weight))
-    lat, lon, both = moved(lat, 2, False), moved(lon, 1, False), moved(both, 3, False)
+    both, lon, lat = moved(both, 3, False), moved(lon, 1, False), moved(lat, 2, False)
     qkv_weight, proj_weight = near_weights(qkv_weight, proj_weight)
     theirs, mine, own, lat, lon_both = block(place, (own, lon, lat, both), qkv_weight, proj_weight)
 
-    near, middle, far = cube_groups(1), cube_groups(2), cube_groups(4)
+    near, middle, far = cube_groups(1), middle_groups(), far_groups()
     tiles = (mine.astype(jnp.float32) + swapped(theirs).astype(jnp.float32)).astype(jnp.bfloat16)
-    tiles, lon_both = lax.optimization_barrier((tiles.reshape(-1, 16, 128), lon_both))
-    tiles, lon_both = lax.optimization_barrier((scattered_sum(tiles, near), moved(lon_both, 1, True)))
+    tiles = scattered_sum(tiles.reshape(-1, 16, 128), near)
+    tiles, lon_both = lax.optimization_barrier((tiles, lon_both))
     tiles = scattered_sum(tiles, middle)
     factor = (LEVELS * ROWS * COLS * lax.axis_size(ALL)) ** (-0.5)
-    tiles = (added(exchanged(tiles, far)) * factor).astype(jnp.bfloat16)
+    tiles, lon_both = lax.optimization_barrier((exchanged(tiles, far), moved(lon_both, 1, True)))
+    tiles = (added(tiles) * factor).astype(jnp.bfloat16)
     lat_both = jnp.concatenate([lat, lon_both[2 * QUARTER :]], axis=0)
-    tiles, lat_both = lax.optimization_barrier((gathered(tiles, middle), lat_both))
-    tiles, lat_both = lax.optimization_barrier((gathered(tiles, near), moved(lat_both, 2, True)))
+    tiles, lat_both = lax.optimization_barrier((tiles, lat_both))
+    tiles, lat_both = lax.optimization_barrier((gathered(tiles, middle), moved(lat_both, 2, True)))
+    input_grad = unpack(place, cotangent, own, lon_both, lat_both)
+    tiles, input_grad = lax.optimization_barrier((gathered(tiles, near), input_grad))
     tiles = tiles.reshape(HALF_TILES.shape)
     arrived = swapped(tiles)
     grads = untile(place, tiles, False)
-    input_grad = unpack(place, cotangent, own, lon_both, lat_both)
-    arrived, grads, input_grad = lax.optimization_barrier((arrived, grads, input_grad))
+    arrived, grads = lax.optimization_barrier((arrived, grads))
     qkv_weight_grad, proj_weight_grad = untile(place, arrived, True, grads)
     return (input_grad, qkv_weight_grad, proj_weight_grad)
 

time: 137 us -> 128 us (0.934)
  blocking collectives: 27.6 us -> 17.3 us
  starting transfers between devices: 50 us -> 58.4 us
  waiting for transfers between devices: 37.9 us -> 31 us
    all_to_all x2 -> x1, blocking collectives: 27.6 us -> 17.3 us  [all_to_all(): return lax.all_to_all(split, ALL, 0, 0, axis_index_groups=groups)]
    ppermute x5, waiting for transfers between devices: 12 us -> 4.45 us  [moved(): return lax.ppermute(value, ALL, pairs)]
    all_to_all x3 -> x4, starting transfers between devices: 10.5 us -> 15.2 us  [all_to_all(): return lax.all_to_all(split, ALL, 0, 0, axis_index_groups=groups)]
    ppermute x5, starting transfers between devices: 25.1 us -> 29.5 us  [moved(): return lax.ppermute(value, ALL, pairs)]
    unnamed x12 -> x10, local copies, waits for them, and re-layouts: 5.38 us -> 4.37 us
    all_to_all x3 -> x4, waiting for transfers between devices: 23.6 us -> 23.7 us  [all_to_all(): return lax.all_to_all(split, ALL, 0, 0, axis_index_groups=groups)]
  transfers between devices with their start and end apart: 10 -> 11, of which waited for: 5 -> 8; matrix products, arithmetic and copies ran while one was open for 0% -> 1% of each run, Pallas kernels for 2% -> 3%
where the time goes in v5:
time: 128 us
  starting transfers between devices  58.4 us (46%)
  waiting for transfers between devices  31 us (24%)
  blocking collectives  17.3 us (14%)
  Pallas kernels  12 us (9%)
  local copies, waits for them, and re-layouts  6.8 us (5%)
    ppermute x5, starting transfers between devices, moved(): return lax.ppermute(value, ALL, pairs)  29.5 us
    all_to_all x4, waiting for transfers between devices, all_to_all(): return lax.all_to_all(split, ALL, 0, 0, axis_index_groups=groups)  23.7 us
    all_to_all x1, blocking collectives, all_to_all(): return lax.all_to_all(split, ALL, 0, 0, axis_index_groups=groups)  17.3 us
    all_to_all x4, starting transfers between devices, all_to_all(): return lax.all_to_all(split, ALL, 0, 0, axis_index_groups=groups)  15.2 us
    ppermute x2, starting transfers between devices, swapped(): return lax.ppermute(value, ALL, [*zip(first, second), *zip(second, first)])  13.7 us
    pallas_call x1, Pallas kernels, block(): pl.pallas_call(block_kernel, out_shape=(HALF_TILES, HALF_TILES, rows_of(2...  6.13 us
    ppermute x5, waiting for transfers between devices, moved(): return lax.ppermute(value, ALL, pairs)  4.45 us
    unnamed x10, local copies, waits for them, and re-layouts  4.37 us
  transfers between devices with their start and end apart: 11, of which 8 were waited for; matrix products, arithmetic and copies ran while one was open for 1% of the time, Pallas kernels for 3%

profile of v5, /device:TPU:1, one launch (start us, length us, event | category | flops | bytes accessed | tf_op | source)
XLA Modules:
  0.0 127.6 jit_solution(1303463376851028490)
XLA Ops:
  3.6 5.6 %collective-permute-start = (bf16[144,512]{1,0:T(8,128)(2,1)S(1)}, bf16[144,512]{1,0:T(8,128)(2,1)S(1)}, u32[]{:S(2)}, u32[]{:S(2)}) collective-permute-start(bf16[144,512]{1,0:T(8,128)(2,1)S(1)} %get-tuple-element.36), channel_id=1, source_target_pairs={{0,8},{1,505},{2,10},{3,507},{4,12},{5,509},{6,14},{7,511},{8,16},... | collective-permute-start | bytes 442376 | tf_op jit(solution)/shard_map/ppermute | solution.py:47
  9.2 1.9 %collective-permute-start.1 = (bf16[144,512]{1,0:T(8,128)(2,1)S(1)}, bf16[144,512]{1,0:T(8,128)(2,1)S(1)}, u32[]{:S(2)}, u32[]{:S(2)}) collective-permute-start(bf16[144,512]{1,0:T(8,128)(2,1)S(1)} %get-tuple-element.37), channel_id=1, source_target_pairs={{0,1},{1,2},{2,3},{3,4},{4,5},{5,6},{6,7},{7,0},{8,9},{9,10},{10,1... | collective-permute-start | bytes 442376 | tf_op jit(solution)/shard_map/ppermute | solution.py:47
  11.1 12.2 %collective-permute-start.2 = (bf16[144,512]{1,0:T(8,128)(2,1)S(1)}, bf16[144,512]{1,0:T(8,128)(2,1)S(1)}, u32[]{:S(2)}, u32[]{:S(2)}) collective-permute-start(bf16[144,512]{1,0:T(8,128)(2,1)S(1)} %get-tuple-element.38), channel_id=1, source_target_pairs={{0,505},{1,10},{2,507},{3,12},{4,509},{5,14},{6,511},{7,8},{8,1},{... | collective-permute-start | bytes 442376 | tf_op jit(solution)/shard_map/ppermute | solution.py:47
  23.3 1.4 %copy-done = bf16[512,1536]{1,0:T(8,128)(2,1)S(1)} copy-done((bf16[512,1536]{1,0:T(8,128)(2,1)S(1)}, bf16[512,1536]{1,0:T(8,128)(2,1)}, u32[]{:S(2)}) %copy-start) | copy-done | bytes 1572888
  25.9 2.4 %collective-permute-done.2.refs_3_ = bf16[144,512]{1,0:T(8,128)(2,1)S(1)} collective-permute-done((bf16[144,512]{1,0:T(8,128)(2,1)S(1)}, bf16[144,512]{1,0:T(8,128)(2,1)S(1)}, u32[]{:S(2)}, u32[]{:S(2)}) %collective-permute-start.2) | collective-permute-done | bytes 147488 | tf_op jit(solution)/shard_map/ppermute | solution.py:47
  28.3 6.1 %block.1 = (bf16[16,16,16,128]{3,2,1,0:T(8,128)(2,1)S(1)}, bf16[16,16,16,128]{3,2,1,0:T(8,128)(2,1)S(1)}, bf16[72,512]{1,0:T(8,128)(2,1)S(1)}, bf16[72,512]{1,0:T(8,128)(2,1)S(1)}, bf16[144,512]{1,0:T(8,128)(2,1)S(1)}) custom-call(s32[4]{0:T(128)S(1)} %add_convert_fusion.3.place, bf16[144,512]{1,0:T(8,128)(2,1)S(1)} %get-tuple-element.35.refs_0_, ...), custom_call_target="tpu_custom_call" | custom-call | flops 2000000000 | bytes 6000000 | tf_op jit(solution)/shard_map/block/pallas_call | solution.py:273
  34.4 7.2 %collective-permute-start.3 = (bf16[16,16,16,128]{3,2,1,0:T(8,128)(2,1)S(1)}, bf16[16,16,16,128]{3,2,1,0:T(8,128)(2,1)S(1)}, u32[]{:S(2)}, u32[]{:S(2)}) collective-permute-start(bf16[16,16,16,128]{3,2,1,0:T(8,128)(2,1)S(1)} %get-tuple-element.44), channel_id=1, source_target_pairs={{0,8},{2,10},{4,12},{6,14},{1,9},{3,11},{5,13},{7,15},{16,24},{18,... | collective-permute-start | bytes 3145736 | tf_op jit(solution)/shard_map/ppermute | solution.py:355
  41.7 2.3 %collective-permute-done.3 = bf16[16,16,16,128]{3,2,1,0:T(8,128)(2,1)S(1)} collective-permute-done((bf16[16,16,16,128]{3,2,1,0:T(8,128)(2,1)S(1)}, bf16[16,16,16,128]{3,2,1,0:T(8,128)(2,1)S(1)}, u32[]{:S(2)}, u32[]{:S(2)}) %collective-permute-start.3) | collective-permute-done | bytes 1048608 | tf_op jit(solution)/shard_map/ppermute | solution.py:355
  44.2 17.3 %all_to_all.25 = bf16[8,32,16,128]{3,2,1,0:T(8,128)(2,1)S(1)} all-to-all(bf16[8,32,16,128]{3,2,1,0:T(8,128)(2,1)S(1)} %bitcast.23), channel_id=1, replica_groups={{0,2,1,3,64,66,65,67},{4,6,5,7,68,70,69,71},{16,18,17,19,80,82,81,83},{..., dimensions={0} | all-to-all | bytes 2097152 | tf_op jit(solution)/shard_map/all_to_all | solution.py:359
  62.3 3.4 %all-to-all-start.1 = ((bf16[8,4,16,128]{3,2,1,0:T(8,128)(2,1)}), bf16[8,4,16,128]{3,2,1,0:T(8,128)(2,1)S(1)}, u32[]{:S(2)}, u32[]{:S(2)}) async-start(bf16[8,4,16,128]{3,2,1,0:T(8,128)(2,1)} %bitcast.8), calls=%async_computation.1 | async-start | bytes 262144 | tf_op jit(solution)/shard_map/all_to_all | solution.py:359
  65.7 3.4 %collective-permute-start.4 = (bf16[144,512]{1,0:T(8,128)(2,1)S(1)}, bf16[144,512]{1,0:T(8,128)(2,1)S(1)}, u32[]{:S(2)}, u32[]{:S(2)}) collective-permute-start(bf16[144,512]{1,0:T(8,128)(2,1)S(1)} %get-tuple-element.47), channel_id=1, source_target_pairs={{8,0},{505,1},{10,2},{507,3},{12,4},{509,5},{14,6},{511,7},{16,8},... | collective-permute-start | bytes 442376 | tf_op jit(solution)/shard_map/ppermute | solution.py:47
  69.1 5.8 %all-to-all-done.1 = bf16[8,4,16,128]{3,2,1,0:T(8,128)(2,1)S(1)} async-done(((bf16[8,4,16,128]{3,2,1,0:T(8,128)(2,1)}), bf16[8,4,16,128]{3,2,1,0:T(8,128)(2,1)S(1)}, u32[]{:S(2)}, u32[]{:S(2)}) %all-to-all-start.1) | async-done | bytes 131104 | tf_op jit(solution)/shard_map/all_to_all | solution.py:359
  75.6 3.3 %all-to-all-start.2 = ((bf16[4,4,16,128]{3,2,1,0:T(8,128)(2,1)}), bf16[4,4,16,128]{3,2,1,0:T(8,128)(2,1)S(1)}, u32[]{:S(2)}, u32[]{:S(2)}) async-start(bf16[4,4,16,128]{3,2,1,0:T(8,128)(2,1)} %broadcast_in_dim.9), calls=%async_computation.2 | async-start | bytes 131072 | tf_op jit(solution)/shard_map/all_to_all | solution.py:359
  78.9 6.8 %all-to-all-done.2 = bf16[4,4,16,128]{3,2,1,0:T(8,128)(2,1)S(1)} async-done(((bf16[4,4,16,128]{3,2,1,0:T(8,128)(2,1)}), bf16[4,4,16,128]{3,2,1,0:T(8,128)(2,1)S(1)}, u32[]{:S(2)}, u32[]{:S(2)}) %all-to-all-start.2) | async-done | bytes 65568 | tf_op jit(solution)/shard_map/all_to_all | solution.py:359
  86.5 3.4 %all-to-all-start.3 = ((bf16[8,4,16,128]{3,2,1,0:T(8,128)(2,1)}), bf16[8,4,16,128]{3,2,1,0:T(8,128)(2,1)S(1)}, u32[]{:S(2)}, u32[]{:S(2)}) async-start(bf16[8,4,16,128]{3,2,1,0:T(8,128)(2,1)} %broadcast_in_dim.10), calls=%async_computation.3 | async-start | bytes 262144 | tf_op jit(solution)/shard_map/all_to_all | solution.py:359
  89.9 6.4 %collective-permute-start.5 = (bf16[144,512]{1,0:T(8,128)(2,1)S(1)}, bf16[144,512]{1,0:T(8,128)(2,1)S(1)}, u32[]{:S(2)}, u32[]{:S(2)}) collective-permute-start(bf16[144,512]{1,0:T(8,128)(2,1)S(1)} %pad_maximum_fusion), channel_id=1, source_target_pairs={{1,0},{2,1},{3,2},{4,3},{5,4},{6,5},{7,6},{0,7},{9,8},{10,9},{11,1... | collective-permute-start | bytes 442376 | tf_op jit(solution)/shard_map/ppermute | solution.py:47
  96.3 2.1 %collective-permute-done.5.lat_both = bf16[144,512]{1,0:T(8,128)(2,1)S(1)} collective-permute-done((bf16[144,512]{1,0:T(8,128)(2,1)S(1)}, bf16[144,512]{1,0:T(8,128)(2,1)S(1)}, u32[]{:S(2)}, u32[]{:S(2)}) %collective-permute-start.5) | collective-permute-done | bytes 147488 | tf_op jit(solution)/shard_map/ppermute | solution.py:47
  99.1 1.1 broadcast_in_dim.11
  100.2 5.2 %all-to-all-start.4 = ((bf16[8,32,16,128]{3,2,1,0:T(8,128)(2,1)}), bf16[8,32,16,128]{3,2,1,0:T(8,128)(2,1)S(1)}, u32[]{:S(2)}, u32[]{:S(2)}) async-start(bf16[8,32,16,128]{3,2,1,0:T(8,128)(2,1)} %broadcast_in_dim.11), calls=%async_computation.4 | async-start | bytes 2097152 | tf_op jit(solution)/shard_map/all_to_all | solution.py:359
  105.4 1.6 %unpack.1 = bf16[6,12,4,512]{3,2,1,0:T(4,128)(2,1)} custom-call(s32[4]{0:T(128)S(1)} %add_convert_fusion.3.place, bf16[72,512]{1,0:T(8,128)(2,1)S(1)} %get-tuple-element.54.own, bf16[144,512]{1,0:T(8,128)(2,1)S(1)} %collective-permute-done.4.lon_ref, bf16[144,512]{1,0:T(8,128)(2,1)S(1)} %collective-permute-done.5.lat_both, bf16[6,12,4,512]{3,2,1,0:T(4,128)(2,1)S(1)} %bitcast.21), custom_call_target="tpu_custom_call" | custom-call | bytes 900000 | tf_op jit(solution)/shard_map/unpack/pallas_call | solution.py:142
  107.0 10.2 %all-to-all-done.4 = bf16[8,32,16,128]{3,2,1,0:T(8,128)(2,1)S(1)} async-done(((bf16[8,32,16,128]{3,2,1,0:T(8,128)(2,1)}), bf16[8,32,16,128]{3,2,1,0:T(8,128)(2,1)S(1)}, u32[]{:S(2)}, u32[]{:S(2)}) %all-to-all-start.4) | async-done | bytes 1048608 | tf_op jit(solution)/shard_map/all_to_all | solution.py:359
  117.2 6.5 %collective-permute-start.6 = (bf16[16,16,16,128]{3,2,1,0:T(8,128)(2,1)S(1)}, bf16[16,16,16,128]{3,2,1,0:T(8,128)(2,1)S(1)}, u32[]{:S(2)}, u32[]{:S(2)}) collective-permute-start(bf16[16,16,16,128]{3,2,1,0:T(8,128)(2,1)S(1)} %bitcast.18), channel_id=1, source_target_pairs={{0,8},{2,10},{4,12},{6,14},{1,9},{3,11},{5,13},{7,15},{16,24},{18,... | collective-permute-start | bytes 3145736 | tf_op jit(solution)/shard_map/ppermute | solution.py:355
  123.7 1.6 %untile_own.1 = (bf16[512,1536]{1,0:T(8,128)(2,1)}, bf16[512,512]{1,0:T(8,128)(2,1)}) custom-call(s32[4]{0:T(128)S(1)} %add_convert_fusion.3.place, bf16[16,16,16,128]{3,2,1,0:T(8,128)(2,1)S(1)} %bitcast.19), custom_call_target="tpu_custom_call" | custom-call | bytes 2097152 | tf_op jit(solution)/shard_map/untile_own/pallas_call | solution.py:401
  125.9 1.6 %untile_other.1 = (bf16[512,1536]{1,0:T(8,128)(2,1)}, bf16[512,512]{1,0:T(8,128)(2,1)}) custom-call(s32[4]{0:T(128)S(1)} %add_convert_fusion.3.place, bf16[16,16,16,128]{3,2,1,0:T(8,128)(2,1)S(1)} %collective-permute-done.6.tiles, bf16[512,1536]{1,0:T(8,128)(2,1)} %get-tuple-element.61.refs_0_, ...), custom_call_target="tpu_custom_call", output_to_operand_aliasing={{0}: (2, {}), {1}: (3, {})} | custom-call | bytes 2097152 | tf_op jit(solution)/shard_map/untile_other/pallas_call | solution.py:401
  (25 shorter events, 8.0 us)
Async XLA Ops:
  0.7 1.0 copy-start.1
  1.7 1.0 copy-start.4
  3.6 22.3 %collective-permute-start = (bf16[144,512]{1,0:T(8,128)(2,1)S(1)}, bf16[144,512]{1,0:T(8,128)(2,1)S(1)}, u32[]{:S(2)}, u32[]{:S(2)}) collective-permute-start(bf16[144,512]{1,0:T(8,128)(2,1)S(1)} %get-tuple-element.36), channel_id=1, source_target_pairs={{0,8},{1,505},{2,10},{3,507},{4,12},{5,509},{6,14},{7,511},{8,16},... | collective-permute-start | bytes 442376 | tf_op jit(solution)/shard_map/ppermute | solution.py:47
  9.2 16.7 %collective-permute-start.1 = (bf16[144,512]{1,0:T(8,128)(2,1)S(1)}, bf16[144,512]{1,0:T(8,128)(2,1)S(1)}, u32[]{:S(2)}, u32[]{:S(2)}) collective-permute-start(bf16[144,512]{1,0:T(8,128)(2,1)S(1)} %get-tuple-element.37), channel_id=1, source_target_pairs={{0,1},{1,2},{2,3},{3,4},{4,5},{5,6},{6,7},{7,0},{8,9},{9,10},{10,1... | collective-permute-start | bytes 442376 | tf_op jit(solution)/shard_map/ppermute | solution.py:47
  11.1 17.2 %collective-permute-start.2 = (bf16[144,512]{1,0:T(8,128)(2,1)S(1)}, bf16[144,512]{1,0:T(8,128)(2,1)S(1)}, u32[]{:S(2)}, u32[]{:S(2)}) collective-permute-start(bf16[144,512]{1,0:T(8,128)(2,1)S(1)} %get-tuple-element.38), channel_id=1, source_target_pairs={{0,505},{1,10},{2,507},{3,12},{4,509},{5,14},{6,511},{7,8},{8,1},{... | collective-permute-start | bytes 442376 | tf_op jit(solution)/shard_map/ppermute | solution.py:47
  23.3 1.4 %copy-start = (bf16[512,1536]{1,0:T(8,128)(2,1)S(1)}, bf16[512,1536]{1,0:T(8,128)(2,1)}, u32[]{:S(2)}) copy-start(bf16[512,1536]{1,0:T(8,128)(2,1)} %qkv_weight) | copy-start | bytes 4718596
  24.7 1.0 copy-start.3
  34.4 9.5 %collective-permute-start.3 = (bf16[16,16,16,128]{3,2,1,0:T(8,128)(2,1)S(1)}, bf16[16,16,16,128]{3,2,1,0:T(8,128)(2,1)S(1)}, u32[]{:S(2)}, u32[]{:S(2)}) collective-permute-start(bf16[16,16,16,128]{3,2,1,0:T(8,128)(2,1)S(1)} %get-tuple-element.44), channel_id=1, source_target_pairs={{0,8},{2,10},{4,12},{6,14},{1,9},{3,11},{5,13},{7,15},{16,24},{18,... | collective-permute-start | bytes 3145736 | tf_op jit(solution)/shard_map/ppermute | solution.py:355
  62.3 12.6 %all-to-all-start.1 = ((bf16[8,4,16,128]{3,2,1,0:T(8,128)(2,1)}), bf16[8,4,16,128]{3,2,1,0:T(8,128)(2,1)S(1)}, u32[]{:S(2)}, u32[]{:S(2)}) async-start(bf16[8,4,16,128]{3,2,1,0:T(8,128)(2,1)} %bitcast.8), calls=%async_computation.1 | async-start | bytes 262144 | tf_op jit(solution)/shard_map/all_to_all | solution.py:359
  65.7 13.2 %collective-permute-start.4 = (bf16[144,512]{1,0:T(8,128)(2,1)S(1)}, bf16[144,512]{1,0:T(8,128)(2,1)S(1)}, u32[]{:S(2)}, u32[]{:S(2)}) collective-permute-start(bf16[144,512]{1,0:T(8,128)(2,1)S(1)} %get-tuple-element.47), channel_id=1, source_target_pairs={{8,0},{505,1},{10,2},{507,3},{12,4},{509,5},{14,6},{511,7},{16,8},... | collective-permute-start | bytes 442376 | tf_op jit(solution)/shard_map/ppermute | solution.py:47
  75.6 10.1 %all-to-all-start.2 = ((bf16[4,4,16,128]{3,2,1,0:T(8,128)(2,1)}), bf16[4,4,16,128]{3,2,1,0:T(8,128)(2,1)S(1)}, u32[]{:S(2)}, u32[]{:S(2)}) async-start(bf16[4,4,16,128]{3,2,1,0:T(8,128)(2,1)} %broadcast_in_dim.9), calls=%async_computation.2 | async-start | bytes 131072 | tf_op jit(solution)/shard_map/all_to_all | solution.py:359
  86.5 12.6 %all-to-all-start.3 = ((bf16[8,4,16,128]{3,2,1,0:T(8,128)(2,1)}), bf16[8,4,16,128]{3,2,1,0:T(8,128)(2,1)S(1)}, u32[]{:S(2)}, u32[]{:S(2)}) async-start(bf16[8,4,16,128]{3,2,1,0:T(8,128)(2,1)} %broadcast_in_dim.10), calls=%async_computation.3 | async-start | bytes 262144 | tf_op jit(solution)/shard_map/all_to_all | solution.py:359
  89.9 8.5 %collective-permute-start.5 = (bf16[144,512]{1,0:T(8,128)(2,1)S(1)}, bf16[144,512]{1,0:T(8,128)(2,1)S(1)}, u32[]{:S(2)}, u32[]{:S(2)}) collective-permute-start(bf16[144,512]{1,0:T(8,128)(2,1)S(1)} %pad_maximum_fusion), channel_id=1, source_target_pairs={{1,0},{2,1},{3,2},{4,3},{5,4},{6,5},{7,6},{0,7},{9,8},{10,9},{11,1... | collective-permute-start | bytes 442376 | tf_op jit(solution)/shard_map/ppermute | solution.py:47
  99.1 6.3 %copy-start.2 = (bf16[4,6,12,512]{3,0,2,1:T(4,128)(2,1)S(1)}, bf16[4,6,12,512]{3,0,2,1:T(4,128)(2,1)}, u32[]{:S(2)}) copy-start(bf16[4,6,12,512]{3,0,2,1:T(4,128)(2,1)} %param.5) | copy-start | bytes 884740
  100.2 17.0 %all-to-all-start.4 = ((bf16[8,32,16,128]{3,2,1,0:T(8,128)(2,1)}), bf16[8,32,16,128]{3,2,1,0:T(8,128)(2,1)S(1)}, u32[]{:S(2)}, u32[]{:S(2)}) async-start(bf16[8,32,16,128]{3,2,1,0:T(8,128)(2,1)} %broadcast_in_dim.11), calls=%async_computation.4 | async-start | bytes 2097152 | tf_op jit(solution)/shard_map/all_to_all | solution.py:359
  117.2 8.7 %collective-permute-start.6 = (bf16[16,16,16,128]{3,2,1,0:T(8,128)(2,1)S(1)}, bf16[16,16,16,128]{3,2,1,0:T(8,128)(2,1)S(1)}, u32[]{:S(2)}, u32[]{:S(2)}) collective-permute-start(bf16[16,16,16,128]{3,2,1,0:T(8,128)(2,1)S(1)} %bitcast.18), channel_id=1, source_target_pairs={{0,8},{2,10},{4,12},{6,14},{1,9},{3,11},{5,13},{7,15},{16,24},{18,... | collective-permute-start | bytes 3145736 | tf_op jit(solution)/shard_map/ppermute | solution.py:355

commit v6 on v5

--- a/solution.py
+++ b/solution.py
@@ -175,9 +175,10 @@
 
 
 def block_kernel(place, *refs):
-    quarters, (qkv_weight, proj_weight), (theirs, mine, own, lat, lon_both) = refs[:4], refs[4:6], refs[6:11]
-    x_held, cot_held, normed, attended, qkv_grad, qkv, upstream, tiles = refs[11:]
-    held = [ref[...].astype(jnp.float32) for ref in quarters]
+    quarters, (qkv_weight, proj_weight), theirs, mine, (own, lat, lon_both) = refs[:4], refs[4:6], refs[6:8], refs[8:10], refs[10:13]
+    x_held, cot_held, normed, attended, qkv_grad, qkv, upstream, tiles = refs[13:]
+    own_ref, both_ref, lon_ref, lat_ref = quarters
+    held = [ref[...].astype(jnp.float32) for ref in (own_ref, lon_ref, lat_ref, both_ref)]
     for kind, target in enumerate((x_held, cot_held)):
         chunks = [
             held[quarter][(2 * kind + window) * QUARTER : (2 * kind + window + 1) * QUARTER]
@@ -245,8 +246,10 @@
     tall = attended[...].T
     for step in range(D // 256):
         put(step + 3 * D // 256, dot(tall, cot_held[:, step * 256 : (step + 1) * 256], 1, 0))
-    theirs[...] = tiles[1 - place[3]]
-    mine[...] = tiles[place[3]]
+    for chunk in range(2):
+        rows = slice(chunk * D // 64, (chunk + 1) * D // 64)
+        theirs[chunk][...] = tiles[1 - place[3], rows]
+        mine[chunk][...] = tiles[place[3], rows]
     normed_grad = dot(qkv_grad[...], qkv_weight[...], 1, 1)
     x = x_held[...].astype(jnp.float32)
     centered = x - jnp.mean(x, axis=-1, keepdims=True)
@@ -262,7 +265,7 @@
         target[...] = jnp.concatenate(chunks, axis=0).astype(jnp.bfloat16)
 
 
-HALF_TILES = jax.ShapeDtypeStruct((D // 32, 4 * D // 128, 16, 128), jnp.bfloat16)
+CHUNK_TILES = jax.ShapeDtypeStruct((D // 64, 4 * D // 128, 16, 128), jnp.bfloat16)
 
 
 def rows_of(count, width=D):
@@ -272,9 +275,9 @@
 def block(place, quarters, qkv_weight, proj_weight):
     return pl.pallas_call(
         block_kernel,
-        out_shape=(HALF_TILES, HALF_TILES, rows_of(2 * QUARTER), rows_of(2 * QUARTER), rows_of(4 * QUARTER)),
+        out_shape=(CHUNK_TILES,) * 4 + (rows_of(2 * QUARTER), rows_of(2 * QUARTER), rows_of(4 * QUARTER)),
         in_specs=[SMEM] + [VMEM] * 6,
-        out_specs=(VMEM,) * 5,
+        out_specs=(VMEM,) * 7,
         scratch_shapes=[
             pltpu.VMEM((TOKENS, D), jnp.bfloat16),
             pltpu.VMEM((TOKENS, D), jnp.bfloat16),
@@ -283,7 +286,7 @@
             pltpu.VMEM((TOKENS, 3 * D), jnp.bfloat16),
             pltpu.VMEM((TOKENS, 3 * D), jnp.bfloat16),
             pltpu.VMEM((TOKENS, D), jnp.bfloat16),
-            pltpu.VMEM((2,) + HALF_TILES.shape, jnp.bfloat16),
+            pltpu.VMEM((2, D // 32, 4 * D // 128, 16, 128), jnp.bfloat16),
         ],
         compiler_params=pltpu.CompilerParams(vmem_limit_bytes=48 * 2**20),
         cost_estimate=pl.CostEstimate(flops=2 * 10**9, bytes_accessed=6 * 10**6, transcendentals=6 * 10**5),
@@ -373,20 +376,21 @@
     return exchanged(tiles, groups).reshape((-1,) + tiles.shape[1:])
 
 
-def untile_kernel(other, place, tiles, *refs):
+def untile_kernel(other, place, *refs):
     qkv_out, proj_out, qkv_held, proj_held, semaphores = refs[-5:]
     first = (1 - place[3] if other else place[3]) * (D // 2)
-    chunk = D // 2 // CHUNKS
+    height = D // 8
     copies = []
-    for at in range(CHUNKS):
-        rows = slice(at * chunk, (at + 1) * chunk)
+    for at in range(4):
+        tiles = refs[at // 2].at[at % 2 * height // 16 : (at % 2 + 1) * height // 16]
+        rows = slice(at * height, (at + 1) * height)
         for col in range(4 * D // 128):
-            strip = tiles[at * chunk // 16 : (at + 1) * chunk // 16, col].reshape(chunk, 128)
+            strip = tiles[:, col].reshape(height, 128)
             if col < 3 * D // 128:
                 qkv_held[rows, 128 * col : 128 * col + 128] = strip
             else:
                 proj_held[rows, 128 * col - 3 * D : 128 * col - 3 * D + 128] = strip
-        target = pl.ds(pl.multiple_of(first + at * chunk, chunk), chunk)
+        target = pl.ds(pl.multiple_of(first + at * height, height), height)
         for kind, (held, out) in enumerate(((qkv_held, qkv_out), (proj_held, proj_out))):
             copies.append(pltpu.make_async_copy(held.at[rows], out.at[target], semaphores.at[2 * at + kind]))
             copies[-1].start()
@@ -394,25 +398,22 @@
         copy.wait()
 
 
-CHUNKS = 4
-
-
-def untile(place, tiles, other, so_far=()):
+def untile(place, chunks, other, so_far=()):
     return pl.pallas_call(
         functools.partial(untile_kernel, other),
-        in_specs=[SMEM, VMEM] + [HBM] * len(so_far),
+        in_specs=[SMEM, VMEM, VMEM] + [HBM] * len(so_far),
         out_specs=(HBM, HBM),
         out_shape=(rows_of(D, 3 * D), rows_of(D)),
         scratch_shapes=[
             pltpu.VMEM((D // 2, 3 * D), jnp.bfloat16),
             pltpu.VMEM((D // 2, D), jnp.bfloat16),
-            pltpu.SemaphoreType.DMA((2 * CHUNKS,)),
+            pltpu.SemaphoreType.DMA((8,)),
         ],
-        input_output_aliases={2: 0, 3: 1} if so_far else {},
+        input_output_aliases={3: 0, 4: 1} if so_far else {},
         compiler_params=pltpu.CompilerParams(vmem_limit_bytes=32 * 2**20),
         cost_estimate=pl.CostEstimate(flops=0, bytes_accessed=2 * 2**20, transcendentals=0),
         name="untile_other" if other else "untile_own",
-    )(place, tiles, *so_far)
+    )(place, *chunks, *so_far)
 
 
 def per_device(activations, cotangent, qkv_weight, proj_weight):
@@ -424,11 +425,14 @@
     own, qkv_weight, proj_weight = lax.optimization_barrier((own, qkv_weight, proj_weight))
     both, lon, lat = moved(both, 3, False), moved(lon, 1, False), moved(lat, 2, False)
     qkv_weight, proj_weight = near_weights(qkv_weight, proj_weight)
-    theirs, mine, own, lat, lon_both = block(place, (own, lon, lat, both), qkv_weight, proj_weight)
+    *grads, own, lat, lon_both = block(place, (own, both, lon, lat), qkv_weight, proj_weight)
 
     near, middle, far = cube_groups(1), middle_groups(), far_groups()
-    tiles = (mine.astype(jnp.float32) + swapped(theirs).astype(jnp.float32)).astype(jnp.bfloat16)
-    tiles = scattered_sum(tiles.reshape(-1, 16, 128), near)
+    chunks = []
+    for theirs, mine in zip(grads[:2], grads[2:]):
+        chunk = (mine.astype(jnp.float32) + swapped(theirs).astype(jnp.float32)).astype(jnp.bfloat16)
+        chunks.append(scattered_sum(chunk.reshape(-1, 16, 128), near))
+    tiles = jnp.concatenate(chunks, axis=0)
     tiles, lon_both = lax.optimization_barrier((tiles, lon_both))
     tiles = scattered_sum(tiles, middle)
     factor = (LEVELS * ROWS * COLS * lax.axis_size(ALL)) ** (-0.5)
@@ -438,10 +442,10 @@
     tiles, lat_both = lax.optimization_barrier((tiles, lat_both))
     tiles, lat_both = lax.optimization_barrier((gathered(tiles, middle), moved(lat_both, 2, True)))
     input_grad = unpack(place, cotangent, own, lon_both, lat_both)
-    tiles, input_grad = lax.optimization_barrier((gathered(tiles, near), input_grad))
-    tiles = tiles.reshape(HALF_TILES.shape)
-    arrived = swapped(tiles)
-    grads = untile(place, tiles, False)
+    chunks = [gathered(chunk, near).reshape(CHUNK_TILES.shape) for chunk in jnp.split(tiles, 2)]
+    arrived = [swapped(chunk) for chunk in chunks]
+    chunks, input_grad = lax.optimization_barrier((chunks, input_grad))
+    grads = untile(place, chunks, False)
     arrived, grads = lax.optimization_barrier((arrived, grads))
     qkv_weight_grad, proj_weight_grad = untile(place, arrived, True, grads)
     return (input_grad, qkv_weight_grad, proj_weight_grad)

time: 128 us -> 144 us (1.12)
  starting transfers between devices: 58.4 us -> 75.2 us
  blocking collectives: 17.3 us -> 9.64 us
  waiting for transfers between devices: 31 us -> 35.7 us
  other arithmetic: 1.2 us -> 2.81 us
    ppermute x2 -> x4, starting transfers between devices: 13.7 us -> 29.1 us  [swapped(): return lax.ppermute(value, ALL, [*zip(first, second), *zip(second, first)])]
    all_to_all x4 -> x6, starting transfers between devices: 15.2 us -> 25.5 us  [all_to_all(): return lax.all_to_all(split, ALL, 0, 0, axis_index_groups=groups)]
    ppermute x5, starting transfers between devices: 29.5 us -> 20.6 us  [moved(): return lax.ppermute(value, ALL, pairs)]
    all_to_all x1, blocking collectives: 17.3 us -> 9.64 us  [all_to_all(): return lax.all_to_all(split, ALL, 0, 0, axis_index_groups=groups)]
    all_to_all x4 -> x6, waiting for transfers between devices: 23.7 us -> 26.3 us  [all_to_all(): return lax.all_to_all(split, ALL, 0, 0, axis_index_groups=groups)]
    ppermute x5, waiting for transfers between devices: 4.45 us -> 6.36 us  [moved(): return lax.ppermute(value, ALL, pairs)]
    convert_element_type x1 -> x2, other arithmetic: 0.28 us -> 1.87 us  [per_device(): (mine.astype(jnp.float32) + swapped(theirs).astype(jnp.float32)).astype(j...]
    ppermute x2 -> x4, waiting for transfers between devices: 2.91 us -> 3.03 us  [swapped(): return lax.ppermute(value, ALL, [*zip(first, second), *zip(second, first)])]
  transfers between devices with their start and end apart: 11 -> 15, of which waited for: 8 -> 9; matrix products, arithmetic and copies ran while one was open for 1% -> 1% of each run, Pallas kernels for 3% -> 2%
where the time goes in v6:
time: 144 us; the launch traced here: 143 us
  starting transfers between devices  75.2 us (52%)
  waiting for transfers between devices  35.7 us (25%)
  Pallas kernels  12 us (8%)
  blocking collectives  9.64 us (7%)
  local copies, waits for them, and re-layouts  6.63 us (5%)
  other arithmetic  2.81 us (2%)
    ppermute x4, starting transfers between devices, swapped(): return lax.ppermute(value, ALL, [*zip(first, second), *zip(second, first)])  29.1 us
    all_to_all x6, waiting for transfers between devices, all_to_all(): return lax.all_to_all(split, ALL, 0, 0, axis_index_groups=groups)  26.3 us
    all_to_all x6, starting transfers between devices, all_to_all(): return lax.all_to_all(split, ALL, 0, 0, axis_index_groups=groups)  25.5 us
    ppermute x5, starting transfers between devices, moved(): return lax.ppermute(value, ALL, pairs)  20.6 us
    all_to_all x1, blocking collectives, all_to_all(): return lax.all_to_all(split, ALL, 0, 0, axis_index_groups=groups)  9.64 us
    ppermute x5, waiting for transfers between devices, moved(): return lax.ppermute(value, ALL, pairs)  6.36 us
    pallas_call x1, Pallas kernels, block(): pl.pallas_call(block_kernel, out_shape=(CHUNK_TILES,) * 4 + (rows_of(2 *...  6.12 us
    unnamed x10, local copies, waits for them, and re-layouts  4.37 us
  transfers between devices with their start and end apart: 15, of which 9 were waited for; matrix products, arithmetic and copies ran while one was open for 1% of the time, Pallas kernels for 2%

profile of v6, /device:TPU:1, one launch (start us, length us, event | category | flops | bytes accessed | tf_op | source)
XLA Modules:
  0.0 142.9 jit_solution(2302863716012206492)
XLA Ops:
  3.6 4.6 %collective-permute-start = (bf16[144,512]{1,0:T(8,128)(2,1)S(1)}, bf16[144,512]{1,0:T(8,128)(2,1)S(1)}, u32[]{:S(2)}, u32[]{:S(2)}) collective-permute-start(bf16[144,512]{1,0:T(8,128)(2,1)S(1)} %get-tuple-element.40), channel_id=1, source_target_pairs={{0,505},{1,10},{2,507},{3,12},{4,509},{5,14},{6,511},{7,8},{8,1},{... | collective-permute-start | bytes 442376 | tf_op jit(solution)/shard_map/ppermute | solution.py:47
  8.2 2.9 %collective-permute-start.1 = (bf16[144,512]{1,0:T(8,128)(2,1)S(1)}, bf16[144,512]{1,0:T(8,128)(2,1)S(1)}, u32[]{:S(2)}, u32[]{:S(2)}) collective-permute-start(bf16[144,512]{1,0:T(8,128)(2,1)S(1)} %get-tuple-element.41), channel_id=1, source_target_pairs={{0,8},{1,505},{2,10},{3,507},{4,12},{5,509},{6,14},{7,511},{8,16},... | collective-permute-start | bytes 442376 | tf_op jit(solution)/shard_map/ppermute | solution.py:47
  11.1 3.1 %collective-permute-start.2 = (bf16[144,512]{1,0:T(8,128)(2,1)S(1)}, bf16[144,512]{1,0:T(8,128)(2,1)S(1)}, u32[]{:S(2)}, u32[]{:S(2)}) collective-permute-start(bf16[144,512]{1,0:T(8,128)(2,1)S(1)} %get-tuple-element.42), channel_id=1, source_target_pairs={{0,1},{1,2},{2,3},{3,4},{4,5},{5,6},{6,7},{7,0},{8,9},{9,10},{10,1... | collective-permute-start | bytes 442376 | tf_op jit(solution)/shard_map/ppermute | solution.py:47
  16.9 4.3 %collective-permute-done.1.refs_2_ = bf16[144,512]{1,0:T(8,128)(2,1)S(1)} collective-permute-done((bf16[144,512]{1,0:T(8,128)(2,1)S(1)}, bf16[144,512]{1,0:T(8,128)(2,1)S(1)}, u32[]{:S(2)}, u32[]{:S(2)}) %collective-permute-start.1) | collective-permute-done | bytes 147488 | tf_op jit(solution)/shard_map/ppermute | solution.py:47
  21.1 6.1 %block.1 = (bf16[8,16,16,128]{3,2,1,0:T(8,128)(2,1)S(1)}, bf16[8,16,16,128]{3,2,1,0:T(8,128)(2,1)S(1)}, bf16[8,16,16,128]{3,2,1,0:T(8,128)(2,1)S(1)}, bf16[8,16,...) custom-call(s32[4]{0:T(128)S(1)} %add_convert_fusion.5.place, ...), custom_call_target="tpu_custom_call" | custom-call | flops 2000000000 | bytes 6000000 | tf_op jit(solution)/shard_map/block/pallas_call | solution.py:276
  27.3 10.2 %collective-permute-start.3 = (bf16[8,16,16,128]{3,2,1,0:T(8,128)(2,1)S(1)}, bf16[8,16,16,128]{3,2,1,0:T(8,128)(2,1)S(1)}, u32[]{:S(2)}, u32[]{:S(2)}) collective-permute-start(bf16[8,16,16,128]{3,2,1,0:T(8,128)(2,1)S(1)} %get-tuple-element.48), channel_id=1, source_target_pairs={{0,8},{2,10},{4,12},{6,14},{1,9},{3,11},{5,13},{7,15},{16,24},{18,... | collective-permute-start | bytes 1572872 | tf_op jit(solution)/shard_map/ppermute | solution.py:358
  39.9 3.5 %all-to-all-start = ((bf16[8,16,16,128]{3,2,1,0:T(8,128)(2,1)}), bf16[8,16,16,128]{3,2,1,0:T(8,128)(2,1)S(1)}, u32[]{:S(2)}, u32[]{:S(2)}) async-start(bf16[8,16,16,128]{3,2,1,0:T(8,128)(2,1)} %add_convert_fusion.1), calls=%async_computation | async-start | bytes 1048576 | tf_op jit(solution)/shard_map/all_to_all | solution.py:362
  43.4 2.3 %collective-permute-start.4 = (bf16[8,16,16,128]{3,2,1,0:T(8,128)(2,1)S(1)}, bf16[8,16,16,128]{3,2,1,0:T(8,128)(2,1)S(1)}, u32[]{:S(2)}, u32[]{:S(2)}) collective-permute-start(bf16[8,16,16,128]{3,2,1,0:T(8,128)(2,1)S(1)} %get-tuple-element.50), channel_id=1, source_target_pairs={{0,8},{2,10},{4,12},{6,14},{1,9},{3,11},{5,13},{7,15},{16,24},{18,... | collective-permute-start | bytes 1572872 | tf_op jit(solution)/shard_map/ppermute | solution.py:358
  48.2 4.4 %all-to-all-done = bf16[8,16,16,128]{3,2,1,0:T(8,128)(2,1)S(1)} async-done(((bf16[8,16,16,128]{3,2,1,0:T(8,128)(2,1)}), bf16[8,16,16,128]{3,2,1,0:T(8,128)(2,1)S(1)}, u32[]{:S(2)}, u32[]{:S(2)}) %all-to-all-start) | async-done | bytes 524320 | tf_op jit(solution)/shard_map/all_to_all | solution.py:362
  52.6 3.5 %all-to-all-start.1 = ((bf16[8,16,16,128]{3,2,1,0:T(8,128)(2,1)}), bf16[8,16,16,128]{3,2,1,0:T(8,128)(2,1)S(1)}, u32[]{:S(2)}, u32[]{:S(2)}) async-start(bf16[8,16,16,128]{3,2,1,0:T(8,128)(2,1)} %add_convert_fusion), calls=%async_computation.1 | async-start | bytes 1048576 | tf_op jit(solution)/shard_map/all_to_all | solution.py:362
  56.2 8.0 %all-to-all-done.1 = bf16[8,16,16,128]{3,2,1,0:T(8,128)(2,1)S(1)} async-done(((bf16[8,16,16,128]{3,2,1,0:T(8,128)(2,1)}), bf16[8,16,16,128]{3,2,1,0:T(8,128)(2,1)S(1)}, u32[]{:S(2)}, u32[]{:S(2)}) %all-to-all-start.1) | async-done | bytes 524320 | tf_op jit(solution)/shard_map/all_to_all | solution.py:362
  65.0 3.7 %all-to-all-start.2 = ((bf16[8,4,16,128]{3,2,1,0:T(8,128)(2,1)}), bf16[8,4,16,128]{3,2,1,0:T(8,128)(2,1)S(1)}, u32[]{:S(2)}, u32[]{:S(2)}) async-start(bf16[8,4,16,128]{3,2,1,0:T(8,128)(2,1)} %bitcast.8), calls=%async_computation.2 | async-start | bytes 262144 | tf_op jit(solution)/shard_map/all_to_all | solution.py:362
  68.7 5.8 %collective-permute-start.5 = (bf16[144,512]{1,0:T(8,128)(2,1)S(1)}, bf16[144,512]{1,0:T(8,128)(2,1)S(1)}, u32[]{:S(2)}, u32[]{:S(2)}) collective-permute-start(bf16[144,512]{1,0:T(8,128)(2,1)S(1)} %get-tuple-element.53), channel_id=1, source_target_pairs={{8,0},{505,1},{10,2},{507,3},{12,4},{509,5},{14,6},{511,7},{16,8},... | collective-permute-start | bytes 442376 | tf_op jit(solution)/shard_map/ppermute | solution.py:47
  74.5 3.6 %all-to-all-done.2 = bf16[8,4,16,128]{3,2,1,0:T(8,128)(2,1)S(1)} async-done(((bf16[8,4,16,128]{3,2,1,0:T(8,128)(2,1)}), bf16[8,4,16,128]{3,2,1,0:T(8,128)(2,1)S(1)}, u32[]{:S(2)}, u32[]{:S(2)}) %all-to-all-start.2) | async-done | bytes 131104 | tf_op jit(solution)/shard_map/all_to_all | solution.py:362
  78.8 6.8 %all-to-all-start.3 = ((bf16[4,4,16,128]{3,2,1,0:T(8,128)(2,1)}), bf16[4,4,16,128]{3,2,1,0:T(8,128)(2,1)S(1)}, u32[]{:S(2)}, u32[]{:S(2)}) async-start(bf16[4,4,16,128]{3,2,1,0:T(8,128)(2,1)} %broadcast_in_dim.11), calls=%async_computation.3 | async-start | bytes 131072 | tf_op jit(solution)/shard_map/all_to_all | solution.py:362
  85.5 7.1 %all-to-all-done.3 = bf16[4,4,16,128]{3,2,1,0:T(8,128)(2,1)S(1)} async-done(((bf16[4,4,16,128]{3,2,1,0:T(8,128)(2,1)}), bf16[4,4,16,128]{3,2,1,0:T(8,128)(2,1)S(1)}, u32[]{:S(2)}, u32[]{:S(2)}) %all-to-all-start.3) | async-done | bytes 65568 | tf_op jit(solution)/shard_map/all_to_all | solution.py:362
  93.3 4.5 %all-to-all-start.4 = ((bf16[8,4,16,128]{3,2,1,0:T(8,128)(2,1)}), bf16[8,4,16,128]{3,2,1,0:T(8,128)(2,1)S(1)}, u32[]{:S(2)}, u32[]{:S(2)}) async-start(bf16[8,4,16,128]{3,2,1,0:T(8,128)(2,1)} %broadcast_in_dim.12), calls=%async_computation.4 | async-start | bytes 262144 | tf_op jit(solution)/shard_map/all_to_all | solution.py:362
  97.8 4.1 %collective-permute-start.6 = (bf16[144,512]{1,0:T(8,128)(2,1)S(1)}, bf16[144,512]{1,0:T(8,128)(2,1)S(1)}, u32[]{:S(2)}, u32[]{:S(2)}) collective-permute-start(bf16[144,512]{1,0:T(8,128)(2,1)S(1)} %pad_maximum_fusion), channel_id=1, source_target_pairs={{1,0},{2,1},{3,2},{4,3},{5,4},{6,5},{7,6},{0,7},{9,8},{10,9},{11,1... | collective-permute-start | bytes 442376 | tf_op jit(solution)/shard_map/ppermute | solution.py:47
  102.0 2.1 %collective-permute-done.6.lat_both = bf16[144,512]{1,0:T(8,128)(2,1)S(1)} collective-permute-done((bf16[144,512]{1,0:T(8,128)(2,1)S(1)}, bf16[144,512]{1,0:T(8,128)(2,1)S(1)}, u32[]{:S(2)}, u32[]{:S(2)}) %collective-permute-start.6) | collective-permute-done | bytes 147488 | tf_op jit(solution)/shard_map/ppermute | solution.py:47
  104.0 3.2 %all-to-all-done.4 = bf16[8,4,16,128]{3,2,1,0:T(8,128)(2,1)S(1)} async-done(((bf16[8,4,16,128]{3,2,1,0:T(8,128)(2,1)}), bf16[8,4,16,128]{3,2,1,0:T(8,128)(2,1)S(1)}, u32[]{:S(2)}, u32[]{:S(2)}) %all-to-all-start.4) | async-done | bytes 131104 | tf_op jit(solution)/shard_map/all_to_all | solution.py:362
  107.3 9.6 %all_to_all.35.refs_0_ = bf16[8,16,16,128]{3,2,1,0:T(8,128)(2,1)S(1)} all-to-all(bf16[8,16,16,128]{3,2,1,0:T(8,128)(2,1)S(1)} %broadcast_in_dim.13), channel_id=1, replica_groups={{0,2,1,3,64,66,65,67},{4,6,5,7,68,70,69,71},{16,18,17,19,80,82,81,83},{..., dimensions={0} | all-to-all | bytes 1048576 | tf_op jit(solution)/shard_map/all_to_all | solution.py:362
  117.8 3.5 %all-to-all-start.6 = ((bf16[8,16,16,128]{3,2,1,0:T(8,128)(2,1)}), bf16[8,16,16,128]{3,2,1,0:T(8,128)(2,1)S(1)}, u32[]{:S(2)}, u32[]{:S(2)}) async-start(bf16[8,16,16,128]{3,2,1,0:T(8,128)(2,1)} %broadcast_in_dim.14), calls=%async_computation.6 | async-start | bytes 1048576 | tf_op jit(solution)/shard_map/all_to_all | solution.py:362
  121.3 8.4 %collective-permute-start.7 = (bf16[8,16,16,128]{3,2,1,0:T(8,128)(2,1)S(1)}, bf16[8,16,16,128]{3,2,1,0:T(8,128)(2,1)S(1)}, u32[]{:S(2)}, u32[]{:S(2)}) collective-permute-start(bf16[8,16,16,128]{3,2,1,0:T(8,128)(2,1)S(1)} %all_to_all.35.refs_0_), channel_id=1, source_target_pairs={{0,8},{2,10},{4,12},{6,14},{1,9},{3,11},{5,13},{7,15},{16,24},{18,... | collective-permute-start | bytes 1572872 | tf_op jit(solution)/shard_map/ppermute | solution.py:358
  129.7 8.3 %collective-permute-start.8 = (bf16[8,16,16,128]{3,2,1,0:T(8,128)(2,1)S(1)}, bf16[8,16,16,128]{3,2,1,0:T(8,128)(2,1)S(1)}, u32[]{:S(2)}, u32[]{:S(2)}) collective-permute-start(bf16[8,16,16,128]{3,2,1,0:T(8,128)(2,1)S(1)} %all-to-all-done.6.refs_1_), channel_id=1, source_target_pairs={{0,8},{2,10},{4,12},{6,14},{1,9},{3,11},{5,13},{7,15},{16,24},{18,... | collective-permute-start | bytes 1572872 | tf_op jit(solution)/shard_map/ppermute | solution.py:358
  (38 shorter events, 18.4 us)
Async XLA Ops:
  0.7 1.0 copy-start.1
  1.7 1.0 copy-start.4
  3.6 13.3 %collective-permute-start = (bf16[144,512]{1,0:T(8,128)(2,1)S(1)}, bf16[144,512]{1,0:T(8,128)(2,1)S(1)}, u32[]{:S(2)}, u32[]{:S(2)}) collective-permute-start(bf16[144,512]{1,0:T(8,128)(2,1)S(1)} %get-tuple-element.40), channel_id=1, source_target_pairs={{0,505},{1,10},{2,507},{3,12},{4,509},{5,14},{6,511},{7,8},{8,1},{... | collective-permute-start | bytes 442376 | tf_op jit(solution)/shard_map/ppermute | solution.py:47
  8.2 13.0 %collective-permute-start.1 = (bf16[144,512]{1,0:T(8,128)(2,1)S(1)}, bf16[144,512]{1,0:T(8,128)(2,1)S(1)}, u32[]{:S(2)}, u32[]{:S(2)}) collective-permute-start(bf16[144,512]{1,0:T(8,128)(2,1)S(1)} %get-tuple-element.41), channel_id=1, source_target_pairs={{0,8},{1,505},{2,10},{3,507},{4,12},{5,509},{6,14},{7,511},{8,16},... | collective-permute-start | bytes 442376 | tf_op jit(solution)/shard_map/ppermute | solution.py:47
  11.1 10.0 %collective-permute-start.2 = (bf16[144,512]{1,0:T(8,128)(2,1)S(1)}, bf16[144,512]{1,0:T(8,128)(2,1)S(1)}, u32[]{:S(2)}, u32[]{:S(2)}) collective-permute-start(bf16[144,512]{1,0:T(8,128)(2,1)S(1)} %get-tuple-element.42), channel_id=1, source_target_pairs={{0,1},{1,2},{2,3},{3,4},{4,5},{5,6},{6,7},{7,0},{8,9},{9,10},{10,1... | collective-permute-start | bytes 442376 | tf_op jit(solution)/shard_map/ppermute | solution.py:47
  14.2 1.4 copy-start
  15.6 1.0 copy-start.3
  27.3 11.7 %collective-permute-start.3 = (bf16[8,16,16,128]{3,2,1,0:T(8,128)(2,1)S(1)}, bf16[8,16,16,128]{3,2,1,0:T(8,128)(2,1)S(1)}, u32[]{:S(2)}, u32[]{:S(2)}) collective-permute-start(bf16[8,16,16,128]{3,2,1,0:T(8,128)(2,1)S(1)} %get-tuple-element.48), channel_id=1, source_target_pairs={{0,8},{2,10},{4,12},{6,14},{1,9},{3,11},{5,13},{7,15},{16,24},{18,... | collective-permute-start | bytes 1572872 | tf_op jit(solution)/shard_map/ppermute | solution.py:358
  39.9 12.7 %all-to-all-start = ((bf16[8,16,16,128]{3,2,1,0:T(8,128)(2,1)}), bf16[8,16,16,128]{3,2,1,0:T(8,128)(2,1)S(1)}, u32[]{:S(2)}, u32[]{:S(2)}) async-start(bf16[8,16,16,128]{3,2,1,0:T(8,128)(2,1)} %add_convert_fusion.1), calls=%async_computation | async-start | bytes 1048576 | tf_op jit(solution)/shard_map/all_to_all | solution.py:362
  43.4 3.8 %collective-permute-start.4 = (bf16[8,16,16,128]{3,2,1,0:T(8,128)(2,1)S(1)}, bf16[8,16,16,128]{3,2,1,0:T(8,128)(2,1)S(1)}, u32[]{:S(2)}, u32[]{:S(2)}) collective-permute-start(bf16[8,16,16,128]{3,2,1,0:T(8,128)(2,1)S(1)} %get-tuple-element.50), channel_id=1, source_target_pairs={{0,8},{2,10},{4,12},{6,14},{1,9},{3,11},{5,13},{7,15},{16,24},{18,... | collective-permute-start | bytes 1572872 | tf_op jit(solution)/shard_map/ppermute | solution.py:358
  52.6 11.6 %all-to-all-start.1 = ((bf16[8,16,16,128]{3,2,1,0:T(8,128)(2,1)}), bf16[8,16,16,128]{3,2,1,0:T(8,128)(2,1)S(1)}, u32[]{:S(2)}, u32[]{:S(2)}) async-start(bf16[8,16,16,128]{3,2,1,0:T(8,128)(2,1)} %add_convert_fusion), calls=%async_computation.1 | async-start | bytes 1048576 | tf_op jit(solution)/shard_map/all_to_all | solution.py:362
  65.0 13.1 %all-to-all-start.2 = ((bf16[8,4,16,128]{3,2,1,0:T(8,128)(2,1)}), bf16[8,4,16,128]{3,2,1,0:T(8,128)(2,1)S(1)}, u32[]{:S(2)}, u32[]{:S(2)}) async-start(bf16[8,4,16,128]{3,2,1,0:T(8,128)(2,1)} %bitcast.8), calls=%async_computation.2 | async-start | bytes 262144 | tf_op jit(solution)/shard_map/all_to_all | solution.py:362
  68.7 16.8 %collective-permute-start.5 = (bf16[144,512]{1,0:T(8,128)(2,1)S(1)}, bf16[144,512]{1,0:T(8,128)(2,1)S(1)}, u32[]{:S(2)}, u32[]{:S(2)}) collective-permute-start(bf16[144,512]{1,0:T(8,128)(2,1)S(1)} %get-tuple-element.53), channel_id=1, source_target_pairs={{8,0},{505,1},{10,2},{507,3},{12,4},{509,5},{14,6},{511,7},{16,8},... | collective-permute-start | bytes 442376 | tf_op jit(solution)/shard_map/ppermute | solution.py:47
  78.8 13.8 %all-to-all-start.3 = ((bf16[4,4,16,128]{3,2,1,0:T(8,128)(2,1)}), bf16[4,4,16,128]{3,2,1,0:T(8,128)(2,1)S(1)}, u32[]{:S(2)}, u32[]{:S(2)}) async-start(bf16[4,4,16,128]{3,2,1,0:T(8,128)(2,1)} %broadcast_in_dim.11), calls=%async_computation.3 | async-start | bytes 131072 | tf_op jit(solution)/shard_map/all_to_all | solution.py:362
  93.3 13.9 %all-to-all-start.4 = ((bf16[8,4,16,128]{3,2,1,0:T(8,128)(2,1)}), bf16[8,4,16,128]{3,2,1,0:T(8,128)(2,1)S(1)}, u32[]{:S(2)}, u32[]{:S(2)}) async-start(bf16[8,4,16,128]{3,2,1,0:T(8,128)(2,1)} %broadcast_in_dim.12), calls=%async_computation.4 | async-start | bytes 262144 | tf_op jit(solution)/shard_map/all_to_all | solution.py:362
  97.8 6.2 %collective-permute-start.6 = (bf16[144,512]{1,0:T(8,128)(2,1)S(1)}, bf16[144,512]{1,0:T(8,128)(2,1)S(1)}, u32[]{:S(2)}, u32[]{:S(2)}) collective-permute-start(bf16[144,512]{1,0:T(8,128)(2,1)S(1)} %pad_maximum_fusion), channel_id=1, source_target_pairs={{1,0},{2,1},{3,2},{4,3},{5,4},{6,5},{7,6},{0,7},{9,8},{10,9},{11,1... | collective-permute-start | bytes 442376 | tf_op jit(solution)/shard_map/ppermute | solution.py:47
  107.2 30.8 %copy-start.2 = (bf16[4,6,12,512]{3,0,2,1:T(4,128)(2,1)S(1)}, bf16[4,6,12,512]{3,0,2,1:T(4,128)(2,1)}, u32[]{:S(2)}) copy-start(bf16[4,6,12,512]{3,0,2,1:T(4,128)(2,1)} %param.5) | copy-start | bytes 884740
  117.8 11.9 %all-to-all-start.6 = ((bf16[8,16,16,128]{3,2,1,0:T(8,128)(2,1)}), bf16[8,16,16,128]{3,2,1,0:T(8,128)(2,1)S(1)}, u32[]{:S(2)}, u32[]{:S(2)}) async-start(bf16[8,16,16,128]{3,2,1,0:T(8,128)(2,1)} %broadcast_in_dim.14), calls=%async_computation.6 | async-start | bytes 1048576 | tf_op jit(solution)/shard_map/all_to_all | solution.py:362
  121.3 19.9 %collective-permute-start.7 = (bf16[8,16,16,128]{3,2,1,0:T(8,128)(2,1)S(1)}, bf16[8,16,16,128]{3,2,1,0:T(8,128)(2,1)S(1)}, u32[]{:S(2)}, u32[]{:S(2)}) collective-permute-start(bf16[8,16,16,128]{3,2,1,0:T(8,128)(2,1)S(1)} %all_to_all.35.refs_0_), channel_id=1, source_target_pairs={{0,8},{2,10},{4,12},{6,14},{1,9},{3,11},{5,13},{7,15},{16,24},{18,... | collective-permute-start | bytes 1572872 | tf_op jit(solution)/shard_map/ppermute | solution.py:358
  129.7 11.5 %collective-permute-start.8 = (bf16[8,16,16,128]{3,2,1,0:T(8,128)(2,1)S(1)}, bf16[8,16,16,128]{3,2,1,0:T(8,128)(2,1)S(1)}, u32[]{:S(2)}, u32[]{:S(2)}) collective-permute-start(bf16[8,16,16,128]{3,2,1,0:T(8,128)(2,1)S(1)} %all-to-all-done.6.refs_1_), channel_id=1, source_target_pairs={{0,8},{2,10},{4,12},{6,14},{1,9},{3,11},{5,13},{7,15},{16,24},{18,... | collective-permute-start | bytes 1572872 | tf_op jit(solution)/shard_map/ppermute | solution.py:358

commit v7 on v5

--- a/solution.py
+++ b/solution.py
@@ -177,7 +177,8 @@
 def block_kernel(place, *refs):
     quarters, (qkv_weight, proj_weight), (theirs, mine, own, lat, lon_both) = refs[:4], refs[4:6], refs[6:11]
     x_held, cot_held, normed, attended, qkv_grad, qkv, upstream, tiles = refs[11:]
-    held = [ref[...].astype(jnp.float32) for ref in quarters]
+    own_ref, both_ref, lon_ref, lat_ref = quarters
+    held = [ref[...].astype(jnp.float32) for ref in (own_ref, lon_ref, lat_ref, both_ref)]
     for kind, target in enumerate((x_held, cot_held)):
         chunks = [
             held[quarter][(2 * kind + window) * QUARTER : (2 * kind + window + 1) * QUARTER]
@@ -424,17 +425,17 @@
     own, qkv_weight, proj_weight = lax.optimization_barrier((own, qkv_weight, proj_weight))
     both, lon, lat = moved(both, 3, False), moved(lon, 1, False), moved(lat, 2, False)
     qkv_weight, proj_weight = near_weights(qkv_weight, proj_weight)
-    theirs, mine, own, lat, lon_both = block(place, (own, lon, lat, both), qkv_weight, proj_weight)
+    theirs, mine, own, lat, lon_both = block(place, (own, both, lon, lat), qkv_weight, proj_weight)
 
     near, middle, far = cube_groups(1), middle_groups(), far_groups()
     tiles = (mine.astype(jnp.float32) + swapped(theirs).astype(jnp.float32)).astype(jnp.bfloat16)
     tiles = scattered_sum(tiles.reshape(-1, 16, 128), near)
     tiles, lon_both = lax.optimization_barrier((tiles, lon_both))
-    tiles = scattered_sum(tiles, middle)
+    tiles, lon_both = lax.optimization_barrier((scattered_sum(tiles, middle), moved(lon_both, 1, True)))
+    lat_both = jnp.concatenate([lat, lon_both[2 * QUARTER :]], axis=0)
+    tiles, lat_both = lax.optimization_barrier((tiles, lat_both))
     factor = (LEVELS * ROWS * COLS * lax.axis_size(ALL)) ** (-0.5)
-    tiles, lon_both = lax.optimization_barrier((exchanged(tiles, far), moved(lon_both, 1, True)))
-    tiles = (added(tiles) * factor).astype(jnp.bfloat16)
-    lat_both = jnp.concatenate([lat, lon_both[2 * QUARTER :]], axis=0)
+    tiles = (added(exchanged(tiles, far)) * factor).astype(jnp.bfloat16)
     tiles, lat_both = lax.optimization_barrier((tiles, lat_both))
     tiles, lat_both = lax.optimization_barrier((gathered(tiles, middle), moved(lat_both, 2, True)))
     input_grad = unpack(place, cotangent, own, lon_both, lat_both)

time: 128 us -> 130 us (1.016)
  blocking collectives: 17.3 us -> 30.8 us
  starting transfers between devices: 58.4 us -> 51.1 us
  waiting for transfers between devices: 31 us -> 27.1 us
    all_to_all x1 -> x2, blocking collectives: 17.3 us -> 30.8 us  [all_to_all(): return lax.all_to_all(split, ALL, 0, 0, axis_index_groups=groups)]
    ppermute x5, starting transfers between devices: 29.5 us -> 18.4 us  [moved(): return lax.ppermute(value, ALL, pairs)]
    all_to_all x4 -> x3, waiting for transfers between devices: 23.7 us -> 16.9 us  [all_to_all(): return lax.all_to_all(split, ALL, 0, 0, axis_index_groups=groups)]
    ppermute x2, starting transfers between devices: 13.7 us -> 17.9 us  [swapped(): return lax.ppermute(value, ALL, [*zip(first, second), *zip(second, first)])]
    ppermute x5, waiting for transfers between devices: 4.45 us -> 7.35 us  [moved(): return lax.ppermute(value, ALL, pairs)]
    all_to_all x4 -> x3, starting transfers between devices: 15.2 us -> 14.8 us  [all_to_all(): return lax.all_to_all(split, ALL, 0, 0, axis_index_groups=groups)]
  transfers between devices with their start and end apart: 11 -> 10, of which waited for: 8 -> 7; matrix products, arithmetic and copies ran while one was open for 1% -> 0% of each run, Pallas kernels for 3% -> 3%
where the time goes in v7:
time: 130 us; the launch traced here: 129 us
  starting transfers between devices  51.1 us (39%)
  blocking collectives  30.8 us (24%)
  waiting for transfers between devices  27.1 us (21%)
  Pallas kernels  12 us (9%)
  local copies, waits for them, and re-layouts  6.17 us (5%)
    all_to_all x2, blocking collectives, all_to_all(): return lax.all_to_all(split, ALL, 0, 0, axis_index_groups=groups)  30.8 us
    ppermute x5, starting transfers between devices, moved(): return lax.ppermute(value, ALL, pairs)  18.4 us
    ppermute x2, starting transfers between devices, swapped(): return lax.ppermute(value, ALL, [*zip(first, second), *zip(second, first)])  17.9 us
    all_to_all x3, waiting for transfers between devices, all_to_all(): return lax.all_to_all(split, ALL, 0, 0, axis_index_groups=groups)  16.9 us
    all_to_all x3, starting transfers between devices, all_to_all(): return lax.all_to_all(split, ALL, 0, 0, axis_index_groups=groups)  14.8 us
    ppermute x5, waiting for transfers between devices, moved(): return lax.ppermute(value, ALL, pairs)  7.35 us
    pallas_call x1, Pallas kernels, block(): pl.pallas_call(block_kernel, out_shape=(HALF_TILES, HALF_TILES, rows_of(2...  6.12 us
    unnamed x10, local copies, waits for them, and re-layouts  4.37 us
  transfers between devices with their start and end apart: 10, of which 7 were waited for; matrix products, arithmetic and copies ran while one was open for 0% of the time, Pallas kernels for 3%

profile of v7, /device:TPU:1, one launch (start us, length us, event | category | flops | bytes accessed | tf_op | source)
XLA Modules:
  0.0 129.2 jit_solution(7778891780998782635)
XLA Ops:
  3.6 4.6 %collective-permute-start = (bf16[144,512]{1,0:T(8,128)(2,1)S(1)}, bf16[144,512]{1,0:T(8,128)(2,1)S(1)}, u32[]{:S(2)}, u32[]{:S(2)}) collective-permute-start(bf16[144,512]{1,0:T(8,128)(2,1)S(1)} %get-tuple-element.38), channel_id=1, source_target_pairs={{0,505},{1,10},{2,507},{3,12},{4,509},{5,14},{6,511},{7,8},{8,1},{... | collective-permute-start | bytes 442376 | tf_op jit(solution)/shard_map/ppermute | solution.py:47
  8.2 2.9 %collective-permute-start.1 = (bf16[144,512]{1,0:T(8,128)(2,1)S(1)}, bf16[144,512]{1,0:T(8,128)(2,1)S(1)}, u32[]{:S(2)}, u32[]{:S(2)}) collective-permute-start(bf16[144,512]{1,0:T(8,128)(2,1)S(1)} %get-tuple-element.39), channel_id=1, source_target_pairs={{0,8},{1,505},{2,10},{3,507},{4,12},{5,509},{6,14},{7,511},{8,16},... | collective-permute-start | bytes 442376 | tf_op jit(solution)/shard_map/ppermute | solution.py:47
  11.1 3.1 %collective-permute-start.2 = (bf16[144,512]{1,0:T(8,128)(2,1)S(1)}, bf16[144,512]{1,0:T(8,128)(2,1)S(1)}, u32[]{:S(2)}, u32[]{:S(2)}) collective-permute-start(bf16[144,512]{1,0:T(8,128)(2,1)S(1)} %get-tuple-element.40), channel_id=1, source_target_pairs={{0,1},{1,2},{2,3},{3,4},{4,5},{5,6},{6,7},{7,0},{8,9},{9,10},{10,1... | collective-permute-start | bytes 442376 | tf_op jit(solution)/shard_map/ppermute | solution.py:47
  14.2 1.4 %copy-done = bf16[512,1536]{1,0:T(8,128)(2,1)S(1)} copy-done((bf16[512,1536]{1,0:T(8,128)(2,1)S(1)}, bf16[512,1536]{1,0:T(8,128)(2,1)}, u32[]{:S(2)}) %copy-start) | copy-done | bytes 1572888
  16.9 4.3 %collective-permute-done.1.refs_2_ = bf16[144,512]{1,0:T(8,128)(2,1)S(1)} collective-permute-done((bf16[144,512]{1,0:T(8,128)(2,1)S(1)}, bf16[144,512]{1,0:T(8,128)(2,1)S(1)}, u32[]{:S(2)}, u32[]{:S(2)}) %collective-permute-start.1) | collective-permute-done | bytes 147488 | tf_op jit(solution)/shard_map/ppermute | solution.py:47
  21.1 6.1 %block.1 = (bf16[16,16,16,128]{3,2,1,0:T(8,128)(2,1)S(1)}, bf16[16,16,16,128]{3,2,1,0:T(8,128)(2,1)S(1)}, bf16[72,512]{1,0:T(8,128)(2,1)S(1)}, bf16[72,512]{1,0:T(8,128)(2,1)S(1)}, bf16[144,512]{1,0:T(8,128)(2,1)S(1)}) custom-call(s32[4]{0:T(128)S(1)} %add_convert_fusion.3.place, bf16[144,512]{1,0:T(8,128)(2,1)S(1)} %get-tuple-element.37.refs_0_, ...), custom_call_target="tpu_custom_call" | custom-call | flops 2000000000 | bytes 6000000 | tf_op jit(solution)/shard_map/block/pallas_call | solution.py:274
  27.3 10.2 %collective-permute-start.3 = (bf16[16,16,16,128]{3,2,1,0:T(8,128)(2,1)S(1)}, bf16[16,16,16,128]{3,2,1,0:T(8,128)(2,1)S(1)}, u32[]{:S(2)}, u32[]{:S(2)}) collective-permute-start(bf16[16,16,16,128]{3,2,1,0:T(8,128)(2,1)S(1)} %get-tuple-element.46), channel_id=1, source_target_pairs={{0,8},{2,10},{4,12},{6,14},{1,9},{3,11},{5,13},{7,15},{16,24},{18,... | collective-permute-start | bytes 3145736 | tf_op jit(solution)/shard_map/ppermute | solution.py:356
  37.5 2.3 %collective-permute-done.3 = bf16[16,16,16,128]{3,2,1,0:T(8,128)(2,1)S(1)} collective-permute-done((bf16[16,16,16,128]{3,2,1,0:T(8,128)(2,1)S(1)}, bf16[16,16,16,128]{3,2,1,0:T(8,128)(2,1)S(1)}, u32[]{:S(2)}, u32[]{:S(2)}) %collective-permute-start.3) | collective-permute-done | bytes 1048608 | tf_op jit(solution)/shard_map/ppermute | solution.py:356
  40.0 17.3 %all_to_all.25 = bf16[8,32,16,128]{3,2,1,0:T(8,128)(2,1)S(1)} all-to-all(bf16[8,32,16,128]{3,2,1,0:T(8,128)(2,1)S(1)} %bitcast.23), channel_id=1, replica_groups={{0,2,1,3,64,66,65,67},{4,6,5,7,68,70,69,71},{16,18,17,19,80,82,81,83},{..., dimensions={0} | all-to-all | bytes 2097152 | tf_op jit(solution)/shard_map/all_to_all | solution.py:360
  58.1 3.9 %all-to-all-start.1 = ((bf16[8,4,16,128]{3,2,1,0:T(8,128)(2,1)}), bf16[8,4,16,128]{3,2,1,0:T(8,128)(2,1)S(1)}, u32[]{:S(2)}, u32[]{:S(2)}) async-start(bf16[8,4,16,128]{3,2,1,0:T(8,128)(2,1)} %bitcast.8), calls=%async_computation.1 | async-start | bytes 262144 | tf_op jit(solution)/shard_map/all_to_all | solution.py:360
  62.0 4.7 %collective-permute-start.4 = (bf16[144,512]{1,0:T(8,128)(2,1)S(1)}, bf16[144,512]{1,0:T(8,128)(2,1)S(1)}, u32[]{:S(2)}, u32[]{:S(2)}) collective-permute-start(bf16[144,512]{1,0:T(8,128)(2,1)S(1)} %get-tuple-element.49), channel_id=1, source_target_pairs={{8,0},{505,1},{10,2},{507,3},{12,4},{509,5},{14,6},{511,7},{16,8},... | collective-permute-start | bytes 442376 | tf_op jit(solution)/shard_map/ppermute | solution.py:47
  66.7 4.6 %all-to-all-done.1 = bf16[8,4,16,128]{3,2,1,0:T(8,128)(2,1)S(1)} async-done(((bf16[8,4,16,128]{3,2,1,0:T(8,128)(2,1)}), bf16[8,4,16,128]{3,2,1,0:T(8,128)(2,1)S(1)}, u32[]{:S(2)}, u32[]{:S(2)}) %all-to-all-start.1) | async-done | bytes 131104 | tf_op jit(solution)/shard_map/all_to_all | solution.py:360
  71.4 13.6 %all_to_all.26 = bf16[4,4,16,128]{3,2,1,0:T(8,128)(2,1)S(1)} all-to-all(bf16[4,4,16,128]{3,2,1,0:T(8,128)(2,1)S(1)} %broadcast_in_dim.6), channel_id=1, replica_groups={{0,16,32,48},{2,18,34,50},{4,20,36,52},{6,22,38,54},{64,80,96,112},{66,..., dimensions={0} | all-to-all | bytes 131072 | tf_op jit(solution)/shard_map/all_to_all | solution.py:360
  85.7 7.3 %all-to-all-start.3 = ((bf16[8,4,16,128]{3,2,1,0:T(8,128)(2,1)}), bf16[8,4,16,128]{3,2,1,0:T(8,128)(2,1)S(1)}, u32[]{:S(2)}, u32[]{:S(2)}) async-start(bf16[8,4,16,128]{3,2,1,0:T(8,128)(2,1)} %broadcast_in_dim.7), calls=%async_computation.3 | async-start | bytes 262144 | tf_op jit(solution)/shard_map/all_to_all | solution.py:360
  93.0 3.1 %collective-permute-start.5 = (bf16[144,512]{1,0:T(8,128)(2,1)S(1)}, bf16[144,512]{1,0:T(8,128)(2,1)S(1)}, u32[]{:S(2)}, u32[]{:S(2)}) collective-permute-start(bf16[144,512]{1,0:T(8,128)(2,1)S(1)} %pad_maximum_fusion), channel_id=1, source_target_pairs={{1,0},{2,1},{3,2},{4,3},{5,4},{6,5},{7,6},{0,7},{9,8},{10,9},{11,1... | collective-permute-start | bytes 442376 | tf_op jit(solution)/shard_map/ppermute | solution.py:47
  96.1 3.1 %collective-permute-done.5.lat_both = bf16[144,512]{1,0:T(8,128)(2,1)S(1)} collective-permute-done((bf16[144,512]{1,0:T(8,128)(2,1)S(1)}, bf16[144,512]{1,0:T(8,128)(2,1)S(1)}, u32[]{:S(2)}, u32[]{:S(2)}) %collective-permute-start.5) | collective-permute-done | bytes 147488 | tf_op jit(solution)/shard_map/ppermute | solution.py:47
  99.2 3.2 %all-to-all-done.3 = bf16[8,4,16,128]{3,2,1,0:T(8,128)(2,1)S(1)} async-done(((bf16[8,4,16,128]{3,2,1,0:T(8,128)(2,1)}), bf16[8,4,16,128]{3,2,1,0:T(8,128)(2,1)S(1)}, u32[]{:S(2)}, u32[]{:S(2)}) %all-to-all-start.3) | async-done | bytes 131104 | tf_op jit(solution)/shard_map/all_to_all | solution.py:360
  102.4 1.1 broadcast_in_dim.8
  103.5 3.6 %all-to-all-start.4 = ((bf16[8,32,16,128]{3,2,1,0:T(8,128)(2,1)}), bf16[8,32,16,128]{3,2,1,0:T(8,128)(2,1)S(1)}, u32[]{:S(2)}, u32[]{:S(2)}) async-start(bf16[8,32,16,128]{3,2,1,0:T(8,128)(2,1)} %broadcast_in_dim.8), calls=%async_computation.4 | async-start | bytes 2097152 | tf_op jit(solution)/shard_map/all_to_all | solution.py:360
  107.1 1.6 %unpack.1 = bf16[6,12,4,512]{3,2,1,0:T(4,128)(2,1)} custom-call(s32[4]{0:T(128)S(1)} %add_convert_fusion.3.place, bf16[72,512]{1,0:T(8,128)(2,1)S(1)} %get-tuple-element.58.own, bf16[144,512]{1,0:T(8,128)(2,1)S(1)} %collective-permute-done.4.lon_ref, bf16[144,512]{1,0:T(8,128)(2,1)S(1)} %collective-permute-done.5.lat_both, bf16[6,12,4,512]{3,2,1,0:T(4,128)(2,1)S(1)} %bitcast.21), custom_call_target="tpu_custom_call" | custom-call | bytes 900000 | tf_op jit(solution)/shard_map/unpack/pallas_call | solution.py:142
  108.7 9.0 %all-to-all-done.4 = bf16[8,32,16,128]{3,2,1,0:T(8,128)(2,1)S(1)} async-done(((bf16[8,32,16,128]{3,2,1,0:T(8,128)(2,1)}), bf16[8,32,16,128]{3,2,1,0:T(8,128)(2,1)S(1)}, u32[]{:S(2)}, u32[]{:S(2)}) %all-to-all-start.4) | async-done | bytes 1048608 | tf_op jit(solution)/shard_map/all_to_all | solution.py:360
  117.7 7.6 %collective-permute-start.6 = (bf16[16,16,16,128]{3,2,1,0:T(8,128)(2,1)S(1)}, bf16[16,16,16,128]{3,2,1,0:T(8,128)(2,1)S(1)}, u32[]{:S(2)}, u32[]{:S(2)}) collective-permute-start(bf16[16,16,16,128]{3,2,1,0:T(8,128)(2,1)S(1)} %bitcast.18), channel_id=1, source_target_pairs={{0,8},{2,10},{4,12},{6,14},{1,9},{3,11},{5,13},{7,15},{16,24},{18,... | collective-permute-start | bytes 3145736 | tf_op jit(solution)/shard_map/ppermute | solution.py:356
  125.3 1.6 %untile_own.1 = (bf16[512,1536]{1,0:T(8,128)(2,1)}, bf16[512,512]{1,0:T(8,128)(2,1)}) custom-call(s32[4]{0:T(128)S(1)} %add_convert_fusion.3.place, bf16[16,16,16,128]{3,2,1,0:T(8,128)(2,1)S(1)} %bitcast.19), custom_call_target="tpu_custom_call" | custom-call | bytes 2097152 | tf_op jit(solution)/shard_map/untile_own/pallas_call | solution.py:402
  127.6 1.6 %untile_other.1 = (bf16[512,1536]{1,0:T(8,128)(2,1)}, bf16[512,512]{1,0:T(8,128)(2,1)}) custom-call(s32[4]{0:T(128)S(1)} %add_convert_fusion.3.place, bf16[16,16,16,128]{3,2,1,0:T(8,128)(2,1)S(1)} %collective-permute-done.6.tiles, bf16[512,1536]{1,0:T(8,128)(2,1)} %get-tuple-element.65.refs_0_, ...), custom_call_target="tpu_custom_call", output_to_operand_aliasing={{0}: (2, {}), {1}: (3, {})} | custom-call | bytes 2097152 | tf_op jit(solution)/shard_map/untile_other/pallas_call | solution.py:402
  (24 shorter events, 6.6 us)
Async XLA Ops:
  0.7 1.0 copy-start.1
  1.7 1.0 copy-start.4
  3.6 13.3 %collective-permute-start = (bf16[144,512]{1,0:T(8,128)(2,1)S(1)}, bf16[144,512]{1,0:T(8,128)(2,1)S(1)}, u32[]{:S(2)}, u32[]{:S(2)}) collective-permute-start(bf16[144,512]{1,0:T(8,128)(2,1)S(1)} %get-tuple-element.38), channel_id=1, source_target_pairs={{0,505},{1,10},{2,507},{3,12},{4,509},{5,14},{6,511},{7,8},{8,1},{... | collective-permute-start | bytes 442376 | tf_op jit(solution)/shard_map/ppermute | solution.py:47
  8.2 13.0 %collective-permute-start.1 = (bf16[144,512]{1,0:T(8,128)(2,1)S(1)}, bf16[144,512]{1,0:T(8,128)(2,1)S(1)}, u32[]{:S(2)}, u32[]{:S(2)}) collective-permute-start(bf16[144,512]{1,0:T(8,128)(2,1)S(1)} %get-tuple-element.39), channel_id=1, source_target_pairs={{0,8},{1,505},{2,10},{3,507},{4,12},{5,509},{6,14},{7,511},{8,16},... | collective-permute-start | bytes 442376 | tf_op jit(solution)/shard_map/ppermute | solution.py:47
  11.1 10.0 %collective-permute-start.2 = (bf16[144,512]{1,0:T(8,128)(2,1)S(1)}, bf16[144,512]{1,0:T(8,128)(2,1)S(1)}, u32[]{:S(2)}, u32[]{:S(2)}) collective-permute-start(bf16[144,512]{1,0:T(8,128)(2,1)S(1)} %get-tuple-element.40), channel_id=1, source_target_pairs={{0,1},{1,2},{2,3},{3,4},{4,5},{5,6},{6,7},{7,0},{8,9},{9,10},{10,1... | collective-permute-start | bytes 442376 | tf_op jit(solution)/shard_map/ppermute | solution.py:47
  14.2 1.4 %copy-start = (bf16[512,1536]{1,0:T(8,128)(2,1)S(1)}, bf16[512,1536]{1,0:T(8,128)(2,1)}, u32[]{:S(2)}) copy-start(bf16[512,1536]{1,0:T(8,128)(2,1)} %qkv_weight) | copy-start | bytes 4718596
  15.6 1.0 copy-start.3
  27.3 12.5 %collective-permute-start.3 = (bf16[16,16,16,128]{3,2,1,0:T(8,128)(2,1)S(1)}, bf16[16,16,16,128]{3,2,1,0:T(8,128)(2,1)S(1)}, u32[]{:S(2)}, u32[]{:S(2)}) collective-permute-start(bf16[16,16,16,128]{3,2,1,0:T(8,128)(2,1)S(1)} %get-tuple-element.46), channel_id=1, source_target_pairs={{0,8},{2,10},{4,12},{6,14},{1,9},{3,11},{5,13},{7,15},{16,24},{18,... | collective-permute-start | bytes 3145736 | tf_op jit(solution)/shard_map/ppermute | solution.py:356
  58.1 13.2 %all-to-all-start.1 = ((bf16[8,4,16,128]{3,2,1,0:T(8,128)(2,1)}), bf16[8,4,16,128]{3,2,1,0:T(8,128)(2,1)S(1)}, u32[]{:S(2)}, u32[]{:S(2)}) async-start(bf16[8,4,16,128]{3,2,1,0:T(8,128)(2,1)} %bitcast.8), calls=%async_computation.1 | async-start | bytes 262144 | tf_op jit(solution)/shard_map/all_to_all | solution.py:360
  62.0 9.3 %collective-permute-start.4 = (bf16[144,512]{1,0:T(8,128)(2,1)S(1)}, bf16[144,512]{1,0:T(8,128)(2,1)S(1)}, u32[]{:S(2)}, u32[]{:S(2)}) collective-permute-start(bf16[144,512]{1,0:T(8,128)(2,1)S(1)} %get-tuple-element.49), channel_id=1, source_target_pairs={{8,0},{505,1},{10,2},{507,3},{12,4},{509,5},{14,6},{511,7},{16,8},... | collective-permute-start | bytes 442376 | tf_op jit(solution)/shard_map/ppermute | solution.py:47
  85.7 16.7 %all-to-all-start.3 = ((bf16[8,4,16,128]{3,2,1,0:T(8,128)(2,1)}), bf16[8,4,16,128]{3,2,1,0:T(8,128)(2,1)S(1)}, u32[]{:S(2)}, u32[]{:S(2)}) async-start(bf16[8,4,16,128]{3,2,1,0:T(8,128)(2,1)} %broadcast_in_dim.7), calls=%async_computation.3 | async-start | bytes 262144 | tf_op jit(solution)/shard_map/all_to_all | solution.py:360
  93.0 6.2 %collective-permute-start.5 = (bf16[144,512]{1,0:T(8,128)(2,1)S(1)}, bf16[144,512]{1,0:T(8,128)(2,1)S(1)}, u32[]{:S(2)}, u32[]{:S(2)}) collective-permute-start(bf16[144,512]{1,0:T(8,128)(2,1)S(1)} %pad_maximum_fusion), channel_id=1, source_target_pairs={{1,0},{2,1},{3,2},{4,3},{5,4},{6,5},{7,6},{0,7},{9,8},{10,9},{11,1... | collective-permute-start | bytes 442376 | tf_op jit(solution)/shard_map/ppermute | solution.py:47
  102.4 4.7 %copy-start.2 = (bf16[4,6,12,512]{3,0,2,1:T(4,128)(2,1)S(1)}, bf16[4,6,12,512]{3,0,2,1:T(4,128)(2,1)}, u32[]{:S(2)}) copy-start(bf16[4,6,12,512]{3,0,2,1:T(4,128)(2,1)} %param.5) | copy-start | bytes 884740
  103.5 14.2 %all-to-all-start.4 = ((bf16[8,32,16,128]{3,2,1,0:T(8,128)(2,1)}), bf16[8,32,16,128]{3,2,1,0:T(8,128)(2,1)S(1)}, u32[]{:S(2)}, u32[]{:S(2)}) async-start(bf16[8,32,16,128]{3,2,1,0:T(8,128)(2,1)} %broadcast_in_dim.8), calls=%async_computation.4 | async-start | bytes 2097152 | tf_op jit(solution)/shard_map/all_to_all | solution.py:360
  117.7 9.9 %collective-permute-start.6 = (bf16[16,16,16,128]{3,2,1,0:T(8,128)(2,1)S(1)}, bf16[16,16,16,128]{3,2,1,0:T(8,128)(2,1)S(1)}, u32[]{:S(2)}, u32[]{:S(2)}) collective-permute-start(bf16[16,16,16,128]{3,2,1,0:T(8,128)(2,1)S(1)} %bitcast.18), channel_id=1, source_target_pairs={{0,8},{2,10},{4,12},{6,14},{1,9},{3,11},{5,13},{7,15},{16,24},{18,... | collective-permute-start | bytes 3145736 | tf_op jit(solution)/shard_map/ppermute | solution.py:356

commit v8 on v7

--- a/solution.py
+++ b/solution.py
@@ -111,10 +111,9 @@
     )(place, activations.transpose(1, 2, 0, 3), cotangent.transpose(1, 2, 0, 3))
 
 
-def unpack_kernel(place, own, lon_ref, lat_both, cot, out, cot_ref, lines, semaphores):
+def unpack_kernel(place, own, lon, lat, both, cot, out, cot_ref, lines, semaphores):
     (copy,) = fetched((cot,), (cot_ref,), semaphores)
-    own, lon = (ref[: 2 * QUARTER].astype(jnp.float32) for ref in (own, lon_ref))
-    lat, both = (lat_both[part * 2 * QUARTER : (part + 1) * 2 * QUARTER].astype(jnp.float32) for part in range(2))
+    own, lon, lat, both = (ref[...].astype(jnp.float32) for ref in (own, lon, lat, both))
     even = place[0] == 0
     whole = {
         (0, 0): jnp.where(even, own, lon),
@@ -142,7 +141,7 @@
     local = pl.pallas_call(
         unpack_kernel,
         out_shape=jax.ShapeDtypeStruct(LOCAL, jnp.bfloat16),
-        in_specs=[SMEM] + [VMEM] * 3 + [HBM],
+        in_specs=[SMEM] + [VMEM] * 4 + [HBM],
         out_specs=VMEM,
         scratch_shapes=[
             pltpu.VMEM(LOCAL, jnp.bfloat16),
@@ -175,8 +174,8 @@
 
 
 def block_kernel(place, *refs):
-    quarters, (qkv_weight, proj_weight), (theirs, mine, own, lat, lon_both) = refs[:4], refs[4:6], refs[6:11]
-    x_held, cot_held, normed, attended, qkv_grad, qkv, upstream, tiles = refs[11:]
+    quarters, (qkv_weight, proj_weight), (theirs, mine), branch = refs[:4], refs[4:6], refs[6:8], refs[8:12]
+    x_held, cot_held, normed, attended, qkv_grad, qkv, upstream, tiles = refs[12:]
     own_ref, both_ref, lon_ref, lat_ref = quarters
     held = [ref[...].astype(jnp.float32) for ref in (own_ref, lon_ref, lat_ref, both_ref)]
     for kind, target in enumerate((x_held, cot_held)):
@@ -256,10 +255,8 @@
     average = jnp.mean(normed_grad, axis=-1, keepdims=True)
     product = jnp.mean(normed_grad * xhat, axis=-1, keepdims=True)
     dx = inverse * (normed_grad - average - xhat * product)
-    for target, kinds in ((own, (0,)), (lat, (2,)), (lon_both, (1, 3))):
-        chunks = [
-            dx[(4 * window + kind) * QUARTER : (4 * window + kind + 1) * QUARTER] for kind in kinds for window in range(2)
-        ]
+    for kind, target in enumerate(branch):
+        chunks = [dx[(4 * window + kind) * QUARTER : (4 * window + kind + 1) * QUARTER] for window in range(2)]
         target[...] = jnp.concatenate(chunks, axis=0).astype(jnp.bfloat16)
 
 
@@ -273,9 +270,9 @@
 def block(place, quarters, qkv_weight, proj_weight):
     return pl.pallas_call(
         block_kernel,
-        out_shape=(HALF_TILES, HALF_TILES, rows_of(2 * QUARTER), rows_of(2 * QUARTER), rows_of(4 * QUARTER)),
+        out_shape=(HALF_TILES, HALF_TILES) + (rows_of(2 * QUARTER),) * 4,
         in_specs=[SMEM] + [VMEM] * 6,
-        out_specs=(VMEM,) * 5,
+        out_specs=(VMEM,) * 6,
         scratch_shapes=[
             pltpu.VMEM((TOKENS, D), jnp.bfloat16),
             pltpu.VMEM((TOKENS, D), jnp.bfloat16),
@@ -313,13 +310,15 @@
     return lax.axis_size("z"), lax.axis_size("y_hi") * lax.axis_size("y_lo"), lax.axis_size("x")
 
 
-def cube_groups(stride):
-    def along(size):
-        firsts = [at for at in range(size) if at // stride % 2 == 0]
-        return [[at, at + stride] if at + stride < size else [at] for at in firsts]
+def near_groups():
+    def along(size, core):
+        if size == 1:
+            return [[0]]
+        return [[(2 * at + 2 * core) % size, 2 * at + 1] for at in range(size // 2)]
 
     def members(core):
-        return [list(itertools.product(*lines)) for lines in itertools.product(*(along(size) for size in chips()))]
+        zs, ys, xs = (along(size, core) for size in chips())
+        return [[(z, y, x) for z in za for y in ya for x in xa] for za in zs for ya in ys for xa in xs]
 
     return device_groups(members)
 
@@ -425,25 +424,23 @@
     own, qkv_weight, proj_weight = lax.optimization_barrier((own, qkv_weight, proj_weight))
     both, lon, lat = moved(both, 3, False), moved(lon, 1, False), moved(lat, 2, False)
     qkv_weight, proj_weight = near_weights(qkv_weight, proj_weight)
-    theirs, mine, own, lat, lon_both = block(place, (own, both, lon, lat), qkv_weight, proj_weight)
-
-    near, middle, far = cube_groups(1), middle_groups(), far_groups()
+    theirs, mine, own, lon, lat, both = block(place, (own, both, lon, lat), qkv_weight, proj_weight)
+
+    near, middle, far = near_groups(), middle_groups(), far_groups()
+    lon = moved(lon, 1, True)
     tiles = (mine.astype(jnp.float32) + swapped(theirs).astype(jnp.float32)).astype(jnp.bfloat16)
-    tiles = scattered_sum(tiles.reshape(-1, 16, 128), near)
-    tiles, lon_both = lax.optimization_barrier((tiles, lon_both))
-    tiles, lon_both = lax.optimization_barrier((scattered_sum(tiles, middle), moved(lon_both, 1, True)))
-    lat_both = jnp.concatenate([lat, lon_both[2 * QUARTER :]], axis=0)
-    tiles, lat_both = lax.optimization_barrier((tiles, lat_both))
+    tiles, lat, both = lax.optimization_barrier((tiles.reshape(-1, 16, 128), lat, both))
+    tiles, lon, lat = lax.optimization_barrier((scattered_sum(tiles, near), lon, moved(lat, 2, True)))
+    tiles = scattered_sum(tiles, middle)
     factor = (LEVELS * ROWS * COLS * lax.axis_size(ALL)) ** (-0.5)
     tiles = (added(exchanged(tiles, far)) * factor).astype(jnp.bfloat16)
-    tiles, lat_both = lax.optimization_barrier((tiles, lat_both))
-    tiles, lat_both = lax.optimization_barrier((gathered(tiles, middle), moved(lat_both, 2, True)))
-    input_grad = unpack(place, cotangent, own, lon_both, lat_both)
-    tiles, input_grad = lax.optimization_barrier((gathered(tiles, near), input_grad))
+    tiles, both = lax.optimization_barrier((gathered(tiles, middle), both))
+    tiles, both = lax.optimization_barrier((gathered(tiles, near), moved(both, 3, True)))
     tiles = tiles.reshape(HALF_TILES.shape)
     arrived = swapped(tiles)
     grads = untile(place, tiles, False)
-    arrived, grads = lax.optimization_barrier((arrived, grads))
+    input_grad = unpack(place, cotangent, own, lon, lat, both)
+    arrived, grads, input_grad = lax.optimization_barrier((arrived, grads, input_grad))
     qkv_weight_grad, proj_weight_grad = untile(place, arrived, True, grads)
     return (input_grad, qkv_weight_grad, proj_weight_grad)
 

time: 130 us -> 125 us (0.962)
  waiting for transfers between devices: 27.1 us -> 21.5 us
  blocking collectives: 30.8 us -> 34 us
  starting transfers between devices: 51.1 us -> 48.9 us
    all_to_all x3 -> x2, waiting for transfers between devices: 16.9 us -> 8.75 us  [all_to_all(): return lax.all_to_all(split, ALL, 0, 0, axis_index_groups=groups)]
    ppermute x5 -> x6, starting transfers between devices: 18.4 us -> 25.8 us  [moved(): return lax.ppermute(value, ALL, pairs)]
    all_to_all x3 -> x2, starting transfers between devices: 14.8 us -> 9.89 us  [all_to_all(): return lax.all_to_all(split, ALL, 0, 0, axis_index_groups=groups)]
    ppermute x2, starting transfers between devices: 17.9 us -> 13.2 us  [swapped(): return lax.ppermute(value, ALL, [*zip(first, second), *zip(second, first)])]
    all_to_all x2 -> x3, blocking collectives: 30.8 us -> 34 us  [all_to_all(): return lax.all_to_all(split, ALL, 0, 0, axis_index_groups=groups)]
    ppermute x5 -> x6, waiting for transfers between devices: 7.35 us -> 10.5 us  [moved(): return lax.ppermute(value, ALL, pairs)]
  transfers between devices with their start and end apart: 10 -> 10, of which waited for: 7 -> 4; matrix products, arithmetic and copies ran while one was open for 0% -> 0% of each run, Pallas kernels for 3% -> 3%
where the time goes in v8:
time: 125 us; the launch traced here: 124 us
  starting transfers between devices  48.9 us (39%)
  blocking collectives  34 us (27%)
  waiting for transfers between devices  21.5 us (17%)
  Pallas kernels  12 us (10%)
  local copies, waits for them, and re-layouts  5.51 us (4%)
  other arithmetic  1.51 us (1%)
    all_to_all x3, blocking collectives, all_to_all(): return lax.all_to_all(split, ALL, 0, 0, axis_index_groups=groups)  34 us
    ppermute x6, starting transfers between devices, moved(): return lax.ppermute(value, ALL, pairs)  25.8 us
    ppermute x2, starting transfers between devices, swapped(): return lax.ppermute(value, ALL, [*zip(first, second), *zip(second, first)])  13.2 us
    ppermute x6, waiting for transfers between devices, moved(): return lax.ppermute(value, ALL, pairs)  10.5 us
    all_to_all x2, starting transfers between devices, all_to_all(): return lax.all_to_all(split, ALL, 0, 0, axis_index_groups=groups)  9.89 us
    all_to_all x2, waiting for transfers between devices, all_to_all(): return lax.all_to_all(split, ALL, 0, 0, axis_index_groups=groups)  8.75 us
    pallas_call x1, Pallas kernels, block(): pl.pallas_call(block_kernel, out_shape=(HALF_TILES, HALF_TILES) + (rows_o...  6.12 us
    unnamed x10, local copies, waits for them, and re-layouts  4.37 us
  transfers between devices with their start and end apart: 10, of which 4 were waited for; matrix products, arithmetic and copies ran while one was open for 0% of the time, Pallas kernels for 3%

profile of v8, /device:TPU:1, one launch (start us, length us, event | category | flops | bytes accessed | tf_op | source)
XLA Modules:
  0.0 124.2 jit_solution(1509126713073572750)
XLA Ops:
  3.6 4.6 %collective-permute-start = (bf16[144,512]{1,0:T(8,128)(2,1)S(1)}, bf16[144,512]{1,0:T(8,128)(2,1)S(1)}, u32[]{:S(2)}, u32[]{:S(2)}) collective-permute-start(bf16[144,512]{1,0:T(8,128)(2,1)S(1)} %get-tuple-element.38), channel_id=1, source_target_pairs={{0,505},{1,10},{2,507},{3,12},{4,509},{5,14},{6,511},{7,8},{8,1},{... | collective-permute-start | bytes 442376 | tf_op jit(solution)/shard_map/ppermute | solution.py:47
  8.2 2.9 %collective-permute-start.1 = (bf16[144,512]{1,0:T(8,128)(2,1)S(1)}, bf16[144,512]{1,0:T(8,128)(2,1)S(1)}, u32[]{:S(2)}, u32[]{:S(2)}) collective-permute-start(bf16[144,512]{1,0:T(8,128)(2,1)S(1)} %get-tuple-element.39), channel_id=1, source_target_pairs={{0,8},{1,505},{2,10},{3,507},{4,12},{5,509},{6,14},{7,511},{8,16},... | collective-permute-start | bytes 442376 | tf_op jit(solution)/shard_map/ppermute | solution.py:47
  11.1 3.1 %collective-permute-start.2 = (bf16[144,512]{1,0:T(8,128)(2,1)S(1)}, bf16[144,512]{1,0:T(8,128)(2,1)S(1)}, u32[]{:S(2)}, u32[]{:S(2)}) collective-permute-start(bf16[144,512]{1,0:T(8,128)(2,1)S(1)} %get-tuple-element.40), channel_id=1, source_target_pairs={{0,1},{1,2},{2,3},{3,4},{4,5},{5,6},{6,7},{7,0},{8,9},{9,10},{10,1... | collective-permute-start | bytes 442376 | tf_op jit(solution)/shard_map/ppermute | solution.py:47
  14.2 1.4 %copy-done = bf16[512,1536]{1,0:T(8,128)(2,1)S(1)} copy-done((bf16[512,1536]{1,0:T(8,128)(2,1)S(1)}, bf16[512,1536]{1,0:T(8,128)(2,1)}, u32[]{:S(2)}) %copy-start) | copy-done | bytes 1572888
  16.9 4.3 %collective-permute-done.1.refs_2_ = bf16[144,512]{1,0:T(8,128)(2,1)S(1)} collective-permute-done((bf16[144,512]{1,0:T(8,128)(2,1)S(1)}, bf16[144,512]{1,0:T(8,128)(2,1)S(1)}, u32[]{:S(2)}, u32[]{:S(2)}) %collective-permute-start.1) | collective-permute-done | bytes 147488 | tf_op jit(solution)/shard_map/ppermute | solution.py:47
  21.1 6.1 %block.1 = (bf16[16,16,16,128]{3,2,1,0:T(8,128)(2,1)S(1)}, bf16[16,16,16,128]{3,2,1,0:T(8,128)(2,1)S(1)}, bf16[72,512]{1,0:T(8,128)(2,1)S(1)}, bf16[72,512]{1,0:...) custom-call(s32[4]{0:T(128)S(1)} %add_convert_fusion.3.place, ...), custom_call_target="tpu_custom_call" | custom-call | flops 2000000000 | bytes 6000000 | tf_op jit(solution)/shard_map/block/pallas_call | solution.py:271
  27.3 10.2 %collective-permute-start.3 = (bf16[16,16,16,128]{3,2,1,0:T(8,128)(2,1)S(1)}, bf16[16,16,16,128]{3,2,1,0:T(8,128)(2,1)S(1)}, u32[]{:S(2)}, u32[]{:S(2)}) collective-permute-start(bf16[16,16,16,128]{3,2,1,0:T(8,128)(2,1)S(1)} %get-tuple-element.46), channel_id=1, source_target_pairs={{0,8},{2,10},{4,12},{6,14},{1,9},{3,11},{5,13},{7,15},{16,24},{18,... | collective-permute-start | bytes 3145736 | tf_op jit(solution)/shard_map/ppermute | solution.py:355
  37.5 2.3 %collective-permute-done.3 = bf16[16,16,16,128]{3,2,1,0:T(8,128)(2,1)S(1)} collective-permute-done((bf16[16,16,16,128]{3,2,1,0:T(8,128)(2,1)S(1)}, bf16[16,16,16,128]{3,2,1,0:T(8,128)(2,1)S(1)}, u32[]{:S(2)}, u32[]{:S(2)}) %collective-permute-start.3) | collective-permute-done | bytes 1048608 | tf_op jit(solution)/shard_map/ppermute | solution.py:355
  39.8 1.3 %add_convert_fusion = bf16[16,16,16,128]{3,2,1,0:T(8,128)(2,1)} fusion(bf16[16,16,16,128]{3,2,1,0:T(8,128)(2,1)S(1)} %collective-permute-done.3, bf16[16,16,16,128]{3,2,1,0:T(8,128)(2,1)S(1)} %get-tuple-element.45), kind=kLoop, calls=%fused_computation | loop fusion | flops 2097152 | bytes 3145728 | tf_op jit(solution)/shard_map/convert_element_type | solution.py:431
  41.0 6.2 %all-to-all-start = ((bf16[8,32,16,128]{3,2,1,0:T(8,128)(2,1)}), bf16[8,32,16,128]{3,2,1,0:T(8,128)(2,1)S(1)}, u32[]{:S(2)}, u32[]{:S(2)}) async-start(bf16[8,32,16,128]{3,2,1,0:T(8,128)(2,1)} %bitcast.7), calls=%async_computation | async-start | bytes 2097152 | tf_op jit(solution)/shard_map/all_to_all | solution.py:359
  47.2 1.9 %collective-permute-start.4 = (bf16[72,512]{1,0:T(8,128)(2,1)S(1)}, bf16[72,512]{1,0:T(8,128)(2,1)S(1)}, u32[]{:S(2)}, u32[]{:S(2)}) collective-permute-start(bf16[72,512]{1,0:T(8,128)(2,1)S(1)} %get-tuple-element.50), channel_id=1, source_target_pairs={{8,0},{505,1},{10,2},{507,3},{12,4},{509,5},{14,6},{511,7},{16,8},... | collective-permute-start | bytes 221192 | tf_op jit(solution)/shard_map/ppermute | solution.py:47
  49.1 3.0 %collective-permute-start.5 = (bf16[72,512]{1,0:T(8,128)(2,1)S(1)}, bf16[72,512]{1,0:T(8,128)(2,1)S(1)}, u32[]{:S(2)}, u32[]{:S(2)}) collective-permute-start(bf16[72,512]{1,0:T(8,128)(2,1)S(1)} %get-tuple-element.51), channel_id=1, source_target_pairs={{1,0},{2,1},{3,2},{4,3},{5,4},{6,5},{7,6},{0,7},{9,8},{10,9},{11,1... | collective-permute-start | bytes 221192 | tf_op jit(solution)/shard_map/ppermute | solution.py:47
  52.1 8.7 %all-to-all-done = bf16[8,32,16,128]{3,2,1,0:T(8,128)(2,1)S(1)} async-done(((bf16[8,32,16,128]{3,2,1,0:T(8,128)(2,1)}), bf16[8,32,16,128]{3,2,1,0:T(8,128)(2,1)S(1)}, u32[]{:S(2)}, u32[]{:S(2)}) %all-to-all-start) | async-done | bytes 1048608 | tf_op jit(solution)/shard_map/all_to_all | solution.py:359
  61.0 13.0 %all_to_all.25 = bf16[8,4,16,128]{3,2,1,0:T(8,128)(2,1)S(1)} all-to-all(bf16[8,4,16,128]{3,2,1,0:T(8,128)(2,1)S(1)} %bitcast.24), channel_id=1, replica_groups={{0,128,256,384,4,132,260,388},{1,129,257,385,5,133,261,389},{16,144,272..., dimensions={0} | all-to-all | bytes 262144 | tf_op jit(solution)/shard_map/all_to_all | solution.py:359
  74.1 9.3 %all_to_all.26 = bf16[4,4,16,128]{3,2,1,0:T(8,128)(2,1)S(1)} all-to-all(bf16[4,4,16,128]{3,2,1,0:T(8,128)(2,1)S(1)} %broadcast_in_dim.11), channel_id=1, replica_groups={{0,16,32,48},{2,18,34,50},{4,20,36,52},{6,22,38,54},{64,80,96,112},{66,..., dimensions={0} | all-to-all | bytes 131072 | tf_op jit(solution)/shard_map/all_to_all | solution.py:359
  83.4 11.7 %all_to_all.27 = bf16[8,4,16,128]{3,2,1,0:T(8,128)(2,1)S(1)} all-to-all(bf16[8,4,16,128]{3,2,1,0:T(8,128)(2,1)S(1)} %broadcast_in_dim.25), channel_id=1, replica_groups={{0,128,256,384,4,132,260,388},{1,129,257,385,5,133,261,389},{16,144,272..., dimensions={0} | all-to-all | bytes 262144 | tf_op jit(solution)/shard_map/all_to_all | solution.py:359
  95.1 1.1 broadcast_in_dim.26
  96.2 3.7 %all-to-all-start.4 = ((bf16[8,32,16,128]{3,2,1,0:T(8,128)(2,1)}), bf16[8,32,16,128]{3,2,1,0:T(8,128)(2,1)S(1)}, u32[]{:S(2)}, u32[]{:S(2)}) async-start(bf16[8,32,16,128]{3,2,1,0:T(8,128)(2,1)} %broadcast_in_dim.26), calls=%async_computation.4 | async-start | bytes 2097152 | tf_op jit(solution)/shard_map/all_to_all | solution.py:359
  99.9 10.2 %collective-permute-start.6 = (bf16[72,512]{1,0:T(8,128)(2,1)S(1)}, bf16[72,512]{1,0:T(8,128)(2,1)S(1)}, u32[]{:S(2)}, u32[]{:S(2)}) collective-permute-start(bf16[72,512]{1,0:T(8,128)(2,1)S(1)} %get-tuple-element.55), channel_id=1, source_target_pairs={{505,0},{10,1},{507,2},{12,3},{509,4},{14,5},{511,6},{8,7},{1,8},{... | collective-permute-start | bytes 221192 | tf_op jit(solution)/shard_map/ppermute | solution.py:47
  110.2 6.2 %collective-permute-done.6.both = bf16[72,512]{1,0:T(8,128)(2,1)S(1)} collective-permute-done((bf16[72,512]{1,0:T(8,128)(2,1)S(1)}, bf16[72,512]{1,0:T(8,128)(2,1)S(1)}, u32[]{:S(2)}, u32[]{:S(2)}) %collective-permute-start.6) | collective-permute-done | bytes 73760 | tf_op jit(solution)/shard_map/ppermute | solution.py:47
  116.4 3.0 %collective-permute-start.7 = (bf16[16,16,16,128]{3,2,1,0:T(8,128)(2,1)S(1)}, bf16[16,16,16,128]{3,2,1,0:T(8,128)(2,1)S(1)}, u32[]{:S(2)}, u32[]{:S(2)}) collective-permute-start(bf16[16,16,16,128]{3,2,1,0:T(8,128)(2,1)S(1)} %bitcast.19), channel_id=1, source_target_pairs={{0,8},{2,10},{4,12},{6,14},{1,9},{3,11},{5,13},{7,15},{16,24},{18,... | collective-permute-start | bytes 3145736 | tf_op jit(solution)/shard_map/ppermute | solution.py:355
  119.3 1.6 %untile_own.1 = (bf16[512,1536]{1,0:T(8,128)(2,1)}, bf16[512,512]{1,0:T(8,128)(2,1)}) custom-call(s32[4]{0:T(128)S(1)} %add_convert_fusion.3.place, bf16[16,16,16,128]{3,2,1,0:T(8,128)(2,1)S(1)} %bitcast.20), custom_call_target="tpu_custom_call" | custom-call | bytes 2097152 | tf_op jit(solution)/shard_map/untile_own/pallas_call | solution.py:401
  121.0 1.6 %unpack.1 = bf16[6,12,4,512]{3,2,1,0:T(4,128)(2,1)} custom-call(s32[4]{0:T(128)S(1)} %add_convert_fusion.3.place, bf16[72,512]{1,0:T(8,128)(2,1)S(1)} %get-tuple-element.59.own, bf16[72,512]{1,0:T(8,128)(2,1)S(1)} %collective-permute-done.4.lon, bf16[72,512]{1,0:T(8,128)(2,1)S(1)} %collective-permute-done.5.lat, ...), custom_call_target="tpu_custom_call" | custom-call | bytes 900000 | tf_op jit(solution)/shard_map/unpack/pallas_call | solution.py:141
  122.6 1.6 %untile_other.1 = (bf16[512,1536]{1,0:T(8,128)(2,1)}, bf16[512,512]{1,0:T(8,128)(2,1)}) custom-call(s32[4]{0:T(128)S(1)} %add_convert_fusion.3.place, bf16[16,16,16,128]{3,2,1,0:T(8,128)(2,1)S(1)} %collective-permute-done.7.tiles, bf16[512,1536]{1,0:T(8,128)(2,1)} %get-tuple-element.65.refs_0_, ...), custom_call_target="tpu_custom_call", output_to_operand_aliasing={{0}: (2, {}), {1}: (3, {})} | custom-call | bytes 2097152 | tf_op jit(solution)/shard_map/untile_other/pallas_call | solution.py:401
  (23 shorter events, 4.3 us)
Async XLA Ops:
  0.7 1.0 copy-start.1
  1.7 1.0 copy-start.4
  3.6 13.3 %collective-permute-start = (bf16[144,512]{1,0:T(8,128)(2,1)S(1)}, bf16[144,512]{1,0:T(8,128)(2,1)S(1)}, u32[]{:S(2)}, u32[]{:S(2)}) collective-permute-start(bf16[144,512]{1,0:T(8,128)(2,1)S(1)} %get-tuple-element.38), channel_id=1, source_target_pairs={{0,505},{1,10},{2,507},{3,12},{4,509},{5,14},{6,511},{7,8},{8,1},{... | collective-permute-start | bytes 442376 | tf_op jit(solution)/shard_map/ppermute | solution.py:47
  8.2 13.0 %collective-permute-start.1 = (bf16[144,512]{1,0:T(8,128)(2,1)S(1)}, bf16[144,512]{1,0:T(8,128)(2,1)S(1)}, u32[]{:S(2)}, u32[]{:S(2)}) collective-permute-start(bf16[144,512]{1,0:T(8,128)(2,1)S(1)} %get-tuple-element.39), channel_id=1, source_target_pairs={{0,8},{1,505},{2,10},{3,507},{4,12},{5,509},{6,14},{7,511},{8,16},... | collective-permute-start | bytes 442376 | tf_op jit(solution)/shard_map/ppermute | solution.py:47
  11.1 10.0 %collective-permute-start.2 = (bf16[144,512]{1,0:T(8,128)(2,1)S(1)}, bf16[144,512]{1,0:T(8,128)(2,1)S(1)}, u32[]{:S(2)}, u32[]{:S(2)}) collective-permute-start(bf16[144,512]{1,0:T(8,128)(2,1)S(1)} %get-tuple-element.40), channel_id=1, source_target_pairs={{0,1},{1,2},{2,3},{3,4},{4,5},{5,6},{6,7},{7,0},{8,9},{9,10},{10,1... | collective-permute-start | bytes 442376 | tf_op jit(solution)/shard_map/ppermute | solution.py:47
  14.2 1.4 %copy-start = (bf16[512,1536]{1,0:T(8,128)(2,1)S(1)}, bf16[512,1536]{1,0:T(8,128)(2,1)}, u32[]{:S(2)}) copy-start(bf16[512,1536]{1,0:T(8,128)(2,1)} %qkv_weight) | copy-start | bytes 4718596
  15.6 1.0 copy-start.3
  27.3 12.5 %collective-permute-start.3 = (bf16[16,16,16,128]{3,2,1,0:T(8,128)(2,1)S(1)}, bf16[16,16,16,128]{3,2,1,0:T(8,128)(2,1)S(1)}, u32[]{:S(2)}, u32[]{:S(2)}) collective-permute-start(bf16[16,16,16,128]{3,2,1,0:T(8,128)(2,1)S(1)} %get-tuple-element.46), channel_id=1, source_target_pairs={{0,8},{2,10},{4,12},{6,14},{1,9},{3,11},{5,13},{7,15},{16,24},{18,... | collective-permute-start | bytes 3145736 | tf_op jit(solution)/shard_map/ppermute | solution.py:355
  41.0 19.9 %all-to-all-start = ((bf16[8,32,16,128]{3,2,1,0:T(8,128)(2,1)}), bf16[8,32,16,128]{3,2,1,0:T(8,128)(2,1)S(1)}, u32[]{:S(2)}, u32[]{:S(2)}) async-start(bf16[8,32,16,128]{3,2,1,0:T(8,128)(2,1)} %bitcast.7), calls=%async_computation | async-start | bytes 2097152 | tf_op jit(solution)/shard_map/all_to_all | solution.py:359
  47.2 13.8 %collective-permute-start.4 = (bf16[72,512]{1,0:T(8,128)(2,1)S(1)}, bf16[72,512]{1,0:T(8,128)(2,1)S(1)}, u32[]{:S(2)}, u32[]{:S(2)}) collective-permute-start(bf16[72,512]{1,0:T(8,128)(2,1)S(1)} %get-tuple-element.50), channel_id=1, source_target_pairs={{8,0},{505,1},{10,2},{507,3},{12,4},{509,5},{14,6},{511,7},{16,8},... | collective-permute-start | bytes 221192 | tf_op jit(solution)/shard_map/ppermute | solution.py:47
  49.1 11.9 %collective-permute-start.5 = (bf16[72,512]{1,0:T(8,128)(2,1)S(1)}, bf16[72,512]{1,0:T(8,128)(2,1)S(1)}, u32[]{:S(2)}, u32[]{:S(2)}) collective-permute-start(bf16[72,512]{1,0:T(8,128)(2,1)S(1)} %get-tuple-element.51), channel_id=1, source_target_pairs={{1,0},{2,1},{3,2},{4,3},{5,4},{6,5},{7,6},{0,7},{9,8},{10,9},{11,1... | collective-permute-start | bytes 221192 | tf_op jit(solution)/shard_map/ppermute | solution.py:47
  96.2 24.7 %copy-start.2 = (bf16[4,6,12,512]{3,0,2,1:T(4,128)(2,1)S(1)}, bf16[4,6,12,512]{3,0,2,1:T(4,128)(2,1)}, u32[]{:S(2)}) copy-start(bf16[4,6,12,512]{3,0,2,1:T(4,128)(2,1)} %param.5) | copy-start | bytes 884740
  96.2 20.2 %all-to-all-start.4 = ((bf16[8,32,16,128]{3,2,1,0:T(8,128)(2,1)}), bf16[8,32,16,128]{3,2,1,0:T(8,128)(2,1)S(1)}, u32[]{:S(2)}, u32[]{:S(2)}) async-start(bf16[8,32,16,128]{3,2,1,0:T(8,128)(2,1)} %broadcast_in_dim.26), calls=%async_computation.4 | async-start | bytes 2097152 | tf_op jit(solution)/shard_map/all_to_all | solution.py:359
  99.9 16.5 %collective-permute-start.6 = (bf16[72,512]{1,0:T(8,128)(2,1)S(1)}, bf16[72,512]{1,0:T(8,128)(2,1)S(1)}, u32[]{:S(2)}, u32[]{:S(2)}) collective-permute-start(bf16[72,512]{1,0:T(8,128)(2,1)S(1)} %get-tuple-element.55), channel_id=1, source_target_pairs={{505,0},{10,1},{507,2},{12,3},{509,4},{14,5},{511,6},{8,7},{1,8},{... | collective-permute-start | bytes 221192 | tf_op jit(solution)/shard_map/ppermute | solution.py:47
  116.4 6.2 %collective-permute-start.7 = (bf16[16,16,16,128]{3,2,1,0:T(8,128)(2,1)S(1)}, bf16[16,16,16,128]{3,2,1,0:T(8,128)(2,1)S(1)}, u32[]{:S(2)}, u32[]{:S(2)}) collective-permute-start(bf16[16,16,16,128]{3,2,1,0:T(8,128)(2,1)S(1)} %bitcast.19), channel_id=1, source_target_pairs={{0,8},{2,10},{4,12},{6,14},{1,9},{3,11},{5,13},{7,15},{16,24},{18,... | collective-permute-start | bytes 3145736 | tf_op jit(solution)/shard_map/ppermute | solution.py:355

commit v9 on v8

--- a/solution.py
+++ b/solution.py
@@ -174,8 +174,8 @@
 
 
 def block_kernel(place, *refs):
-    quarters, (qkv_weight, proj_weight), (theirs, mine), branch = refs[:4], refs[4:6], refs[6:8], refs[8:12]
-    x_held, cot_held, normed, attended, qkv_grad, qkv, upstream, tiles = refs[12:]
+    quarters, (qkv_weight, proj_weight), (theirs, mine, x_held, qkv_grad) = refs[:4], refs[4:6], refs[6:10]
+    cot_held, normed, attended, qkv, upstream, tiles = refs[10:]
     own_ref, both_ref, lon_ref, lat_ref = quarters
     held = [ref[...].astype(jnp.float32) for ref in (own_ref, lon_ref, lat_ref, both_ref)]
     for kind, target in enumerate((x_held, cot_held)):
@@ -247,6 +247,9 @@
         put(step + 3 * D // 256, dot(tall, cot_held[:, step * 256 : (step + 1) * 256], 1, 0))
     theirs[...] = tiles[1 - place[3]]
     mine[...] = tiles[place[3]]
+
+
+def rest_kernel(x_held, qkv_grad, qkv_weight, *branch):
     normed_grad = dot(qkv_grad[...], qkv_weight[...], 1, 1)
     x = x_held[...].astype(jnp.float32)
     centered = x - jnp.mean(x, axis=-1, keepdims=True)
@@ -270,15 +273,13 @@
 def block(place, quarters, qkv_weight, proj_weight):
     return pl.pallas_call(
         block_kernel,
-        out_shape=(HALF_TILES, HALF_TILES) + (rows_of(2 * QUARTER),) * 4,
+        out_shape=(HALF_TILES, HALF_TILES, rows_of(TOKENS), rows_of(TOKENS, 3 * D)),
         in_specs=[SMEM] + [VMEM] * 6,
-        out_specs=(VMEM,) * 6,
+        out_specs=(VMEM,) * 4,
         scratch_shapes=[
             pltpu.VMEM((TOKENS, D), jnp.bfloat16),
             pltpu.VMEM((TOKENS, D), jnp.bfloat16),
             pltpu.VMEM((TOKENS, D), jnp.bfloat16),
-            pltpu.VMEM((TOKENS, D), jnp.bfloat16),
-            pltpu.VMEM((TOKENS, 3 * D), jnp.bfloat16),
             pltpu.VMEM((TOKENS, 3 * D), jnp.bfloat16),
             pltpu.VMEM((TOKENS, D), jnp.bfloat16),
             pltpu.VMEM((2,) + HALF_TILES.shape, jnp.bfloat16),
@@ -287,6 +288,18 @@
         cost_estimate=pl.CostEstimate(flops=2 * 10**9, bytes_accessed=6 * 10**6, transcendentals=6 * 10**5),
         name="block",
     )(place, *quarters, qkv_weight, proj_weight)
+
+
+def rest(x_held, qkv_grad, qkv_weight):
+    return pl.pallas_call(
+        rest_kernel,
+        out_shape=(rows_of(2 * QUARTER),) * 4,
+        in_specs=[VMEM] * 3,
+        out_specs=(VMEM,) * 4,
+        compiler_params=pltpu.CompilerParams(vmem_limit_bytes=48 * 2**20),
+        cost_estimate=pl.CostEstimate(flops=5 * 10**8, bytes_accessed=3 * 10**6, transcendentals=300),
+        name="rest",
+    )(x_held, qkv_grad, qkv_weight)
 
 
 def added(arrived):
@@ -424,7 +437,8 @@
     own, qkv_weight, proj_weight = lax.optimization_barrier((own, qkv_weight, proj_weight))
     both, lon, lat = moved(both, 3, False), moved(lon, 1, False), moved(lat, 2, False)
     qkv_weight, proj_weight = near_weights(qkv_weight, proj_weight)
-    theirs, mine, own, lon, lat, both = block(place, (own, both, lon, lat), qkv_weight, proj_weight)
+    theirs, mine, x_held, qkv_grad = block(place, (own, both, lon, lat), qkv_weight, proj_weight)
+    own, lon, lat, both = rest(x_held, qkv_grad, qkv_weight)
 
     near, middle, far = near_groups(), middle_groups(), far_groups()
     lon = moved(lon, 1, True)

time: 125 us -> 124 us (level)
    pallas_call x1 -> x2, Pallas kernels: 6.12 us -> 6.26 us  [the longest x1 5.47 us: block(): pl.pallas_call(block_kernel, out_shape=(HALF_TILES, HALF_TILES, rows_of(T...]
where the time goes in v9:
time: 124 us
  starting transfers between devices  48.9 us (39%)
  blocking collectives  34 us (27%)
  waiting for transfers between devices  20.7 us (17%)
  Pallas kernels  12.1 us (10%)
  local copies, waits for them, and re-layouts  5.51 us (4%)
  other arithmetic  1.51 us (1%)
    all_to_all x3, blocking collectives, all_to_all(): return lax.all_to_all(split, ALL, 0, 0, axis_index_groups=groups)  34 us
    ppermute x6, starting transfers between devices, moved(): return lax.ppermute(value, ALL, pairs)  25.8 us
    ppermute x2, starting transfers between devices, swapped(): return lax.ppermute(value, ALL, [*zip(first, second), *zip(second, first)])  13.2 us
    ppermute x6, waiting for transfers between devices, moved(): return lax.ppermute(value, ALL, pairs)  10.5 us
    all_to_all x2, starting transfers between devices, all_to_all(): return lax.all_to_all(split, ALL, 0, 0, axis_index_groups=groups)  9.89 us
    all_to_all x2, waiting for transfers between devices, all_to_all(): return lax.all_to_all(split, ALL, 0, 0, axis_index_groups=groups)  8.75 us
    pallas_call x1, Pallas kernels, block(): pl.pallas_call(block_kernel, out_shape=(HALF_TILES, HALF_TILES, rows_of(T...  5.47 us
    unnamed x10, local copies, waits for them, and re-layouts  4.37 us
  transfers between devices with their start and end apart: 10, of which 4 were waited for; matrix products, arithmetic and copies ran while one was open for 0% of the time, Pallas kernels for 3%

profile of v9, /device:TPU:1, one launch (start us, length us, event | category | flops | bytes accessed | tf_op | source)
XLA Modules:
  0.0 123.5 jit_solution(9790816691981974886)
XLA Ops:
  3.6 4.6 %collective-permute-start = (bf16[144,512]{1,0:T(8,128)(2,1)S(1)}, bf16[144,512]{1,0:T(8,128)(2,1)S(1)}, u32[]{:S(2)}, u32[]{:S(2)}) collective-permute-start(bf16[144,512]{1,0:T(8,128)(2,1)S(1)} %get-tuple-element.40), channel_id=1, source_target_pairs={{0,505},{1,10},{2,507},{3,12},{4,509},{5,14},{6,511},{7,8},{8,1},{... | collective-permute-start | bytes 442376 | tf_op jit(solution)/shard_map/ppermute | solution.py:47
  8.2 2.9 %collective-permute-start.1 = (bf16[144,512]{1,0:T(8,128)(2,1)S(1)}, bf16[144,512]{1,0:T(8,128)(2,1)S(1)}, u32[]{:S(2)}, u32[]{:S(2)}) collective-permute-start(bf16[144,512]{1,0:T(8,128)(2,1)S(1)} %get-tuple-element.41), channel_id=1, source_target_pairs={{0,8},{1,505},{2,10},{3,507},{4,12},{5,509},{6,14},{7,511},{8,16},... | collective-permute-start | bytes 442376 | tf_op jit(solution)/shard_map/ppermute | solution.py:47
  11.1 3.1 %collective-permute-start.2 = (bf16[144,512]{1,0:T(8,128)(2,1)S(1)}, bf16[144,512]{1,0:T(8,128)(2,1)S(1)}, u32[]{:S(2)}, u32[]{:S(2)}) collective-permute-start(bf16[144,512]{1,0:T(8,128)(2,1)S(1)} %get-tuple-element.42), channel_id=1, source_target_pairs={{0,1},{1,2},{2,3},{3,4},{4,5},{5,6},{6,7},{7,0},{8,9},{9,10},{10,1... | collective-permute-start | bytes 442376 | tf_op jit(solution)/shard_map/ppermute | solution.py:47
  14.2 1.4 %copy-done = bf16[512,1536]{1,0:T(8,128)(2,1)S(1)} copy-done((bf16[512,1536]{1,0:T(8,128)(2,1)S(1)}, bf16[512,1536]{1,0:T(8,128)(2,1)}, u32[]{:S(2)}) %copy-start) | copy-done | bytes 1572888
  16.9 4.3 %collective-permute-done.1.refs_2_ = bf16[144,512]{1,0:T(8,128)(2,1)S(1)} collective-permute-done((bf16[144,512]{1,0:T(8,128)(2,1)S(1)}, bf16[144,512]{1,0:T(8,128)(2,1)S(1)}, u32[]{:S(2)}, u32[]{:S(2)}) %collective-permute-start.1) | collective-permute-done | bytes 147488 | tf_op jit(solution)/shard_map/ppermute | solution.py:47
  21.1 5.5 %block.1 = (bf16[16,16,16,128]{3,2,1,0:T(8,128)(2,1)S(1)}, bf16[16,16,16,128]{3,2,1,0:T(8,128)(2,1)S(1)}, bf16[288,512]{1,0:T(8,128)(2,1)S(1)}, bf16[288,1536]{1,0:T(8,128)(2,1)S(1)}) custom-call(s32[4]{0:T(128)S(1)} %add_convert_fusion.3.place, bf16[144,512]{1,0:T(8,128)(2,1)S(1)} %get-tuple-element.39.refs_0_, ...), custom_call_target="tpu_custom_call" | custom-call | flops 2000000000 | bytes 6000000 | tf_op jit(solution)/shard_map/block/pallas_call | solution.py:274
  26.6 10.2 %collective-permute-start.3 = (bf16[16,16,16,128]{3,2,1,0:T(8,128)(2,1)S(1)}, bf16[16,16,16,128]{3,2,1,0:T(8,128)(2,1)S(1)}, u32[]{:S(2)}, u32[]{:S(2)}) collective-permute-start(bf16[16,16,16,128]{3,2,1,0:T(8,128)(2,1)S(1)} %get-tuple-element.48), channel_id=1, source_target_pairs={{0,8},{2,10},{4,12},{6,14},{1,9},{3,11},{5,13},{7,15},{16,24},{18,... | collective-permute-start | bytes 3145736 | tf_op jit(solution)/shard_map/ppermute | solution.py:368
  37.6 1.5 %collective-permute-done.3 = bf16[16,16,16,128]{3,2,1,0:T(8,128)(2,1)S(1)} collective-permute-done((bf16[16,16,16,128]{3,2,1,0:T(8,128)(2,1)S(1)}, bf16[16,16,16,128]{3,2,1,0:T(8,128)(2,1)S(1)}, u32[]{:S(2)}, u32[]{:S(2)}) %collective-permute-start.3) | collective-permute-done | bytes 1048608 | tf_op jit(solution)/shard_map/ppermute | solution.py:368
  39.1 1.3 %add_convert_fusion = bf16[16,16,16,128]{3,2,1,0:T(8,128)(2,1)} fusion(bf16[16,16,16,128]{3,2,1,0:T(8,128)(2,1)S(1)} %collective-permute-done.3, bf16[16,16,16,128]{3,2,1,0:T(8,128)(2,1)S(1)} %get-tuple-element.47), kind=kLoop, calls=%fused_computation | loop fusion | flops 2097152 | bytes 3145728 | tf_op jit(solution)/shard_map/convert_element_type | solution.py:445
  40.4 6.2 %all-to-all-start = ((bf16[8,32,16,128]{3,2,1,0:T(8,128)(2,1)}), bf16[8,32,16,128]{3,2,1,0:T(8,128)(2,1)S(1)}, u32[]{:S(2)}, u32[]{:S(2)}) async-start(bf16[8,32,16,128]{3,2,1,0:T(8,128)(2,1)} %bitcast.7), calls=%async_computation | async-start | bytes 2097152 | tf_op jit(solution)/shard_map/all_to_all | solution.py:372
  46.6 1.9 %collective-permute-start.4 = (bf16[72,512]{1,0:T(8,128)(2,1)S(1)}, bf16[72,512]{1,0:T(8,128)(2,1)S(1)}, u32[]{:S(2)}, u32[]{:S(2)}) collective-permute-start(bf16[72,512]{1,0:T(8,128)(2,1)S(1)} %get-tuple-element.54), channel_id=1, source_target_pairs={{8,0},{505,1},{10,2},{507,3},{12,4},{509,5},{14,6},{511,7},{16,8},... | collective-permute-start | bytes 221192 | tf_op jit(solution)/shard_map/ppermute | solution.py:47
  48.5 3.0 %collective-permute-start.5 = (bf16[72,512]{1,0:T(8,128)(2,1)S(1)}, bf16[72,512]{1,0:T(8,128)(2,1)S(1)}, u32[]{:S(2)}, u32[]{:S(2)}) collective-permute-start(bf16[72,512]{1,0:T(8,128)(2,1)S(1)} %get-tuple-element.55), channel_id=1, source_target_pairs={{1,0},{2,1},{3,2},{4,3},{5,4},{6,5},{7,6},{0,7},{9,8},{10,9},{11,1... | collective-permute-start | bytes 221192 | tf_op jit(solution)/shard_map/ppermute | solution.py:47
  51.5 8.7 %all-to-all-done = bf16[8,32,16,128]{3,2,1,0:T(8,128)(2,1)S(1)} async-done(((bf16[8,32,16,128]{3,2,1,0:T(8,128)(2,1)}), bf16[8,32,16,128]{3,2,1,0:T(8,128)(2,1)S(1)}, u32[]{:S(2)}, u32[]{:S(2)}) %all-to-all-start) | async-done | bytes 1048608 | tf_op jit(solution)/shard_map/all_to_all | solution.py:372
  60.4 13.0 %all_to_all.25 = bf16[8,4,16,128]{3,2,1,0:T(8,128)(2,1)S(1)} all-to-all(bf16[8,4,16,128]{3,2,1,0:T(8,128)(2,1)S(1)} %bitcast.24), channel_id=1, replica_groups={{0,128,256,384,4,132,260,388},{1,129,257,385,5,133,261,389},{16,144,272..., dimensions={0} | all-to-all | bytes 262144 | tf_op jit(solution)/shard_map/all_to_all | solution.py:372
  73.4 9.3 %all_to_all.26 = bf16[4,4,16,128]{3,2,1,0:T(8,128)(2,1)S(1)} all-to-all(bf16[4,4,16,128]{3,2,1,0:T(8,128)(2,1)S(1)} %broadcast_in_dim.11), channel_id=1, replica_groups={{0,16,32,48},{2,18,34,50},{4,20,36,52},{6,22,38,54},{64,80,96,112},{66,..., dimensions={0} | all-to-all | bytes 131072 | tf_op jit(solution)/shard_map/all_to_all | solution.py:372
  82.7 11.7 %all_to_all.27 = bf16[8,4,16,128]{3,2,1,0:T(8,128)(2,1)S(1)} all-to-all(bf16[8,4,16,128]{3,2,1,0:T(8,128)(2,1)S(1)} %broadcast_in_dim.25), channel_id=1, replica_groups={{0,128,256,384,4,132,260,388},{1,129,257,385,5,133,261,389},{16,144,272..., dimensions={0} | all-to-all | bytes 262144 | tf_op jit(solution)/shard_map/all_to_all | solution.py:372
  94.5 1.1 broadcast_in_dim.26
  95.6 3.7 %all-to-all-start.4 = ((bf16[8,32,16,128]{3,2,1,0:T(8,128)(2,1)}), bf16[8,32,16,128]{3,2,1,0:T(8,128)(2,1)S(1)}, u32[]{:S(2)}, u32[]{:S(2)}) async-start(bf16[8,32,16,128]{3,2,1,0:T(8,128)(2,1)} %broadcast_in_dim.26), calls=%async_computation.4 | async-start | bytes 2097152 | tf_op jit(solution)/shard_map/all_to_all | solution.py:372
  99.3 10.3 %collective-permute-start.6 = (bf16[72,512]{1,0:T(8,128)(2,1)S(1)}, bf16[72,512]{1,0:T(8,128)(2,1)S(1)}, u32[]{:S(2)}, u32[]{:S(2)}) collective-permute-start(bf16[72,512]{1,0:T(8,128)(2,1)S(1)} %get-tuple-element.59), channel_id=1, source_target_pairs={{505,0},{10,1},{507,2},{12,3},{509,4},{14,5},{511,6},{8,7},{1,8},{... | collective-permute-start | bytes 221192 | tf_op jit(solution)/shard_map/ppermute | solution.py:47
  109.5 6.2 %collective-permute-done.6.both = bf16[72,512]{1,0:T(8,128)(2,1)S(1)} collective-permute-done((bf16[72,512]{1,0:T(8,128)(2,1)S(1)}, bf16[72,512]{1,0:T(8,128)(2,1)S(1)}, u32[]{:S(2)}, u32[]{:S(2)}) %collective-permute-start.6) | collective-permute-done | bytes 73760 | tf_op jit(solution)/shard_map/ppermute | solution.py:47
  115.7 3.0 %collective-permute-start.7 = (bf16[16,16,16,128]{3,2,1,0:T(8,128)(2,1)S(1)}, bf16[16,16,16,128]{3,2,1,0:T(8,128)(2,1)S(1)}, u32[]{:S(2)}, u32[]{:S(2)}) collective-permute-start(bf16[16,16,16,128]{3,2,1,0:T(8,128)(2,1)S(1)} %bitcast.19), channel_id=1, source_target_pairs={{0,8},{2,10},{4,12},{6,14},{1,9},{3,11},{5,13},{7,15},{16,24},{18,... | collective-permute-start | bytes 3145736 | tf_op jit(solution)/shard_map/ppermute | solution.py:368
  118.7 1.6 %untile_own.1 = (bf16[512,1536]{1,0:T(8,128)(2,1)}, bf16[512,512]{1,0:T(8,128)(2,1)}) custom-call(s32[4]{0:T(128)S(1)} %add_convert_fusion.3.place, bf16[16,16,16,128]{3,2,1,0:T(8,128)(2,1)S(1)} %bitcast.20), custom_call_target="tpu_custom_call" | custom-call | bytes 2097152 | tf_op jit(solution)/shard_map/untile_own/pallas_call | solution.py:414
  120.3 1.6 %unpack.1 = bf16[6,12,4,512]{3,2,1,0:T(4,128)(2,1)} custom-call(s32[4]{0:T(128)S(1)} %add_convert_fusion.3.place, bf16[72,512]{1,0:T(8,128)(2,1)S(1)} %get-tuple-element.63.own, bf16[72,512]{1,0:T(8,128)(2,1)S(1)} %collective-permute-done.4.lon, bf16[72,512]{1,0:T(8,128)(2,1)S(1)} %collective-permute-done.5.lat, ...), custom_call_target="tpu_custom_call" | custom-call | bytes 900000 | tf_op jit(solution)/shard_map/unpack/pallas_call | solution.py:141
  121.9 1.6 %untile_other.1 = (bf16[512,1536]{1,0:T(8,128)(2,1)}, bf16[512,512]{1,0:T(8,128)(2,1)}) custom-call(s32[4]{0:T(128)S(1)} %add_convert_fusion.3.place, bf16[16,16,16,128]{3,2,1,0:T(8,128)(2,1)S(1)} %collective-permute-done.7.tiles, bf16[512,1536]{1,0:T(8,128)(2,1)} %get-tuple-element.69.refs_0_, ...), custom_call_target="tpu_custom_call", output_to_operand_aliasing={{0}: (2, {}), {1}: (3, {})} | custom-call | bytes 2097152 | tf_op jit(solution)/shard_map/untile_other/pallas_call | solution.py:414
  (24 shorter events, 5.1 us)
Async XLA Ops:
  0.7 1.0 copy-start.1
  1.7 1.0 copy-start.4
  3.6 13.3 %collective-permute-start = (bf16[144,512]{1,0:T(8,128)(2,1)S(1)}, bf16[144,512]{1,0:T(8,128)(2,1)S(1)}, u32[]{:S(2)}, u32[]{:S(2)}) collective-permute-start(bf16[144,512]{1,0:T(8,128)(2,1)S(1)} %get-tuple-element.40), channel_id=1, source_target_pairs={{0,505},{1,10},{2,507},{3,12},{4,509},{5,14},{6,511},{7,8},{8,1},{... | collective-permute-start | bytes 442376 | tf_op jit(solution)/shard_map/ppermute | solution.py:47
  8.2 13.0 %collective-permute-start.1 = (bf16[144,512]{1,0:T(8,128)(2,1)S(1)}, bf16[144,512]{1,0:T(8,128)(2,1)S(1)}, u32[]{:S(2)}, u32[]{:S(2)}) collective-permute-start(bf16[144,512]{1,0:T(8,128)(2,1)S(1)} %get-tuple-element.41), channel_id=1, source_target_pairs={{0,8},{1,505},{2,10},{3,507},{4,12},{5,509},{6,14},{7,511},{8,16},... | collective-permute-start | bytes 442376 | tf_op jit(solution)/shard_map/ppermute | solution.py:47
  11.1 10.0 %collective-permute-start.2 = (bf16[144,512]{1,0:T(8,128)(2,1)S(1)}, bf16[144,512]{1,0:T(8,128)(2,1)S(1)}, u32[]{:S(2)}, u32[]{:S(2)}) collective-permute-start(bf16[144,512]{1,0:T(8,128)(2,1)S(1)} %get-tuple-element.42), channel_id=1, source_target_pairs={{0,1},{1,2},{2,3},{3,4},{4,5},{5,6},{6,7},{7,0},{8,9},{9,10},{10,1... | collective-permute-start | bytes 442376 | tf_op jit(solution)/shard_map/ppermute | solution.py:47
  14.2 1.4 %copy-start = (bf16[512,1536]{1,0:T(8,128)(2,1)S(1)}, bf16[512,1536]{1,0:T(8,128)(2,1)}, u32[]{:S(2)}) copy-start(bf16[512,1536]{1,0:T(8,128)(2,1)} %qkv_weight) | copy-start | bytes 4718596
  15.6 1.0 copy-start.3
  26.6 12.5 %collective-permute-start.3 = (bf16[16,16,16,128]{3,2,1,0:T(8,128)(2,1)S(1)}, bf16[16,16,16,128]{3,2,1,0:T(8,128)(2,1)S(1)}, u32[]{:S(2)}, u32[]{:S(2)}) collective-permute-start(bf16[16,16,16,128]{3,2,1,0:T(8,128)(2,1)S(1)} %get-tuple-element.48), channel_id=1, source_target_pairs={{0,8},{2,10},{4,12},{6,14},{1,9},{3,11},{5,13},{7,15},{16,24},{18,... | collective-permute-start | bytes 3145736 | tf_op jit(solution)/shard_map/ppermute | solution.py:368
  40.4 19.9 %all-to-all-start = ((bf16[8,32,16,128]{3,2,1,0:T(8,128)(2,1)}), bf16[8,32,16,128]{3,2,1,0:T(8,128)(2,1)S(1)}, u32[]{:S(2)}, u32[]{:S(2)}) async-start(bf16[8,32,16,128]{3,2,1,0:T(8,128)(2,1)} %bitcast.7), calls=%async_computation | async-start | bytes 2097152 | tf_op jit(solution)/shard_map/all_to_all | solution.py:372
  46.6 13.8 %collective-permute-start.4 = (bf16[72,512]{1,0:T(8,128)(2,1)S(1)}, bf16[72,512]{1,0:T(8,128)(2,1)S(1)}, u32[]{:S(2)}, u32[]{:S(2)}) collective-permute-start(bf16[72,512]{1,0:T(8,128)(2,1)S(1)} %get-tuple-element.54), channel_id=1, source_target_pairs={{8,0},{505,1},{10,2},{507,3},{12,4},{509,5},{14,6},{511,7},{16,8},... | collective-permute-start | bytes 221192 | tf_op jit(solution)/shard_map/ppermute | solution.py:47
  48.5 11.9 %collective-permute-start.5 = (bf16[72,512]{1,0:T(8,128)(2,1)S(1)}, bf16[72,512]{1,0:T(8,128)(2,1)S(1)}, u32[]{:S(2)}, u32[]{:S(2)}) collective-permute-start(bf16[72,512]{1,0:T(8,128)(2,1)S(1)} %get-tuple-element.55), channel_id=1, source_target_pairs={{1,0},{2,1},{3,2},{4,3},{5,4},{6,5},{7,6},{0,7},{9,8},{10,9},{11,1... | collective-permute-start | bytes 221192 | tf_op jit(solution)/shard_map/ppermute | solution.py:47
  95.6 24.7 %copy-start.2 = (bf16[4,6,12,512]{3,0,2,1:T(4,128)(2,1)S(1)}, bf16[4,6,12,512]{3,0,2,1:T(4,128)(2,1)}, u32[]{:S(2)}) copy-start(bf16[4,6,12,512]{3,0,2,1:T(4,128)(2,1)} %param.5) | copy-start | bytes 884740
  95.6 20.2 %all-to-all-start.4 = ((bf16[8,32,16,128]{3,2,1,0:T(8,128)(2,1)}), bf16[8,32,16,128]{3,2,1,0:T(8,128)(2,1)S(1)}, u32[]{:S(2)}, u32[]{:S(2)}) async-start(bf16[8,32,16,128]{3,2,1,0:T(8,128)(2,1)} %broadcast_in_dim.26), calls=%async_computation.4 | async-start | bytes 2097152 | tf_op jit(solution)/shard_map/all_to_all | solution.py:372
  99.3 16.5 %collective-permute-start.6 = (bf16[72,512]{1,0:T(8,128)(2,1)S(1)}, bf16[72,512]{1,0:T(8,128)(2,1)S(1)}, u32[]{:S(2)}, u32[]{:S(2)}) collective-permute-start(bf16[72,512]{1,0:T(8,128)(2,1)S(1)} %get-tuple-element.59), channel_id=1, source_target_pairs={{505,0},{10,1},{507,2},{12,3},{509,4},{14,5},{511,6},{8,7},{1,8},{... | collective-permute-start | bytes 221192 | tf_op jit(solution)/shard_map/ppermute | solution.py:47
  115.7 6.2 %collective-permute-start.7 = (bf16[16,16,16,128]{3,2,1,0:T(8,128)(2,1)S(1)}, bf16[16,16,16,128]{3,2,1,0:T(8,128)(2,1)S(1)}, u32[]{:S(2)}, u32[]{:S(2)}) collective-permute-start(bf16[16,16,16,128]{3,2,1,0:T(8,128)(2,1)S(1)} %bitcast.19), channel_id=1, source_target_pairs={{0,8},{2,10},{4,12},{6,14},{1,9},{3,11},{5,13},{7,15},{16,24},{18,... | collective-permute-start | bytes 3145736 | tf_op jit(solution)/shard_map/ppermute | solution.py:368

commit v10 on v9

--- a/solution.py
+++ b/solution.py
@@ -1,4 +1,3 @@
-import functools
 import itertools
 
 import jax
@@ -386,46 +385,27 @@
     return exchanged(tiles, groups).reshape((-1,) + tiles.shape[1:])
 
 
-def untile_kernel(other, place, tiles, *refs):
-    qkv_out, proj_out, qkv_held, proj_held, semaphores = refs[-5:]
-    first = (1 - place[3] if other else place[3]) * (D // 2)
-    chunk = D // 2 // CHUNKS
-    copies = []
-    for at in range(CHUNKS):
-        rows = slice(at * chunk, (at + 1) * chunk)
+def untile_kernel(place, mine, theirs, qkv_out, proj_out):
+    for core, tiles in ((place[3], mine), (1 - place[3], theirs)):
+        rows = pl.ds(pl.multiple_of(core * (D // 2), D // 2), D // 2)
         for col in range(4 * D // 128):
-            strip = tiles[at * chunk // 16 : (at + 1) * chunk // 16, col].reshape(chunk, 128)
+            strip = tiles[:, col].reshape(D // 2, 128)
             if col < 3 * D // 128:
-                qkv_held[rows, 128 * col : 128 * col + 128] = strip
+                qkv_out[rows, 128 * col : 128 * col + 128] = strip
             else:
-                proj_held[rows, 128 * col - 3 * D : 128 * col - 3 * D + 128] = strip
-        target = pl.ds(pl.multiple_of(first + at * chunk, chunk), chunk)
-        for kind, (held, out) in enumerate(((qkv_held, qkv_out), (proj_held, proj_out))):
-            copies.append(pltpu.make_async_copy(held.at[rows], out.at[target], semaphores.at[2 * at + kind]))
-            copies[-1].start()
-    for copy in copies:
-        copy.wait()
-
-
-CHUNKS = 4
-
-
-def untile(place, tiles, other, so_far=()):
+                proj_out[rows, 128 * col - 3 * D : 128 * col - 3 * D + 128] = strip
+
+
+def untile(place, mine, theirs):
     return pl.pallas_call(
-        functools.partial(untile_kernel, other),
-        in_specs=[SMEM, VMEM] + [HBM] * len(so_far),
-        out_specs=(HBM, HBM),
+        untile_kernel,
+        in_specs=[SMEM, VMEM, VMEM],
+        out_specs=(VMEM, VMEM),
         out_shape=(rows_of(D, 3 * D), rows_of(D)),
-        scratch_shapes=[
-            pltpu.VMEM((D // 2, 3 * D), jnp.bfloat16),
-            pltpu.VMEM((D // 2, D), jnp.bfloat16),
-            pltpu.SemaphoreType.DMA((2 * CHUNKS,)),
-        ],
-        input_output_aliases={2: 0, 3: 1} if so_far else {},
         compiler_params=pltpu.CompilerParams(vmem_limit_bytes=32 * 2**20),
-        cost_estimate=pl.CostEstimate(flops=0, bytes_accessed=2 * 2**20, transcendentals=0),
-        name="untile_other" if other else "untile_own",
-    )(place, tiles, *so_far)
+        cost_estimate=pl.CostEstimate(flops=0, bytes_accessed=4 * 2**20, transcendentals=0),
+        name="untile",
+    )(place, mine, theirs)
 
 
 def per_device(activations, cotangent, qkv_weight, proj_weight):
@@ -441,21 +421,19 @@
     own, lon, lat, both = rest(x_held, qkv_grad, qkv_weight)
 
     near, middle, far = near_groups(), middle_groups(), far_groups()
-    lon = moved(lon, 1, True)
     tiles = (mine.astype(jnp.float32) + swapped(theirs).astype(jnp.float32)).astype(jnp.bfloat16)
-    tiles, lat, both = lax.optimization_barrier((tiles.reshape(-1, 16, 128), lat, both))
-    tiles, lon, lat = lax.optimization_barrier((scattered_sum(tiles, near), lon, moved(lat, 2, True)))
-    tiles = scattered_sum(tiles, middle)
+    tiles, lon, lat, both = lax.optimization_barrier((tiles.reshape(-1, 16, 128), lon, lat, both))
+    tiles, lat, lon = lax.optimization_barrier((scattered_sum(tiles, near), moved(lat, 2, True), lon))
+    tiles, lon = lax.optimization_barrier((scattered_sum(tiles, middle), moved(lon, 1, True)))
     factor = (LEVELS * ROWS * COLS * lax.axis_size(ALL)) ** (-0.5)
     tiles = (added(exchanged(tiles, far)) * factor).astype(jnp.bfloat16)
     tiles, both = lax.optimization_barrier((gathered(tiles, middle), both))
     tiles, both = lax.optimization_barrier((gathered(tiles, near), moved(both, 3, True)))
     tiles = tiles.reshape(HALF_TILES.shape)
     arrived = swapped(tiles)
-    grads = untile(place, tiles, False)
     input_grad = unpack(place, cotangent, own, lon, lat, both)
-    arrived, grads, input_grad = lax.optimization_barrier((arrived, grads, input_grad))
-    qkv_weight_grad, proj_weight_grad = untile(place, arrived, True, grads)
+    arrived, input_grad = lax.optimization_barrier((arrived, input_grad))
+    qkv_weight_grad, proj_weight_grad = untile(place, tiles, arrived)
     return (input_grad, qkv_weight_grad, proj_weight_grad)
 
 

time: 124 us -> 126 us (1.016)
  waiting for transfers between devices: 20.7 us -> 30.6 us
  blocking collectives: 34 us -> 25.1 us
  starting transfers between devices: 48.9 us -> 50.3 us
    all_to_all x2 -> x3, waiting for transfers between devices: 8.75 us -> 18.2 us  [all_to_all(): return lax.all_to_all(split, ALL, 0, 0, axis_index_groups=groups)]
    all_to_all x3 -> x2, blocking collectives: 34 us -> 25.1 us  [all_to_all(): return lax.all_to_all(split, ALL, 0, 0, axis_index_groups=groups)]
    all_to_all x2 -> x3, starting transfers between devices: 9.89 us -> 13.7 us  [all_to_all(): return lax.all_to_all(split, ALL, 0, 0, axis_index_groups=groups)]
    ppermute x6, starting transfers between devices: 25.8 us -> 23.4 us  [moved(): return lax.ppermute(value, ALL, pairs)]
    pallas_call x2 -> x1, Pallas kernels: 3.22 us -> 2.21 us  [untile(): pl.pallas_call(untile_kernel, in_specs=[SMEM, VMEM, VMEM], out_specs=(VME...]
  transfers between devices with their start and end apart: 10 -> 11, of which waited for: 4 -> 6; matrix products, arithmetic and copies ran while one was open for 0% -> 1% of each run, Pallas kernels for 3% -> 2%
where the time goes in v10:
time: 126 us
  starting transfers between devices  50.3 us (40%)
  waiting for transfers between devices  30.6 us (24%)
  blocking collectives  25.1 us (20%)
  Pallas kernels  11.1 us (9%)
  local copies, waits for them, and re-layouts  5.51 us (4%)
  other arithmetic  2.16 us (2%)
    all_to_all x2, blocking collectives, all_to_all(): return lax.all_to_all(split, ALL, 0, 0, axis_index_groups=groups)  25.1 us
    ppermute x6, starting transfers between devices, moved(): return lax.ppermute(value, ALL, pairs)  23.4 us
    all_to_all x3, waiting for transfers between devices, all_to_all(): return lax.all_to_all(split, ALL, 0, 0, axis_index_groups=groups)  18.2 us
    all_to_all x3, starting transfers between devices, all_to_all(): return lax.all_to_all(split, ALL, 0, 0, axis_index_groups=groups)  13.7 us
    ppermute x2, starting transfers between devices, swapped(): return lax.ppermute(value, ALL, [*zip(first, second), *zip(second, first)])  13.2 us
    ppermute x6, waiting for transfers between devices, moved(): return lax.ppermute(value, ALL, pairs)  10.3 us
    pallas_call x1, Pallas kernels, block(): pl.pallas_call(block_kernel, out_shape=(HALF_TILES, HALF_TILES, rows_of(T...  5.47 us
    unnamed x10, local copies, waits for them, and re-layouts  4.37 us
  transfers between devices with their start and end apart: 11, of which 6 were waited for; matrix products, arithmetic and copies ran while one was open for 1% of the time, Pallas kernels for 2%

profile of v10, /device:TPU:1, one launch (start us, length us, event | category | flops | bytes accessed | tf_op | source)
XLA Modules:
  0.0 125.6 jit_solution(7664524628401200964)
XLA Ops:
  3.6 4.6 %collective-permute-start = (bf16[144,512]{1,0:T(8,128)(2,1)S(1)}, bf16[144,512]{1,0:T(8,128)(2,1)S(1)}, u32[]{:S(2)}, u32[]{:S(2)}) collective-permute-start(bf16[144,512]{1,0:T(8,128)(2,1)S(1)} %get-tuple-element.39), channel_id=1, source_target_pairs={{0,505},{1,10},{2,507},{3,12},{4,509},{5,14},{6,511},{7,8},{8,1},{... | collective-permute-start | bytes 442376 | tf_op jit(solution)/shard_map/ppermute | solution.py:46
  8.2 2.9 %collective-permute-start.1 = (bf16[144,512]{1,0:T(8,128)(2,1)S(1)}, bf16[144,512]{1,0:T(8,128)(2,1)S(1)}, u32[]{:S(2)}, u32[]{:S(2)}) collective-permute-start(bf16[144,512]{1,0:T(8,128)(2,1)S(1)} %get-tuple-element.40), channel_id=1, source_target_pairs={{0,8},{1,505},{2,10},{3,507},{4,12},{5,509},{6,14},{7,511},{8,16},... | collective-permute-start | bytes 442376 | tf_op jit(solution)/shard_map/ppermute | solution.py:46
  11.1 3.1 %collective-permute-start.2 = (bf16[144,512]{1,0:T(8,128)(2,1)S(1)}, bf16[144,512]{1,0:T(8,128)(2,1)S(1)}, u32[]{:S(2)}, u32[]{:S(2)}) collective-permute-start(bf16[144,512]{1,0:T(8,128)(2,1)S(1)} %get-tuple-element.41), channel_id=1, source_target_pairs={{0,1},{1,2},{2,3},{3,4},{4,5},{5,6},{6,7},{7,0},{8,9},{9,10},{10,1... | collective-permute-start | bytes 442376 | tf_op jit(solution)/shard_map/ppermute | solution.py:46
  14.2 1.4 %copy-done = bf16[512,1536]{1,0:T(8,128)(2,1)S(1)} copy-done((bf16[512,1536]{1,0:T(8,128)(2,1)S(1)}, bf16[512,1536]{1,0:T(8,128)(2,1)}, u32[]{:S(2)}) %copy-start) | copy-done | bytes 1572888
  16.9 4.3 %collective-permute-done.1.refs_2_ = bf16[144,512]{1,0:T(8,128)(2,1)S(1)} collective-permute-done((bf16[144,512]{1,0:T(8,128)(2,1)S(1)}, bf16[144,512]{1,0:T(8,128)(2,1)S(1)}, u32[]{:S(2)}, u32[]{:S(2)}) %collective-permute-start.1) | collective-permute-done | bytes 147488 | tf_op jit(solution)/shard_map/ppermute | solution.py:46
  21.1 5.5 %block.1 = (bf16[16,16,16,128]{3,2,1,0:T(8,128)(2,1)S(1)}, bf16[16,16,16,128]{3,2,1,0:T(8,128)(2,1)S(1)}, bf16[288,512]{1,0:T(8,128)(2,1)S(1)}, bf16[288,1536]{1,0:T(8,128)(2,1)S(1)}) custom-call(s32[4]{0:T(128)S(1)} %add_convert_fusion.3.place, bf16[144,512]{1,0:T(8,128)(2,1)S(1)} %get-tuple-element.38.refs_0_, ...), custom_call_target="tpu_custom_call" | custom-call | flops 2000000000 | bytes 6000000 | tf_op jit(solution)/shard_map/block/pallas_call | solution.py:273
  26.6 10.2 %collective-permute-start.3 = (bf16[16,16,16,128]{3,2,1,0:T(8,128)(2,1)S(1)}, bf16[16,16,16,128]{3,2,1,0:T(8,128)(2,1)S(1)}, u32[]{:S(2)}, u32[]{:S(2)}) collective-permute-start(bf16[16,16,16,128]{3,2,1,0:T(8,128)(2,1)S(1)} %get-tuple-element.47), channel_id=1, source_target_pairs={{0,8},{2,10},{4,12},{6,14},{1,9},{3,11},{5,13},{7,15},{16,24},{18,... | collective-permute-start | bytes 3145736 | tf_op jit(solution)/shard_map/ppermute | solution.py:367
  37.6 1.5 %collective-permute-done.3 = bf16[16,16,16,128]{3,2,1,0:T(8,128)(2,1)S(1)} collective-permute-done((bf16[16,16,16,128]{3,2,1,0:T(8,128)(2,1)S(1)}, bf16[16,16,16,128]{3,2,1,0:T(8,128)(2,1)S(1)}, u32[]{:S(2)}, u32[]{:S(2)}) %collective-permute-start.3) | collective-permute-done | bytes 1048608 | tf_op jit(solution)/shard_map/ppermute | solution.py:367
  39.1 1.2 add_convert_fusion
  40.3 6.2 %all-to-all-start = ((bf16[8,32,16,128]{3,2,1,0:T(8,128)(2,1)}), bf16[8,32,16,128]{3,2,1,0:T(8,128)(2,1)S(1)}, u32[]{:S(2)}, u32[]{:S(2)}) async-start(bf16[8,32,16,128]{3,2,1,0:T(8,128)(2,1)} %bitcast.7), calls=%async_computation | async-start | bytes 2097152 | tf_op jit(solution)/shard_map/all_to_all | solution.py:371
  46.5 3.0 %collective-permute-start.4 = (bf16[72,512]{1,0:T(8,128)(2,1)S(1)}, bf16[72,512]{1,0:T(8,128)(2,1)S(1)}, u32[]{:S(2)}, u32[]{:S(2)}) collective-permute-start(bf16[72,512]{1,0:T(8,128)(2,1)S(1)} %get-tuple-element.54), channel_id=1, source_target_pairs={{1,0},{2,1},{3,2},{4,3},{5,4},{6,5},{7,6},{0,7},{9,8},{10,9},{11,1... | collective-permute-start | bytes 221192 | tf_op jit(solution)/shard_map/ppermute | solution.py:46
  49.5 10.7 %all-to-all-done = bf16[8,32,16,128]{3,2,1,0:T(8,128)(2,1)S(1)} async-done(((bf16[8,32,16,128]{3,2,1,0:T(8,128)(2,1)}), bf16[8,32,16,128]{3,2,1,0:T(8,128)(2,1)S(1)}, u32[]{:S(2)}, u32[]{:S(2)}) %all-to-all-start) | async-done | bytes 1048608 | tf_op jit(solution)/shard_map/all_to_all | solution.py:371
  61.0 3.9 %all-to-all-start.1 = ((bf16[8,4,16,128]{3,2,1,0:T(8,128)(2,1)}), bf16[8,4,16,128]{3,2,1,0:T(8,128)(2,1)S(1)}, u32[]{:S(2)}, u32[]{:S(2)}) async-start(bf16[8,4,16,128]{3,2,1,0:T(8,128)(2,1)} %bitcast.9), calls=%async_computation.1 | async-start | bytes 262144 | tf_op jit(solution)/shard_map/all_to_all | solution.py:371
  64.9 1.9 %collective-permute-start.5 = (bf16[72,512]{1,0:T(8,128)(2,1)S(1)}, bf16[72,512]{1,0:T(8,128)(2,1)S(1)}, u32[]{:S(2)}, u32[]{:S(2)}) collective-permute-start(bf16[72,512]{1,0:T(8,128)(2,1)S(1)} %get-tuple-element.57), channel_id=1, source_target_pairs={{8,0},{505,1},{10,2},{507,3},{12,4},{509,5},{14,6},{511,7},{16,8},... | collective-permute-start | bytes 221192 | tf_op jit(solution)/shard_map/ppermute | solution.py:46
  66.8 7.5 %all-to-all-done.1 = bf16[8,4,16,128]{3,2,1,0:T(8,128)(2,1)S(1)} async-done(((bf16[8,4,16,128]{3,2,1,0:T(8,128)(2,1)}), bf16[8,4,16,128]{3,2,1,0:T(8,128)(2,1)S(1)}, u32[]{:S(2)}, u32[]{:S(2)}) %all-to-all-start.1) | async-done | bytes 131104 | tf_op jit(solution)/shard_map/all_to_all | solution.py:371
  74.4 9.6 %all_to_all.25 = bf16[4,4,16,128]{3,2,1,0:T(8,128)(2,1)S(1)} all-to-all(bf16[4,4,16,128]{3,2,1,0:T(8,128)(2,1)S(1)} %broadcast_in_dim.8), channel_id=1, replica_groups={{0,16,32,48},{2,18,34,50},{4,20,36,52},{6,22,38,54},{64,80,96,112},{66,..., dimensions={0} | all-to-all | bytes 131072 | tf_op jit(solution)/shard_map/all_to_all | solution.py:371
  84.0 15.5 %all_to_all.26 = bf16[8,4,16,128]{3,2,1,0:T(8,128)(2,1)S(1)} all-to-all(bf16[8,4,16,128]{3,2,1,0:T(8,128)(2,1)S(1)} %broadcast_in_dim.10), channel_id=1, replica_groups={{0,128,256,384,4,132,260,388},{1,129,257,385,5,133,261,389},{16,144,272..., dimensions={0} | all-to-all | bytes 262144 | tf_op jit(solution)/shard_map/all_to_all | solution.py:371
  99.5 1.1 broadcast_in_dim.11
  100.6 3.6 %all-to-all-start.4 = ((bf16[8,32,16,128]{3,2,1,0:T(8,128)(2,1)}), bf16[8,32,16,128]{3,2,1,0:T(8,128)(2,1)S(1)}, u32[]{:S(2)}, u32[]{:S(2)}) async-start(bf16[8,32,16,128]{3,2,1,0:T(8,128)(2,1)} %broadcast_in_dim.11), calls=%async_computation.4 | async-start | bytes 2097152 | tf_op jit(solution)/shard_map/all_to_all | solution.py:371
  104.2 7.9 %collective-permute-start.6 = (bf16[72,512]{1,0:T(8,128)(2,1)S(1)}, bf16[72,512]{1,0:T(8,128)(2,1)S(1)}, u32[]{:S(2)}, u32[]{:S(2)}) collective-permute-start(bf16[72,512]{1,0:T(8,128)(2,1)S(1)} %get-tuple-element.61), channel_id=1, source_target_pairs={{505,0},{10,1},{507,2},{12,3},{509,4},{14,5},{511,6},{8,7},{1,8},{... | collective-permute-start | bytes 221192 | tf_op jit(solution)/shard_map/ppermute | solution.py:46
  112.1 6.0 %collective-permute-done.6.both = bf16[72,512]{1,0:T(8,128)(2,1)S(1)} collective-permute-done((bf16[72,512]{1,0:T(8,128)(2,1)S(1)}, bf16[72,512]{1,0:T(8,128)(2,1)S(1)}, u32[]{:S(2)}, u32[]{:S(2)}) %collective-permute-start.6) | collective-permute-done | bytes 73760 | tf_op jit(solution)/shard_map/ppermute | solution.py:46
  118.1 3.0 %collective-permute-start.7 = (bf16[16,16,16,128]{3,2,1,0:T(8,128)(2,1)S(1)}, bf16[16,16,16,128]{3,2,1,0:T(8,128)(2,1)S(1)}, u32[]{:S(2)}, u32[]{:S(2)}) collective-permute-start(bf16[16,16,16,128]{3,2,1,0:T(8,128)(2,1)S(1)} %bitcast.19), channel_id=1, source_target_pairs={{0,8},{2,10},{4,12},{6,14},{1,9},{3,11},{5,13},{7,15},{16,24},{18,... | collective-permute-start | bytes 3145736 | tf_op jit(solution)/shard_map/ppermute | solution.py:367
  121.1 1.6 %unpack.1 = bf16[6,12,4,512]{3,2,1,0:T(4,128)(2,1)} custom-call(s32[4]{0:T(128)S(1)} %add_convert_fusion.3.place, bf16[72,512]{1,0:T(8,128)(2,1)S(1)} %get-tuple-element.63.own, bf16[72,512]{1,0:T(8,128)(2,1)S(1)} %collective-permute-done.5.lon, bf16[72,512]{1,0:T(8,128)(2,1)S(1)} %collective-permute-done.4.lat, ...), custom_call_target="tpu_custom_call" | custom-call | bytes 900000 | tf_op jit(solution)/shard_map/unpack/pallas_call | solution.py:140
  123.4 2.2 %untile.1 = (bf16[512,1536]{1,0:T(8,128)(2,1)}, bf16[512,512]{1,0:T(8,128)(2,1)}) custom-call(s32[4]{0:T(128)S(1)} %add_convert_fusion.3.place, bf16[16,16,16,128]{3,2,1,0:T(8,128)(2,1)S(1)} %bitcast.20, bf16[16,16,16,128]{3,2,1,0:T(8,128)(2,1)S(1)} %collective-permute-done.7.theirs), custom_call_target="tpu_custom_call" | custom-call | bytes 4194304 | tf_op jit(solution)/shard_map/untile/pallas_call | solution.py:400
  (24 shorter events, 6.4 us)
Async XLA Ops:
  0.7 1.0 copy-start.1
  1.7 1.0 copy-start.4
  3.6 13.3 %collective-permute-start = (bf16[144,512]{1,0:T(8,128)(2,1)S(1)}, bf16[144,512]{1,0:T(8,128)(2,1)S(1)}, u32[]{:S(2)}, u32[]{:S(2)}) collective-permute-start(bf16[144,512]{1,0:T(8,128)(2,1)S(1)} %get-tuple-element.39), channel_id=1, source_target_pairs={{0,505},{1,10},{2,507},{3,12},{4,509},{5,14},{6,511},{7,8},{8,1},{... | collective-permute-start | bytes 442376 | tf_op jit(solution)/shard_map/ppermute | solution.py:46
  8.2 13.0 %collective-permute-start.1 = (bf16[144,512]{1,0:T(8,128)(2,1)S(1)}, bf16[144,512]{1,0:T(8,128)(2,1)S(1)}, u32[]{:S(2)}, u32[]{:S(2)}) collective-permute-start(bf16[144,512]{1,0:T(8,128)(2,1)S(1)} %get-tuple-element.40), channel_id=1, source_target_pairs={{0,8},{1,505},{2,10},{3,507},{4,12},{5,509},{6,14},{7,511},{8,16},... | collective-permute-start | bytes 442376 | tf_op jit(solution)/shard_map/ppermute | solution.py:46
  11.1 10.0 %collective-permute-start.2 = (bf16[144,512]{1,0:T(8,128)(2,1)S(1)}, bf16[144,512]{1,0:T(8,128)(2,1)S(1)}, u32[]{:S(2)}, u32[]{:S(2)}) collective-permute-start(bf16[144,512]{1,0:T(8,128)(2,1)S(1)} %get-tuple-element.41), channel_id=1, source_target_pairs={{0,1},{1,2},{2,3},{3,4},{4,5},{5,6},{6,7},{7,0},{8,9},{9,10},{10,1... | collective-permute-start | bytes 442376 | tf_op jit(solution)/shard_map/ppermute | solution.py:46
  14.2 1.4 %copy-start = (bf16[512,1536]{1,0:T(8,128)(2,1)S(1)}, bf16[512,1536]{1,0:T(8,128)(2,1)}, u32[]{:S(2)}) copy-start(bf16[512,1536]{1,0:T(8,128)(2,1)} %qkv_weight) | copy-start | bytes 4718596
  15.6 1.0 copy-start.3
  26.6 12.5 %collective-permute-start.3 = (bf16[16,16,16,128]{3,2,1,0:T(8,128)(2,1)S(1)}, bf16[16,16,16,128]{3,2,1,0:T(8,128)(2,1)S(1)}, u32[]{:S(2)}, u32[]{:S(2)}) collective-permute-start(bf16[16,16,16,128]{3,2,1,0:T(8,128)(2,1)S(1)} %get-tuple-element.47), channel_id=1, source_target_pairs={{0,8},{2,10},{4,12},{6,14},{1,9},{3,11},{5,13},{7,15},{16,24},{18,... | collective-permute-start | bytes 3145736 | tf_op jit(solution)/shard_map/ppermute | solution.py:367
  40.3 19.9 %all-to-all-start = ((bf16[8,32,16,128]{3,2,1,0:T(8,128)(2,1)}), bf16[8,32,16,128]{3,2,1,0:T(8,128)(2,1)S(1)}, u32[]{:S(2)}, u32[]{:S(2)}) async-start(bf16[8,32,16,128]{3,2,1,0:T(8,128)(2,1)} %bitcast.7), calls=%async_computation | async-start | bytes 2097152 | tf_op jit(solution)/shard_map/all_to_all | solution.py:371
  46.5 14.5 %collective-permute-start.4 = (bf16[72,512]{1,0:T(8,128)(2,1)S(1)}, bf16[72,512]{1,0:T(8,128)(2,1)S(1)}, u32[]{:S(2)}, u32[]{:S(2)}) collective-permute-start(bf16[72,512]{1,0:T(8,128)(2,1)S(1)} %get-tuple-element.54), channel_id=1, source_target_pairs={{1,0},{2,1},{3,2},{4,3},{5,4},{6,5},{7,6},{0,7},{9,8},{10,9},{11,1... | collective-permute-start | bytes 221192 | tf_op jit(solution)/shard_map/ppermute | solution.py:46
  61.0 13.3 %all-to-all-start.1 = ((bf16[8,4,16,128]{3,2,1,0:T(8,128)(2,1)}), bf16[8,4,16,128]{3,2,1,0:T(8,128)(2,1)S(1)}, u32[]{:S(2)}, u32[]{:S(2)}) async-start(bf16[8,4,16,128]{3,2,1,0:T(8,128)(2,1)} %bitcast.9), calls=%async_computation.1 | async-start | bytes 262144 | tf_op jit(solution)/shard_map/all_to_all | solution.py:371
  64.9 9.4 %collective-permute-start.5 = (bf16[72,512]{1,0:T(8,128)(2,1)S(1)}, bf16[72,512]{1,0:T(8,128)(2,1)S(1)}, u32[]{:S(2)}, u32[]{:S(2)}) collective-permute-start(bf16[72,512]{1,0:T(8,128)(2,1)S(1)} %get-tuple-element.57), channel_id=1, source_target_pairs={{8,0},{505,1},{10,2},{507,3},{12,4},{509,5},{14,6},{511,7},{16,8},... | collective-permute-start | bytes 221192 | tf_op jit(solution)/shard_map/ppermute | solution.py:46
  99.5 21.6 %copy-start.2 = (bf16[4,6,12,512]{3,0,2,1:T(4,128)(2,1)S(1)}, bf16[4,6,12,512]{3,0,2,1:T(4,128)(2,1)}, u32[]{:S(2)}) copy-start(bf16[4,6,12,512]{3,0,2,1:T(4,128)(2,1)} %param.5) | copy-start | bytes 884740
  100.6 17.5 %all-to-all-start.4 = ((bf16[8,32,16,128]{3,2,1,0:T(8,128)(2,1)}), bf16[8,32,16,128]{3,2,1,0:T(8,128)(2,1)S(1)}, u32[]{:S(2)}, u32[]{:S(2)}) async-start(bf16[8,32,16,128]{3,2,1,0:T(8,128)(2,1)} %broadcast_in_dim.11), calls=%async_computation.4 | async-start | bytes 2097152 | tf_op jit(solution)/shard_map/all_to_all | solution.py:371
  104.2 13.9 %collective-permute-start.6 = (bf16[72,512]{1,0:T(8,128)(2,1)S(1)}, bf16[72,512]{1,0:T(8,128)(2,1)S(1)}, u32[]{:S(2)}, u32[]{:S(2)}) collective-permute-start(bf16[72,512]{1,0:T(8,128)(2,1)S(1)} %get-tuple-element.61), channel_id=1, source_target_pairs={{505,0},{10,1},{507,2},{12,3},{509,4},{14,5},{511,6},{8,7},{1,8},{... | collective-permute-start | bytes 221192 | tf_op jit(solution)/shard_map/ppermute | solution.py:46
  118.1 5.2 %collective-permute-start.7 = (bf16[16,16,16,128]{3,2,1,0:T(8,128)(2,1)S(1)}, bf16[16,16,16,128]{3,2,1,0:T(8,128)(2,1)S(1)}, u32[]{:S(2)}, u32[]{:S(2)}) collective-permute-start(bf16[16,16,16,128]{3,2,1,0:T(8,128)(2,1)S(1)} %bitcast.19), channel_id=1, source_target_pairs={{0,8},{2,10},{4,12},{6,14},{1,9},{3,11},{5,13},{7,15},{16,24},{18,... | collective-permute-start | bytes 3145736 | tf_op jit(solution)/shard_map/ppermute | solution.py:367

commit v11 on v9

--- a/solution.py
+++ b/solution.py
@@ -444,8 +444,8 @@
     lon = moved(lon, 1, True)
     tiles = (mine.astype(jnp.float32) + swapped(theirs).astype(jnp.float32)).astype(jnp.bfloat16)
     tiles, lat, both = lax.optimization_barrier((tiles.reshape(-1, 16, 128), lat, both))
-    tiles, lon, lat = lax.optimization_barrier((scattered_sum(tiles, near), lon, moved(lat, 2, True)))
-    tiles = scattered_sum(tiles, middle)
+    tiles, lon, lat = lax.optimization_barrier((scattered_sum(tiles, near), lon, lat))
+    tiles, lat = lax.optimization_barrier((scattered_sum(tiles, middle), moved(lat, 2, True)))
     factor = (LEVELS * ROWS * COLS * lax.axis_size(ALL)) ** (-0.5)
     tiles = (added(exchanged(tiles, far)) * factor).astype(jnp.bfloat16)
     tiles, both = lax.optimization_barrier((gathered(tiles, middle), both))

time: 124 us -> 128 us (1.032)
  blocking collectives: 34 us -> 23.1 us
  waiting for transfers between devices: 20.7 us -> 29.6 us
  starting transfers between devices: 48.9 us -> 54.3 us
    all_to_all x3 -> x2, blocking collectives: 34 us -> 23.1 us  [all_to_all(): return lax.all_to_all(split, ALL, 0, 0, axis_index_groups=groups)]
    all_to_all x2 -> x3, waiting for transfers between devices: 8.75 us -> 17.7 us  [all_to_all(): return lax.all_to_all(split, ALL, 0, 0, axis_index_groups=groups)]
    all_to_all x2 -> x3, starting transfers between devices: 9.89 us -> 13.8 us  [all_to_all(): return lax.all_to_all(split, ALL, 0, 0, axis_index_groups=groups)]
    ppermute x6, starting transfers between devices: 25.8 us -> 27.3 us  [moved(): return lax.ppermute(value, ALL, pairs)]
  transfers between devices with their start and end apart: 10 -> 11, of which waited for: 4 -> 5; matrix products, arithmetic and copies ran while one was open for 0% -> 1% of each run, Pallas kernels for 3% -> 3%
where the time goes in v11:
time: 128 us
  starting transfers between devices  54.3 us (42%)
  waiting for transfers between devices  29.6 us (23%)
  blocking collectives  23.1 us (18%)
  Pallas kernels  12.1 us (9%)
  local copies, waits for them, and re-layouts  5.51 us (4%)
  other arithmetic  2.16 us (2%)
    ppermute x6, starting transfers between devices, moved(): return lax.ppermute(value, ALL, pairs)  27.3 us
    all_to_all x2, blocking collectives, all_to_all(): return lax.all_to_all(split, ALL, 0, 0, axis_index_groups=groups)  23.1 us
    all_to_all x3, waiting for transfers between devices, all_to_all(): return lax.all_to_all(split, ALL, 0, 0, axis_index_groups=groups)  17.7 us
    all_to_all x3, starting transfers between devices, all_to_all(): return lax.all_to_all(split, ALL, 0, 0, axis_index_groups=groups)  13.8 us
    ppermute x2, starting transfers between devices, swapped(): return lax.ppermute(value, ALL, [*zip(first, second), *zip(second, first)])  13.2 us
    ppermute x6, waiting for transfers between devices, moved(): return lax.ppermute(value, ALL, pairs)  10.5 us
    pallas_call x1, Pallas kernels, block(): pl.pallas_call(block_kernel, out_shape=(HALF_TILES, HALF_TILES, rows_of(T...  5.47 us
    unnamed x10, local copies, waits for them, and re-layouts  4.37 us
  transfers between devices with their start and end apart: 11, of which 5 were waited for; matrix products, arithmetic and copies ran while one was open for 1% of the time, Pallas kernels for 3%

profile of v11, /device:TPU:1, one launch (start us, length us, event | category | flops | bytes accessed | tf_op | source)
XLA Modules:
  0.0 127.6 jit_solution(11686070328307699650)
XLA Ops:
  3.6 4.6 %collective-permute-start = (bf16[144,512]{1,0:T(8,128)(2,1)S(1)}, bf16[144,512]{1,0:T(8,128)(2,1)S(1)}, u32[]{:S(2)}, u32[]{:S(2)}) collective-permute-start(bf16[144,512]{1,0:T(8,128)(2,1)S(1)} %get-tuple-element.42), channel_id=1, source_target_pairs={{0,505},{1,10},{2,507},{3,12},{4,509},{5,14},{6,511},{7,8},{8,1},{... | collective-permute-start | bytes 442376 | tf_op jit(solution)/shard_map/ppermute | solution.py:47
  8.2 2.9 %collective-permute-start.1 = (bf16[144,512]{1,0:T(8,128)(2,1)S(1)}, bf16[144,512]{1,0:T(8,128)(2,1)S(1)}, u32[]{:S(2)}, u32[]{:S(2)}) collective-permute-start(bf16[144,512]{1,0:T(8,128)(2,1)S(1)} %get-tuple-element.43), channel_id=1, source_target_pairs={{0,8},{1,505},{2,10},{3,507},{4,12},{5,509},{6,14},{7,511},{8,16},... | collective-permute-start | bytes 442376 | tf_op jit(solution)/shard_map/ppermute | solution.py:47
  11.1 3.1 %collective-permute-start.2 = (bf16[144,512]{1,0:T(8,128)(2,1)S(1)}, bf16[144,512]{1,0:T(8,128)(2,1)S(1)}, u32[]{:S(2)}, u32[]{:S(2)}) collective-permute-start(bf16[144,512]{1,0:T(8,128)(2,1)S(1)} %get-tuple-element.44), channel_id=1, source_target_pairs={{0,1},{1,2},{2,3},{3,4},{4,5},{5,6},{6,7},{7,0},{8,9},{9,10},{10,1... | collective-permute-start | bytes 442376 | tf_op jit(solution)/shard_map/ppermute | solution.py:47
  14.2 1.4 %copy-done = bf16[512,1536]{1,0:T(8,128)(2,1)S(1)} copy-done((bf16[512,1536]{1,0:T(8,128)(2,1)S(1)}, bf16[512,1536]{1,0:T(8,128)(2,1)}, u32[]{:S(2)}) %copy-start) | copy-done | bytes 1572888
  16.9 4.3 %collective-permute-done.1.refs_2_ = bf16[144,512]{1,0:T(8,128)(2,1)S(1)} collective-permute-done((bf16[144,512]{1,0:T(8,128)(2,1)S(1)}, bf16[144,512]{1,0:T(8,128)(2,1)S(1)}, u32[]{:S(2)}, u32[]{:S(2)}) %collective-permute-start.1) | collective-permute-done | bytes 147488 | tf_op jit(solution)/shard_map/ppermute | solution.py:47
  21.1 5.5 %block.1 = (bf16[16,16,16,128]{3,2,1,0:T(8,128)(2,1)S(1)}, bf16[16,16,16,128]{3,2,1,0:T(8,128)(2,1)S(1)}, bf16[288,512]{1,0:T(8,128)(2,1)S(1)}, bf16[288,1536]{1,0:T(8,128)(2,1)S(1)}) custom-call(s32[4]{0:T(128)S(1)} %add_convert_fusion.3.place, bf16[144,512]{1,0:T(8,128)(2,1)S(1)} %get-tuple-element.41.refs_0_, ...), custom_call_target="tpu_custom_call" | custom-call | flops 2000000000 | bytes 6000000 | tf_op jit(solution)/shard_map/block/pallas_call | solution.py:274
  26.6 10.2 %collective-permute-start.3 = (bf16[16,16,16,128]{3,2,1,0:T(8,128)(2,1)S(1)}, bf16[16,16,16,128]{3,2,1,0:T(8,128)(2,1)S(1)}, u32[]{:S(2)}, u32[]{:S(2)}) collective-permute-start(bf16[16,16,16,128]{3,2,1,0:T(8,128)(2,1)S(1)} %get-tuple-element.50), channel_id=1, source_target_pairs={{0,8},{2,10},{4,12},{6,14},{1,9},{3,11},{5,13},{7,15},{16,24},{18,... | collective-permute-start | bytes 3145736 | tf_op jit(solution)/shard_map/ppermute | solution.py:368
  37.6 1.5 %collective-permute-done.3 = bf16[16,16,16,128]{3,2,1,0:T(8,128)(2,1)S(1)} collective-permute-done((bf16[16,16,16,128]{3,2,1,0:T(8,128)(2,1)S(1)}, bf16[16,16,16,128]{3,2,1,0:T(8,128)(2,1)S(1)}, u32[]{:S(2)}, u32[]{:S(2)}) %collective-permute-start.3) | collective-permute-done | bytes 1048608 | tf_op jit(solution)/shard_map/ppermute | solution.py:368
  39.1 1.2 add_convert_fusion
  40.3 6.2 %all-to-all-start = ((bf16[8,32,16,128]{3,2,1,0:T(8,128)(2,1)}), bf16[8,32,16,128]{3,2,1,0:T(8,128)(2,1)S(1)}, u32[]{:S(2)}, u32[]{:S(2)}) async-start(bf16[8,32,16,128]{3,2,1,0:T(8,128)(2,1)} %bitcast.7), calls=%async_computation | async-start | bytes 2097152 | tf_op jit(solution)/shard_map/all_to_all | solution.py:372
  46.5 1.9 %collective-permute-start.4 = (bf16[72,512]{1,0:T(8,128)(2,1)S(1)}, bf16[72,512]{1,0:T(8,128)(2,1)S(1)}, u32[]{:S(2)}, u32[]{:S(2)}) collective-permute-start(bf16[72,512]{1,0:T(8,128)(2,1)S(1)} %get-tuple-element.56), channel_id=1, source_target_pairs={{8,0},{505,1},{10,2},{507,3},{12,4},{509,5},{14,6},{511,7},{16,8},... | collective-permute-start | bytes 221192 | tf_op jit(solution)/shard_map/ppermute | solution.py:47
  48.5 11.8 %all-to-all-done = bf16[8,32,16,128]{3,2,1,0:T(8,128)(2,1)S(1)} async-done(((bf16[8,32,16,128]{3,2,1,0:T(8,128)(2,1)}), bf16[8,32,16,128]{3,2,1,0:T(8,128)(2,1)S(1)}, u32[]{:S(2)}, u32[]{:S(2)}) %all-to-all-start) | async-done | bytes 1048608 | tf_op jit(solution)/shard_map/all_to_all | solution.py:372
  61.0 3.9 %all-to-all-start.1 = ((bf16[8,4,16,128]{3,2,1,0:T(8,128)(2,1)}), bf16[8,4,16,128]{3,2,1,0:T(8,128)(2,1)S(1)}, u32[]{:S(2)}, u32[]{:S(2)}) async-start(bf16[8,4,16,128]{3,2,1,0:T(8,128)(2,1)} %bitcast.9), calls=%async_computation.1 | async-start | bytes 262144 | tf_op jit(solution)/shard_map/all_to_all | solution.py:372
  64.9 3.4 %collective-permute-start.5 = (bf16[72,512]{1,0:T(8,128)(2,1)S(1)}, bf16[72,512]{1,0:T(8,128)(2,1)S(1)}, u32[]{:S(2)}, u32[]{:S(2)}) collective-permute-start(bf16[72,512]{1,0:T(8,128)(2,1)S(1)} %get-tuple-element.59), channel_id=1, source_target_pairs={{1,0},{2,1},{3,2},{4,3},{5,4},{6,5},{7,6},{0,7},{9,8},{10,9},{11,1... | collective-permute-start | bytes 221192 | tf_op jit(solution)/shard_map/ppermute | solution.py:47
  68.3 5.9 %all-to-all-done.1 = bf16[8,4,16,128]{3,2,1,0:T(8,128)(2,1)S(1)} async-done(((bf16[8,4,16,128]{3,2,1,0:T(8,128)(2,1)}), bf16[8,4,16,128]{3,2,1,0:T(8,128)(2,1)S(1)}, u32[]{:S(2)}, u32[]{:S(2)}) %all-to-all-start.1) | async-done | bytes 131104 | tf_op jit(solution)/shard_map/all_to_all | solution.py:372
  74.3 9.6 %all_to_all.25 = bf16[4,4,16,128]{3,2,1,0:T(8,128)(2,1)S(1)} all-to-all(bf16[4,4,16,128]{3,2,1,0:T(8,128)(2,1)S(1)} %broadcast_in_dim.8), channel_id=1, replica_groups={{0,16,32,48},{2,18,34,50},{4,20,36,52},{6,22,38,54},{64,80,96,112},{66,..., dimensions={0} | all-to-all | bytes 131072 | tf_op jit(solution)/shard_map/all_to_all | solution.py:372
  84.0 13.5 %all_to_all.26 = bf16[8,4,16,128]{3,2,1,0:T(8,128)(2,1)S(1)} all-to-all(bf16[8,4,16,128]{3,2,1,0:T(8,128)(2,1)S(1)} %broadcast_in_dim.10), channel_id=1, replica_groups={{0,128,256,384,4,132,260,388},{1,129,257,385,5,133,261,389},{16,144,272..., dimensions={0} | all-to-all | bytes 262144 | tf_op jit(solution)/shard_map/all_to_all | solution.py:372
  98.6 3.7 %all-to-all-start.4 = ((bf16[8,32,16,128]{3,2,1,0:T(8,128)(2,1)}), bf16[8,32,16,128]{3,2,1,0:T(8,128)(2,1)S(1)}, u32[]{:S(2)}, u32[]{:S(2)}) async-start(bf16[8,32,16,128]{3,2,1,0:T(8,128)(2,1)} %broadcast_in_dim.11), calls=%async_computation.4 | async-start | bytes 2097152 | tf_op jit(solution)/shard_map/all_to_all | solution.py:372
  102.3 11.3 %collective-permute-start.6 = (bf16[72,512]{1,0:T(8,128)(2,1)S(1)}, bf16[72,512]{1,0:T(8,128)(2,1)S(1)}, u32[]{:S(2)}, u32[]{:S(2)}) collective-permute-start(bf16[72,512]{1,0:T(8,128)(2,1)S(1)} %get-tuple-element.63), channel_id=1, source_target_pairs={{505,0},{10,1},{507,2},{12,3},{509,4},{14,5},{511,6},{8,7},{1,8},{... | collective-permute-start | bytes 221192 | tf_op jit(solution)/shard_map/ppermute | solution.py:47
  113.6 6.2 %collective-permute-done.6.both = bf16[72,512]{1,0:T(8,128)(2,1)S(1)} collective-permute-done((bf16[72,512]{1,0:T(8,128)(2,1)S(1)}, bf16[72,512]{1,0:T(8,128)(2,1)S(1)}, u32[]{:S(2)}, u32[]{:S(2)}) %collective-permute-start.6) | collective-permute-done | bytes 73760 | tf_op jit(solution)/shard_map/ppermute | solution.py:47
  119.8 3.0 %collective-permute-start.7 = (bf16[16,16,16,128]{3,2,1,0:T(8,128)(2,1)S(1)}, bf16[16,16,16,128]{3,2,1,0:T(8,128)(2,1)S(1)}, u32[]{:S(2)}, u32[]{:S(2)}) collective-permute-start(bf16[16,16,16,128]{3,2,1,0:T(8,128)(2,1)S(1)} %bitcast.19), channel_id=1, source_target_pairs={{0,8},{2,10},{4,12},{6,14},{1,9},{3,11},{5,13},{7,15},{16,24},{18,... | collective-permute-start | bytes 3145736 | tf_op jit(solution)/shard_map/ppermute | solution.py:368
  122.8 1.6 %untile_own.1 = (bf16[512,1536]{1,0:T(8,128)(2,1)}, bf16[512,512]{1,0:T(8,128)(2,1)}) custom-call(s32[4]{0:T(128)S(1)} %add_convert_fusion.3.place, bf16[16,16,16,128]{3,2,1,0:T(8,128)(2,1)S(1)} %bitcast.20), custom_call_target="tpu_custom_call" | custom-call | bytes 2097152 | tf_op jit(solution)/shard_map/untile_own/pallas_call | solution.py:414
  124.4 1.6 %unpack.1 = bf16[6,12,4,512]{3,2,1,0:T(4,128)(2,1)} custom-call(s32[4]{0:T(128)S(1)} %add_convert_fusion.3.place, bf16[72,512]{1,0:T(8,128)(2,1)S(1)} %get-tuple-element.67.own, bf16[72,512]{1,0:T(8,128)(2,1)S(1)} %collective-permute-done.4.lon, bf16[72,512]{1,0:T(8,128)(2,1)S(1)} %collective-permute-done.5.lat, ...), custom_call_target="tpu_custom_call" | custom-call | bytes 900000 | tf_op jit(solution)/shard_map/unpack/pallas_call | solution.py:141
  126.0 1.6 %untile_other.1 = (bf16[512,1536]{1,0:T(8,128)(2,1)}, bf16[512,512]{1,0:T(8,128)(2,1)}) custom-call(s32[4]{0:T(128)S(1)} %add_convert_fusion.3.place, bf16[16,16,16,128]{3,2,1,0:T(8,128)(2,1)S(1)} %collective-permute-done.7.tiles, bf16[512,1536]{1,0:T(8,128)(2,1)} %get-tuple-element.73.refs_0_, ...), custom_call_target="tpu_custom_call", output_to_operand_aliasing={{0}: (2, {}), {1}: (3, {})} | custom-call | bytes 2097152 | tf_op jit(solution)/shard_map/untile_other/pallas_call | solution.py:414
  (25 shorter events, 6.9 us)
Async XLA Ops:
  0.7 1.0 copy-start.1
  1.7 1.0 copy-start.4
  3.6 13.3 %collective-permute-start = (bf16[144,512]{1,0:T(8,128)(2,1)S(1)}, bf16[144,512]{1,0:T(8,128)(2,1)S(1)}, u32[]{:S(2)}, u32[]{:S(2)}) collective-permute-start(bf16[144,512]{1,0:T(8,128)(2,1)S(1)} %get-tuple-element.42), channel_id=1, source_target_pairs={{0,505},{1,10},{2,507},{3,12},{4,509},{5,14},{6,511},{7,8},{8,1},{... | collective-permute-start | bytes 442376 | tf_op jit(solution)/shard_map/ppermute | solution.py:47
  8.2 13.0 %collective-permute-start.1 = (bf16[144,512]{1,0:T(8,128)(2,1)S(1)}, bf16[144,512]{1,0:T(8,128)(2,1)S(1)}, u32[]{:S(2)}, u32[]{:S(2)}) collective-permute-start(bf16[144,512]{1,0:T(8,128)(2,1)S(1)} %get-tuple-element.43), channel_id=1, source_target_pairs={{0,8},{1,505},{2,10},{3,507},{4,12},{5,509},{6,14},{7,511},{8,16},... | collective-permute-start | bytes 442376 | tf_op jit(solution)/shard_map/ppermute | solution.py:47
  11.1 10.0 %collective-permute-start.2 = (bf16[144,512]{1,0:T(8,128)(2,1)S(1)}, bf16[144,512]{1,0:T(8,128)(2,1)S(1)}, u32[]{:S(2)}, u32[]{:S(2)}) collective-permute-start(bf16[144,512]{1,0:T(8,128)(2,1)S(1)} %get-tuple-element.44), channel_id=1, source_target_pairs={{0,1},{1,2},{2,3},{3,4},{4,5},{5,6},{6,7},{7,0},{8,9},{9,10},{10,1... | collective-permute-start | bytes 442376 | tf_op jit(solution)/shard_map/ppermute | solution.py:47
  14.2 1.4 %copy-start = (bf16[512,1536]{1,0:T(8,128)(2,1)S(1)}, bf16[512,1536]{1,0:T(8,128)(2,1)}, u32[]{:S(2)}) copy-start(bf16[512,1536]{1,0:T(8,128)(2,1)} %qkv_weight) | copy-start | bytes 4718596
  15.6 1.0 copy-start.3
  26.6 12.5 %collective-permute-start.3 = (bf16[16,16,16,128]{3,2,1,0:T(8,128)(2,1)S(1)}, bf16[16,16,16,128]{3,2,1,0:T(8,128)(2,1)S(1)}, u32[]{:S(2)}, u32[]{:S(2)}) collective-permute-start(bf16[16,16,16,128]{3,2,1,0:T(8,128)(2,1)S(1)} %get-tuple-element.50), channel_id=1, source_target_pairs={{0,8},{2,10},{4,12},{6,14},{1,9},{3,11},{5,13},{7,15},{16,24},{18,... | collective-permute-start | bytes 3145736 | tf_op jit(solution)/shard_map/ppermute | solution.py:368
  40.3 19.9 %all-to-all-start = ((bf16[8,32,16,128]{3,2,1,0:T(8,128)(2,1)}), bf16[8,32,16,128]{3,2,1,0:T(8,128)(2,1)S(1)}, u32[]{:S(2)}, u32[]{:S(2)}) async-start(bf16[8,32,16,128]{3,2,1,0:T(8,128)(2,1)} %bitcast.7), calls=%async_computation | async-start | bytes 2097152 | tf_op jit(solution)/shard_map/all_to_all | solution.py:372
  46.5 14.5 %collective-permute-start.4 = (bf16[72,512]{1,0:T(8,128)(2,1)S(1)}, bf16[72,512]{1,0:T(8,128)(2,1)S(1)}, u32[]{:S(2)}, u32[]{:S(2)}) collective-permute-start(bf16[72,512]{1,0:T(8,128)(2,1)S(1)} %get-tuple-element.56), channel_id=1, source_target_pairs={{8,0},{505,1},{10,2},{507,3},{12,4},{509,5},{14,6},{511,7},{16,8},... | collective-permute-start | bytes 221192 | tf_op jit(solution)/shard_map/ppermute | solution.py:47
  61.0 13.3 %all-to-all-start.1 = ((bf16[8,4,16,128]{3,2,1,0:T(8,128)(2,1)}), bf16[8,4,16,128]{3,2,1,0:T(8,128)(2,1)S(1)}, u32[]{:S(2)}, u32[]{:S(2)}) async-start(bf16[8,4,16,128]{3,2,1,0:T(8,128)(2,1)} %bitcast.9), calls=%async_computation.1 | async-start | bytes 262144 | tf_op jit(solution)/shard_map/all_to_all | solution.py:372
  64.9 9.4 %collective-permute-start.5 = (bf16[72,512]{1,0:T(8,128)(2,1)S(1)}, bf16[72,512]{1,0:T(8,128)(2,1)S(1)}, u32[]{:S(2)}, u32[]{:S(2)}) collective-permute-start(bf16[72,512]{1,0:T(8,128)(2,1)S(1)} %get-tuple-element.59), channel_id=1, source_target_pairs={{1,0},{2,1},{3,2},{4,3},{5,4},{6,5},{7,6},{0,7},{9,8},{10,9},{11,1... | collective-permute-start | bytes 221192 | tf_op jit(solution)/shard_map/ppermute | solution.py:47
  98.6 25.8 %copy-start.2 = (bf16[4,6,12,512]{3,0,2,1:T(4,128)(2,1)S(1)}, bf16[4,6,12,512]{3,0,2,1:T(4,128)(2,1)}, u32[]{:S(2)}) copy-start(bf16[4,6,12,512]{3,0,2,1:T(4,128)(2,1)} %param.5) | copy-start | bytes 884740
  98.6 21.2 %all-to-all-start.4 = ((bf16[8,32,16,128]{3,2,1,0:T(8,128)(2,1)}), bf16[8,32,16,128]{3,2,1,0:T(8,128)(2,1)S(1)}, u32[]{:S(2)}, u32[]{:S(2)}) async-start(bf16[8,32,16,128]{3,2,1,0:T(8,128)(2,1)} %broadcast_in_dim.11), calls=%async_computation.4 | async-start | bytes 2097152 | tf_op jit(solution)/shard_map/all_to_all | solution.py:372
  102.3 17.5 %collective-permute-start.6 = (bf16[72,512]{1,0:T(8,128)(2,1)S(1)}, bf16[72,512]{1,0:T(8,128)(2,1)S(1)}, u32[]{:S(2)}, u32[]{:S(2)}) collective-permute-start(bf16[72,512]{1,0:T(8,128)(2,1)S(1)} %get-tuple-element.63), channel_id=1, source_target_pairs={{505,0},{10,1},{507,2},{12,3},{509,4},{14,5},{511,6},{8,7},{1,8},{... | collective-permute-start | bytes 221192 | tf_op jit(solution)/shard_map/ppermute | solution.py:47
  119.8 6.2 %collective-permute-start.7 = (bf16[16,16,16,128]{3,2,1,0:T(8,128)(2,1)S(1)}, bf16[16,16,16,128]{3,2,1,0:T(8,128)(2,1)S(1)}, u32[]{:S(2)}, u32[]{:S(2)}) collective-permute-start(bf16[16,16,16,128]{3,2,1,0:T(8,128)(2,1)S(1)} %bitcast.19), channel_id=1, source_target_pairs={{0,8},{2,10},{4,12},{6,14},{1,9},{3,11},{5,13},{7,15},{16,24},{18,... | collective-permute-start | bytes 3145736 | tf_op jit(solution)/shard_map/ppermute | solution.py:368
